TPU v7x, 32 devices: a whole 2x2x4 slice. The times are simulated.
32 devices in a mesh: gx: 4 (over x, core), gy: 8 (over z, y).
Axes of the slice: x: 2, y: 2, z: 4, core: 2. Of those that a mesh axis runs over, the one named last changes fastest.
Arguments:
- flat_master: float32 [13326112], P(('gx', 'gy'))
- flat_first: float32 [13326112], P(('gx', 'gy'))
- flat_second: float32 [13326112], P(('gx', 'gy'))
- table: float32 [49408, 512], P('gy'), may hold values from -6 to 6
- table_first: float32 [49408, 512], P('gy')
- table_second: float32 [49408, 512], P('gy')
- pixels: bfloat16 [256, 49, 3072], P(('gx', 'gy')), may hold values from -6 to 6
- token_ids: int32 [256, 77], P(('gx', 'gy')), may hold values from 0 to 49407
- end_pos: int32 [256], P(('gx', 'gy')), may hold values from 19 to 76
- pair_counts: int32 [4, 8], replicated, may hold values from 1 to 8, as said below
- groups: int32 [256], replicated, may hold values from 0 to 169, as said below
- cached_image: bfloat16 [256, 512], P(('gx', 'gy')), may hold values from -0.625 to 0.625
- cached_text: bfloat16 [256, 512], P(('gx', 'gy')), may hold values from -0.625 to 0.625
Outputs:
- master_out: float32 [13326112], P(('gx', 'gy'))
- first_out: float32 [13326112], P(('gx', 'gy'))
- second_out: float32 [13326112], P(('gx', 'gy'))
- table_out: float32 [49408, 512], P('gy')
- table_first_out: float32 [49408, 512], P('gy')
- table_second_out: float32 [49408, 512], P('gy')
- loss_sum: float32 [], replicated
- positives: float32 [], replicated
- grad_norm: float32 [], replicated
Inputs may be any that keep to these rules, and one draw needn't show every extreme that they name: `pair_counts`: each device's valid pairs fill its first slots; the last device is full. `groups`: pairs with equal ids are duplicates of one another. `end_pos`: tokens after a text's end token are padding.
All inputs are finite; a program needn't handle non-finite values.
Results may differ from a plain program's by a relative error of at most 0.0024.
The roundings to bfloat16 on the way count: a program that leaves them out, or rounds other values in their place, can miss the bound.
Values may be sent and summed in bfloat16 or wider, within the bound.
A program may use at most 384 MiB of HBM per device.

v0:
```python
import jax
import jax.numpy as jnp
from jax import lax
from jax.sharding import PartitionSpec as P

D_IMG = 768
IMG_HEADS = 12
IMG_MLP = 3072
PATCH_DIM = 3072
D_TXT = 512
TXT_HEADS = 8
TXT_MLP = 2048
CTX = 77
EMBED = 512
STEP = 10
IMG_TOK = 50


clip_limit = 0.1
beta_one = 0.9
beta_two = 0.999
adam_eps = 1e-08
decay_rate = 0.1
rate_matrix = 0.01
rate_vector = 0.2
rate_table = 0.2
norm_eps = 1e-05


def segment_list():
    return [
        ("patch_embed", PATCH_DIM, D_IMG),
        ("image_attn", D_IMG, 4 * D_IMG),
        ("image_up", D_IMG, IMG_MLP),
        ("image_down", IMG_MLP, D_IMG),
        ("image_proj", D_IMG, EMBED),
        ("text_attn", D_TXT, 4 * D_TXT),
        ("text_up", D_TXT, TXT_MLP),
        ("text_down", TXT_MLP, D_TXT),
        ("text_proj", D_TXT, EMBED),
        ("image_vec", IMG_TOK + 9, D_IMG),
        ("text_vec", CTX + 6, D_TXT),
        ("temper", 1, 1),
    ]


def unpack(flat_vals):
    pieces = {}
    offset = 0
    for seg_name, seg_rows, seg_cols in segment_list():
        pieces[seg_name] = flat_vals[offset : offset + seg_rows * seg_cols].reshape(
            seg_rows, seg_cols
        )
        offset = offset + seg_rows * seg_cols
    return pieces


def layer_norm(values, gain_vec, shift_vec):
    center = values - jnp.mean(values, -1, keepdims=True)
    spread = jnp.mean(center * center, -1, keepdims=True)
    return center * lax.rsqrt(spread + norm_eps) * gain_vec + shift_vec


def quick_gelu(values):
    return values * jax.nn.sigmoid(1.702 * values)


def unit_rows(values):
    return values * lax.rsqrt(jnp.sum(values * values, -1, keepdims=True) + 1e-06)


def fwd_dot(left_side, right_side):
    return jnp.dot(left_side, right_side, preferred_element_type=jnp.float32)


def back_dot(left_side, right_side):
    return lax.dot_general(
        left_side,
        right_side,
        (((left_side.ndim - 1,), (1,)), ((), ())),
        preferred_element_type=jnp.float32,
    )


def weight_grad(left_side, right_side):
    flat_left = left_side.reshape(-1, left_side.shape[-1])
    flat_right = right_side.reshape(-1, right_side.shape[-1])
    return lax.dot_general(
        flat_left, flat_right, (((0,), (0,)), ((), ())), preferred_element_type=jnp.float32
    )


def block_forward(hidden, attn_w, up_w, down_w, gain_rows, head_count, causal):
    seq_count, length, model_width = hidden.shape
    head_dim = model_width // head_count
    normed = layer_norm(hidden, gain_rows[0], gain_rows[1]).astype(jnp.bfloat16)
    triple = fwd_dot(normed, attn_w[:, : 3 * model_width]).astype(jnp.bfloat16)
    query_part = triple[..., :model_width].reshape(seq_count, length, head_count, head_dim)
    key_part = triple[..., model_width : 2 * model_width].reshape(
        seq_count, length, head_count, head_dim
    )
    value_part = triple[..., 2 * model_width :].reshape(seq_count, length, head_count, head_dim)
    scores = jnp.einsum(
        "slhd,smhd->shlm", query_part, key_part, preferred_element_type=jnp.float32
    ) * head_dim ** (-0.5)
    if causal:
        allowed = jnp.arange(length)[:, None] >= jnp.arange(length)[None, :]
        scores = jnp.where(allowed, scores, -1e30)
    attn_probs = jax.nn.softmax(scores, axis=-1)
    attended = jnp.einsum(
        "shlm,smhd->slhd",
        attn_probs.astype(jnp.bfloat16),
        value_part,
        preferred_element_type=jnp.float32,
    ).astype(jnp.bfloat16)
    attended = attended.reshape(seq_count, length, model_width)
    middle = hidden + fwd_dot(attended, attn_w[:, 3 * model_width :])
    normed_two = layer_norm(middle, gain_rows[2], gain_rows[3]).astype(jnp.bfloat16)
    upper = fwd_dot(normed_two, up_w)
    act_low = quick_gelu(upper).astype(jnp.bfloat16)
    output = middle + fwd_dot(act_low, down_w)
    return (
        output,
        (
            hidden,
            normed,
            query_part,
            key_part,
            value_part,
            attn_probs,
            attended,
            middle,
            normed_two,
            upper,
            act_low,
        ),
    )


def block_backward(grad_out, saved_vals, attn_w, up_w, down_w, gain_rows, head_count):
    (
        hidden,
        normed,
        query_part,
        key_part,
        value_part,
        attn_probs,
        attended,
        middle,
        normed_two,
        upper,
        act_low,
    ) = saved_vals
    seq_count, length, model_width = hidden.shape
    head_dim = model_width // head_count
    grad_mlp = grad_out.astype(jnp.bfloat16)
    grad_down = weight_grad(act_low, grad_mlp)
    grad_act = back_dot(grad_mlp, down_w)
    gelu_pull = jax.vjp(quick_gelu, upper)[1]
    grad_upper = gelu_pull(grad_act)[0].astype(jnp.bfloat16)
    grad_up = weight_grad(normed_two, grad_upper)
    norm_pull = jax.vjp(layer_norm, middle, gain_rows[2], gain_rows[3])[1]
    grad_mid, grad_gain_two, grad_shift_two = norm_pull(back_dot(grad_upper, up_w))
    grad_middle = grad_out + grad_mid
    grad_att_out = grad_middle.astype(jnp.bfloat16)
    grad_wout = weight_grad(attended, grad_att_out)
    grad_attended = back_dot(grad_att_out, attn_w[:, 3 * model_width :]).astype(jnp.bfloat16)
    grad_attended = grad_attended.reshape(seq_count, length, head_count, head_dim)
    grad_probs = jnp.einsum(
        "slhd,smhd->shlm", grad_attended, value_part, preferred_element_type=jnp.float32
    )
    grad_value = jnp.einsum(
        "shlm,slhd->smhd",
        attn_probs.astype(jnp.bfloat16),
        grad_attended,
        preferred_element_type=jnp.float32,
    )
    grad_scores = attn_probs * (grad_probs - jnp.sum(grad_probs * attn_probs, -1, keepdims=True))
    grad_scores = grad_scores.astype(jnp.bfloat16)
    grad_query = jnp.einsum(
        "shlm,smhd->slhd", grad_scores, key_part, preferred_element_type=jnp.float32
    ) * head_dim ** (-0.5)
    grad_key = jnp.einsum(
        "shlm,slhd->smhd", grad_scores, query_part, preferred_element_type=jnp.float32
    ) * head_dim ** (-0.5)
    grad_triple = jnp.concatenate(
        [
            grad_query.reshape(seq_count, length, model_width),
            grad_key.reshape(seq_count, length, model_width),
            grad_value.reshape(seq_count, length, model_width),
        ],
        -1,
    ).astype(jnp.bfloat16)
    grad_qkv = weight_grad(normed, grad_triple)
    norm_pull_one = jax.vjp(layer_norm, hidden, gain_rows[0], gain_rows[1])[1]
    grad_in, grad_gain_one, grad_shift_one = norm_pull_one(
        back_dot(grad_triple, attn_w[:, : 3 * model_width])
    )
    grad_gains = jnp.stack([grad_gain_one, grad_shift_one, grad_gain_two, grad_shift_two])
    return (
        grad_middle + grad_in,
        jnp.concatenate([grad_qkv, grad_wout], 1),
        grad_up,
        grad_down,
        grad_gains,
    )


def image_forward(pieces, pixels):
    image_vec = pieces["image_vec"].astype(jnp.float32)
    patch_out = fwd_dot(pixels, pieces["patch_embed"])
    class_row = jnp.broadcast_to(image_vec[0], (pixels.shape[0], 1, D_IMG))
    tokens = jnp.concatenate([class_row, patch_out], 1) + image_vec[1 : IMG_TOK + 1]
    start_rows = layer_norm(tokens, image_vec[IMG_TOK + 1], image_vec[IMG_TOK + 2])
    hidden, saved_vals = block_forward(
        start_rows,
        pieces["image_attn"],
        pieces["image_up"],
        pieces["image_down"],
        image_vec[IMG_TOK + 3 : IMG_TOK + 7],
        IMG_HEADS,
        False,
    )
    head_in = layer_norm(hidden[:, 0], image_vec[IMG_TOK + 7], image_vec[IMG_TOK + 8]).astype(
        jnp.bfloat16
    )
    raw_embed = fwd_dot(head_in, pieces["image_proj"])
    return (
        unit_rows(raw_embed).astype(jnp.bfloat16),
        (tokens, saved_vals, hidden, head_in, raw_embed),
    )


def image_backward(pieces, pixels, kept_vals, grad_emb):
    tokens, saved_vals, hidden, head_in, raw_embed = kept_vals
    image_vec = pieces["image_vec"].astype(jnp.float32)
    grad_raw = jax.vjp(unit_rows, raw_embed)[1](grad_emb)[0].astype(jnp.bfloat16)
    grad_proj = weight_grad(head_in, grad_raw)
    post_pull = jax.vjp(layer_norm, hidden[:, 0], image_vec[IMG_TOK + 7], image_vec[IMG_TOK + 8])[1]
    grad_class_out, grad_gain_post, grad_shift_post = post_pull(
        back_dot(grad_raw, pieces["image_proj"])
    )
    grad_hidden = jnp.concatenate([grad_class_out[:, None], jnp.zeros_like(hidden[:, 1:])], 1)
    grad_start, grad_attn, grad_up, grad_down, grad_gains = block_backward(
        grad_hidden,
        saved_vals,
        pieces["image_attn"],
        pieces["image_up"],
        pieces["image_down"],
        image_vec[IMG_TOK + 3 : IMG_TOK + 7],
        IMG_HEADS,
    )
    pre_pull = jax.vjp(layer_norm, tokens, image_vec[IMG_TOK + 1], image_vec[IMG_TOK + 2])[1]
    grad_tokens, grad_gain_pre, grad_shift_pre = pre_pull(grad_start)
    grad_patch = weight_grad(pixels, grad_tokens[:, 1:].astype(jnp.bfloat16))
    grad_vec = jnp.concatenate(
        [
            jnp.sum(grad_tokens[:, 0], 0)[None],
            jnp.sum(grad_tokens, 0),
            grad_gain_pre[None],
            grad_shift_pre[None],
            grad_gains,
            grad_gain_post[None],
            grad_shift_post[None],
        ]
    )
    return ((grad_patch, grad_attn, grad_up, grad_down, grad_proj), grad_vec)


def text_forward(pieces, token_rows, end_pos):
    text_vec = pieces["text_vec"].astype(jnp.float32)
    start_rows = token_rows + text_vec[:CTX]
    hidden, saved_vals = block_forward(
        start_rows,
        pieces["text_attn"],
        pieces["text_up"],
        pieces["text_down"],
        text_vec[CTX : CTX + 4],
        TXT_HEADS,
        True,
    )
    final_rows = jnp.take_along_axis(hidden, end_pos[:, None, None], 1)[:, 0]
    head_in = layer_norm(final_rows, text_vec[CTX + 4], text_vec[CTX + 5]).astype(jnp.bfloat16)
    raw_embed = fwd_dot(head_in, pieces["text_proj"])
    return (unit_rows(raw_embed).astype(jnp.bfloat16), (saved_vals, final_rows, head_in, raw_embed))


def text_backward(pieces, kept_vals, grad_emb, end_pos):
    saved_vals, final_rows, head_in, raw_embed = kept_vals
    text_vec = pieces["text_vec"].astype(jnp.float32)
    grad_raw = jax.vjp(unit_rows, raw_embed)[1](grad_emb)[0].astype(jnp.bfloat16)
    grad_proj = weight_grad(head_in, grad_raw)
    final_pull = jax.vjp(layer_norm, final_rows, text_vec[CTX + 4], text_vec[CTX + 5])[1]
    grad_final, grad_gain_fin, grad_shift_fin = final_pull(back_dot(grad_raw, pieces["text_proj"]))
    picks = (jnp.arange(CTX)[None, :] == end_pos[:, None]).astype(jnp.float32)
    grad_hidden = picks[:, :, None] * grad_final[:, None, :]
    grad_start, grad_attn, grad_up, grad_down, grad_gains = block_backward(
        grad_hidden,
        saved_vals,
        pieces["text_attn"],
        pieces["text_up"],
        pieces["text_down"],
        text_vec[CTX : CTX + 4],
        TXT_HEADS,
    )
    grad_vec = jnp.concatenate(
        [jnp.sum(grad_start, 0), grad_gains, grad_gain_fin[None], grad_shift_fin[None]]
    )
    return ((grad_attn, grad_up, grad_down, grad_proj), grad_vec, grad_start.astype(jnp.bfloat16))


def side_terms(row_embed, columns, column_ok, same_rows, positives_own, logit_scale, total_count):
    dot_vals = back_dot(row_embed, columns)
    logits = logit_scale * dot_vals
    masked = jnp.where(column_ok[None, :], logits, -1e30)
    row_max = jnp.max(masked, 1, keepdims=True)
    log_total = row_max[:, 0] + jnp.log(jnp.sum(jnp.exp(masked - row_max), 1))
    weights_pos = jnp.concatenate(
        [
            same_rows,
            jnp.zeros((same_rows.shape[0], columns.shape[0] - same_rows.shape[1]), jnp.float32),
        ],
        1,
    )
    loss_part = -jnp.sum(weights_pos * (logits - log_total[:, None]))
    grad_logits = (
        positives_own[:, None] * jnp.exp(masked - log_total[:, None]) - weights_pos
    ) / total_count
    grad_dots = (logit_scale * grad_logits).astype(jnp.bfloat16)
    grad_temper = logit_scale * jnp.sum(grad_logits * dot_vals)
    grad_rows = fwd_dot(grad_dots, columns)
    grad_columns = weight_grad(grad_dots, row_embed)[: same_rows.shape[1]]
    return (loss_part, grad_temper, grad_rows, grad_columns, log_total)


def adam_step(weight, first, second, grad, rate, decay):
    first = beta_one * first + (1.0 - beta_one) * grad
    second = beta_two * second + (1.0 - beta_two) * grad * grad
    first_hat = first / (1.0 - beta_one**STEP)
    second_hat = second / (1.0 - beta_two**STEP)
    weight = weight - rate * (first_hat / (jnp.sqrt(second_hat) + adam_eps) + decay * weight)
    return (weight, first, second)


def body(
    flat_master,
    flat_first,
    flat_second,
    table,
    table_first,
    table_second,
    pixels,
    token_ids,
    end_pos,
    pair_counts,
    groups,
    cached_image,
    cached_text,
):
    device_count = lax.axis_size("gx") * lax.axis_size("gy")
    my_index = lax.axis_index("gx") * lax.axis_size("gy") + lax.axis_index("gy")
    pairs_dev = pixels.shape[0]
    weights_all = lax.all_gather(flat_master.astype(jnp.bfloat16), ("gx", "gy"), axis=0, tiled=True)
    pieces = unpack(weights_all)
    all_ids = lax.all_gather(token_ids, "gy", axis=0, tiled=True).reshape(-1)
    vocab_dev = table.shape[0]
    table_low = table.astype(jnp.bfloat16)
    row_base = lax.axis_index("gy") * vocab_dev
    wanted = all_ids - row_base
    inside = (wanted >= 0) & (wanted < vocab_dev)
    picked = jnp.take(table_low, jnp.clip(wanted, 0, vocab_dev - 1), axis=0)
    token_rows = (
        lax.psum_scatter(
            jnp.where(inside[:, None], picked.astype(jnp.float32), 0.0).astype(jnp.bfloat16),
            "gy",
            scatter_dimension=0,
            tiled=True,
        )
        .astype(jnp.float32)
        .reshape(pairs_dev, CTX, D_TXT)
    )
    image_emb, image_kept = image_forward(pieces, pixels)
    text_emb, text_kept = text_forward(pieces, token_rows, end_pos)
    all_img, all_txt, cache_img, cache_txt = (
        lax.all_gather(image_emb, ("gx", "gy"), axis=0, tiled=True),
        lax.all_gather(text_emb, ("gx", "gy"), axis=0, tiled=True),
        lax.all_gather(cached_image, ("gx", "gy"), axis=0, tiled=True),
        lax.all_gather(cached_text, ("gx", "gy"), axis=0, tiled=True),
    )
    total_pairs = all_img.shape[0]
    valid_all = jnp.arange(total_pairs) % pairs_dev < jnp.repeat(pair_counts.reshape(-1), pairs_dev)
    matches = (
        (groups[:, None] == groups[None, :]) & valid_all[:, None] & valid_all[None, :]
    ).astype(jnp.float32)
    positives_all = jnp.sum(matches, 1)
    total_count = 2.0 * jnp.sum(positives_all)
    own_start = my_index * pairs_dev
    same_own = lax.dynamic_slice_in_dim(matches, own_start, pairs_dev, 0)
    positives_own = lax.dynamic_slice_in_dim(positives_all, own_start, pairs_dev)
    logit_scale = jnp.exp(pieces["temper"].astype(jnp.float32)[0, 0])
    column_ok = jnp.concatenate([valid_all, jnp.ones((cache_img.shape[0],), jnp.bool_)])
    loss_one, temper_one, grad_img, txt_cols, log_img = side_terms(
        image_emb,
        jnp.concatenate([all_txt, cache_txt]),
        column_ok,
        same_own,
        positives_own,
        logit_scale,
        total_count,
    )
    loss_two, temper_two, grad_txt, img_cols, log_txt = side_terms(
        text_emb,
        jnp.concatenate([all_img, cache_img]),
        column_ok,
        same_own,
        positives_own,
        logit_scale,
        total_count,
    )
    back_img, back_txt = (
        lax.psum_scatter(img_cols, ("gx", "gy"), scatter_dimension=0, tiled=True),
        lax.psum_scatter(txt_cols, ("gx", "gy"), scatter_dimension=0, tiled=True),
    )
    grad_img = grad_img + back_img
    grad_txt = grad_txt + back_txt
    pixels_again, rows_again, grad_img, grad_txt = lax.optimization_barrier(
        (pixels, token_rows, grad_img, grad_txt)
    )
    image_again, image_kept = image_forward(pieces, pixels_again)
    text_again, text_kept = text_forward(pieces, rows_again, end_pos)
    image_mats, image_vec_grad = image_backward(pieces, pixels, image_kept, grad_img)
    text_mats, text_vec_grad, grad_rows = text_backward(pieces, text_kept, grad_txt, end_pos)
    wanted = all_ids - row_base
    inside = (wanted >= 0) & (wanted < vocab_dev)
    values = jnp.where(
        inside[:, None],
        lax.all_gather(grad_rows.reshape(-1, D_TXT), "gy", axis=0, tiled=True).astype(jnp.float32),
        0.0,
    )
    table_part = jax.ops.segment_sum(values, jnp.clip(wanted, 0, vocab_dev - 1), vocab_dev)
    table_grad = lax.psum(table_part.astype(jnp.bfloat16), "gx").astype(jnp.float32)
    used = sum((seg_rows * seg_cols for seg_name, seg_rows, seg_cols in segment_list()))
    matrix_stop = sum((seg_rows * seg_cols for seg_name, seg_rows, seg_cols in segment_list()[:9]))
    local_flat = jnp.concatenate(
        [part_grad.reshape(-1) for part_grad in image_mats + text_mats]
        + [
            image_vec_grad.reshape(-1),
            text_vec_grad.reshape(-1),
            (temper_one + temper_two).reshape(1),
            jnp.zeros((flat_master.shape[0] * device_count - used,), jnp.float32),
        ]
    )
    grad_shard = lax.psum_scatter(local_flat, ("gx", "gy"), scatter_dimension=0, tiled=True)
    table_squares = jnp.where(lax.axis_index("gx") == 0, jnp.sum(table_grad * table_grad), 0.0)
    squares = jnp.sum(grad_shard * grad_shard) + table_squares
    total_sq, loss_sum = lax.psum((squares, loss_one + loss_two), ("gx", "gy"))
    grad_norm = jnp.sqrt(total_sq)
    factor = jnp.minimum(1.0, clip_limit / (grad_norm + 1e-06))
    position = my_index * flat_master.shape[0] + jnp.arange(flat_master.shape[0])
    is_matrix = position < matrix_stop
    rates = jnp.where(is_matrix, rate_matrix, rate_vector)
    decays = jnp.where(is_matrix, decay_rate, 0.0)
    master_out, first_out, second_out = adam_step(
        flat_master, flat_first, flat_second, grad_shard * factor, rates, decays
    )
    table_out, table_first_out, table_second_out = adam_step(
        table, table_first, table_second, table_grad * factor, rate_table, 0.0
    )
    return (
        master_out,
        first_out,
        second_out,
        table_out,
        table_first_out,
        table_second_out,
        loss_sum,
        total_count,
        grad_norm,
    )


def solution(mesh):
    placed = (
        P(("gx", "gy")),
        P(("gx", "gy")),
        P(("gx", "gy")),
        P("gy", None),
        P("gy", None),
        P("gy", None),
        P(("gx", "gy"), None, None),
        P(("gx", "gy"), None),
        P(("gx", "gy")),
        P(),
        P(),
        P(("gx", "gy"), None),
        P(("gx", "gy"), None),
    )
    return jax.shard_map(
        body,
        mesh=mesh,
        in_specs=placed,
        out_specs=(
            P(("gx", "gy")),
            P(("gx", "gy")),
            P(("gx", "gy")),
            P("gy", None),
            P("gy", None),
            P("gy", None),
            P(),
            P(),
            P(),
        ),
        check_vma=False,
    )
```

profile of v0, /device:TPU:0, one launch (start us, length us, event | category | flops | bytes accessed | tf_op | source)
XLA Modules:
  0.0 2814.5 jit_solution(11771955576273774978)
XLA Ops:
  8.1 32.5 %all_gather.21 = s32[64,77]{1,0:T(8,128)S(1)} all-gather(s32[8,77]{1,0:T(8,128)} %param.22), channel_id=1, replica_groups=mesh['gx'=4,'gy'=8] {'gy'}, dimensions={0}, use_global_device_ids=true | all-gather | bytes 22176 | tf_op jit(solution)/shard_map/all_gather | solution.py:365
  41.0 8.1 convert_element_type.218
  49.3 19.0 gather_fusion
  68.2 7.6 select_convert_fusion
  77.4 9.0 broadcast.818
  86.5 13.5 dynamic-update-slice
  104.9 76.2 %all_gather.24 = bf16[256,512]{1,0:T(8,128)(2,1)} all-gather(bf16[8,512]{1,0:T(8,128)(2,1)S(1)} %copy-done.112), channel_id=1, replica_groups=mesh['gx'=4,'gy'=8] {'gx','gy'}, dimensions={0}, use_global_device_ids=true | all-gather | bytes 270336 | tf_op jit(solution)/shard_map/all_gather | solution.py:388
  181.1 75.7 %all_gather.26 = bf16[256,512]{1,0:T(8,128)(2,1)} all-gather(bf16[8,512]{1,0:T(8,128)(2,1)S(1)} %copy-done.113), channel_id=1, replica_groups=mesh['gx'=4,'gy'=8] {'gx','gy'}, dimensions={0}, use_global_device_ids=true | all-gather | bytes 270336 | tf_op jit(solution)/shard_map/all_gather | solution.py:387
  260.1 293.8 %all-reduce.12.cloned.1.call-done = bf16[13326112]{0:T(1024)(128)(2,1)} async-done(((bf16[13326112]{0:T(1024)(128)(2,1)}), bf16[13326112]{0:T(1024)(128)(2,1)}) %all-reduce.12.cloned.1.call-update) | async-done | bytes 26652240
  557.7 13.8 fusion.219
  571.5 9.2 reshape.985
  580.8 4.4 convolution_bitcast_fusion.8
  592.2 8.2 reshape.889
  602.7 3.8 convolution_convert_fusion.1
  628.1 3.4 fusion.230
  633.4 8.2 reshape.988
  641.7 9.2 reshape.989
  652.5 9.7 fusion.22
  675.8 5.7 fusion.220
  681.6 4.2 reshape.897
  697.3 4.2 fusion.227
  707.3 4.2 reshape.992
  711.5 4.3 reshape.993
  715.8 7.2 fusion.45
  730.7 67.6 %all_gather.23 = bf16[256,512]{1,0:T(8,128)(2,1)S(1)} all-gather(bf16[8,512]{1,0:T(8,128)(2,1)S(1)} %multiply_convert_fusion.19), channel_id=1, replica_groups=mesh['gx'=4,'gy'=8] {'gx','gy'}, dimensions={0}, use_global_device_ids=true | all-gather | bytes 270336 | tf_op jit(solution)/shard_map/all_gather | solution.py:386
  800.3 64.8 %all_gather.25 = bf16[256,512]{1,0:T(8,128)(2,1)S(1)} all-gather(bf16[8,512]{1,0:T(8,128)(2,1)S(1)} %multiply_convert_fusion.20), channel_id=1, replica_groups=mesh['gx'=4,'gy'=8] {'gx','gy'}, dimensions={0}, use_global_device_ids=true | all-gather | bytes 270336 | tf_op jit(solution)/shard_map/all_gather | solution.py:385
  871.0 129.5 %reduce-scatter.8.cloned.1.call-done = f32[8,512]{1,0:T(8,128)} async-done(((f32[256,512]{1,0:T(8,128)}), f32[8,512]{1,0:T(8,128)}) %reduce-scatter.8.cloned.1.call-update) | async-done | bytes 16400 | tf_op jit(solution)/shard_map/reduce_scatter | solution.py:422
  1001.7 131.7 %reduce-scatter.6.cloned.1.call-done = f32[8,512]{1,0:T(8,128)} async-done(((f32[256,512]{1,0:T(8,128)}), f32[8,512]{1,0:T(8,128)}) %reduce-scatter.6.cloned.1.call-update) | async-done | bytes 16400 | tf_op jit(solution)/shard_map/reduce_scatter | solution.py:421
  1146.3 4.2 fusion.233
  1155.6 3.8 multiply_convert_fusion.2
  1166.3 5.5 fusion.19
  1203.3 4.0 convolution_convert_fusion
  1232.1 3.6 fusion.232
  1239.2 5.5 multiply_convert_fusion
  1244.7 5.7 fusion.238
  1252.6 3.8 fusion.15
  1261.0 3.4 fusion.216
  1272.6 4.4 fusion.42
  1285.0 3.9 convolution_bitcast_fusion.5
  1288.9 4.0 convolution_bitcast_fusion.6
  1300.0 5.0 multiply_reduce_fusion.6
  1312.1 8.3 convolution_bitcast_fusion
  1340.6 3.4 reshape.1016
  1345.5 4.6 fusion.235
  1355.3 4.2 fusion.208
  1369.1 5.5 copy.614
  1388.4 11.0 reshape.917
  1400.5 4.9 convolution_bitcast_fusion.3
  1405.4 5.7 copy.610
  1417.7 5.0 convolution_bitcast_fusion.2
  1422.7 8.1 maximum_bitcast_fusion
  1430.9 9.8 copy.609
  1440.7 40.1 %all-gather.2.cloned.1.call-done = bf16[4928,512]{1,0:T(8,128)(2,1)} async-done(((bf16[616,512]{1,0:T(8,128)(2,1)}), bf16[4928,512]{1,0:T(8,128)(2,1)}) %all-gather.2.cloned.1.call-update) | async-done | bytes 5046288 | tf_op jit(solution)/shard_map/all_gather | solution.py:437
  1480.8 45.9 %scatter_custom_fusion = f32[6176,512]{1,0:T(8,128)} fusion(s32[4928]{0:T(1024)} %copy-done.73, bf16[4928,512]{1,0:T(8,128)(2,1)} %all-gather.2.cloned.1.call-done, f32[]{:T(128)} %constant.162.clone.1, pred[4928]{0:T(1024)(128)(4,1)S(1)} %copy-done.79), kind=kCustom, calls=%fused_computation.16 | custom fusion | flops 7569408 | bytes 17700672 | tf_op jit(solution)/shard_map/scatter-add | solution.py:440
  1526.7 8.0 convert_element_type.284
  1534.8 6.8 convolution_bitcast_fusion.1
  1541.6 9.6 copy.508
  1551.2 10.8 reshape.913
  1562.0 405.2 %concatenate.58 = f32[13326112]{0:T(1024)} concatenate(f32[2359296]{0:T(1024)} %reshape.913, f32[2359296]{0:T(1024)} %bitcast.301, f32[2359296]{0:T(1024)} %bitcast.300, f32[2359296]{0:T(1024)} %reshape.917, f32[393216]{0:T(1024)} %bitcast.305, f32[1048576]{0:T(1024)} %bitcast.304, f32[1048576]{0:T(1024)} %bitcast.303, f32[1048576]{0:T(1024)} %bitcast.302, f32[262144]{0:T(1024)S(1)} %bitcast.312, ...), dimensions={0} | concatenate | bytes 106608896 | tf_op jit(solution)/shard_map/concatenate | solution.py:444
  1968.6 6.9 fusion.6
  1976.1 746.9 %all-reduce.14.cloned.1.call-done = f32[13326112]{0:T(1024)} async-done(((f32[13326112]{0:T(1024)}), f32[13326112]{0:T(1024)}) %all-reduce.14.cloned.1.call-update) | async-done | bytes 53304464
  2726.2 39.7 %all-reduce.5 = (f32[]{:T(128)}, f32[]{:T(128)}) all-reduce(f32[]{:T(128)S(6)} %add.572, f32[]{:T(128)S(6)} %add.584), channel_id=1, replica_groups=mesh['gx'=4,'gy'=8] {'gx','gy'}, use_global_device_ids=true, to_apply=%region_91.93 | all-reduce | flops 2 | bytes 16 | tf_op jit(solution)/shard_map/psum | solution.py:456
  2766.7 30.7 %multiply_subtract_fusion = (f32[6176,512]{1,0:T(8,128)}, f32[6176,512]{1,0:T(8,128)}, f32[6176,512]{1,0:T(8,128)}) fusion(f32[6176,512]{1,0:T(8,128)} %param.18, f32[]{:T(128)S(6)} %min.24, bf16[6176,512]{1,0:T(8,128)(2,1)} %all-reduce.10.cloned.1.call-done, f32[6176,512]{1,0:T(8,128)} %param.19, f32[6176,512]{1,0:T(8,128)} %param.20), kind=kLoop, calls=%fused_computation.15 | loop fusion | flops 53755904 | bytes 82214912 | tf_op jit(solution)/shard_map/sub | solution.py:341
  2797.4 7.0 multiply_subtract_fusion.1
  (592 shorter events, 274.5 us)
Async XLA Ops:
  8.0 572.7 %copy-start = (bf16[8,49,3072]{2,0,1:T(8,128)(2,1)S(1)}, bf16[8,49,3072]{2,0,1:T(8,128)(2,1)}, u32[]{:S(2)}) copy-start(bf16[8,49,3072]{2,0,1:T(8,128)(2,1)} %param.21) | copy-start | bytes 7225348
  8.0 249.8 %reduce-scatter.4.cloned.1.call-start = ((), (), s32[]{:S(2)}) async-start(), calls=%async_computation.3 | async-start | bytes 5677056 | tf_op jit(solution)/shard_map/reduce_scatter | solution.py:373
  40.7 8.4 copy-start.73
  49.2 19.0 copy-start.78
  75.9 478.1 %all-reduce.12.cloned.1.call-start = ((), (), s32[]{:S(2)}) async-start(), calls=%async_computation.8 | async-start | bytes 53305344
  99.9 5.0 copy-start.112
  99.9 81.1 %copy-start.113 = (bf16[8,512]{1,0:T(8,128)(2,1)S(1)}, bf16[8,512]{1,0:T(8,128)(2,1)}, u32[]{:S(2)}) copy-start(bf16[8,512]{1,0:T(8,128)(2,1)} %param.26) | copy-start | bytes 24580
  100.0 900.5 %reduce-scatter.8.cloned.1.call-start = ((), (), s32[]{:S(2)}) async-start(), calls=%async_computation.5 | async-start | bytes 540672 | tf_op jit(solution)/shard_map/reduce_scatter | solution.py:422
  555.5 45.0 %copy-start.68 = (f32[768]{0:T(1024)}, f32[768]{0:T(1024)S(1)}, u32[]{:S(2)}) copy-start(f32[768]{0:T(1024)S(1)} %get-tuple-element.101) | copy-start | bytes 9220
  555.5 45.0 %copy-start.82 = (f32[768]{0:T(1024)}, f32[768]{0:T(1024)S(1)}, u32[]{:S(2)}) copy-start(f32[768]{0:T(1024)S(1)} %get-tuple-element.100) | copy-start | bytes 9220
  555.5 72.7 %copy-start.62 = (f32[768]{0:T(1024)}, f32[768]{0:T(1024)S(1)}, u32[]{:S(2)}) copy-start(f32[768]{0:T(1024)S(1)} %get-tuple-element.102) | copy-start | bytes 9220
  555.5 95.4 %copy-start.71 = (f32[768]{0:T(1024)}, f32[768]{0:T(1024)S(1)}, u32[]{:S(2)}) copy-start(f32[768]{0:T(1024)S(1)} %get-tuple-element.96) | copy-start | bytes 9220
  555.5 95.4 %copy-start.80 = (f32[768]{0:T(1024)}, f32[768]{0:T(1024)S(1)}, u32[]{:S(2)}) copy-start(f32[768]{0:T(1024)S(1)} %get-tuple-element.99) | copy-start | bytes 9220
  692.8 4.5 copy-start.107
  711.5 4.4 copy-start.74
  711.5 4.4 copy-start.76
  723.1 4.5 copy-start.97
  723.1 4.9 slice-start.1
  729.1 136.0 %copy-start.50 = (bf16[256,512]{1,0:T(8,128)(2,1)S(1)}, bf16[256,512]{1,0:T(8,128)(2,1)}, u32[]{:S(2)}) copy-start(bf16[256,512]{1,0:T(8,128)(2,1)} %all_gather.24) | copy-start | bytes 786436
  729.1 136.0 %copy-start.49 = (bf16[256,512]{1,0:T(8,128)(2,1)S(1)}, bf16[256,512]{1,0:T(8,128)(2,1)}, u32[]{:S(2)}) copy-start(bf16[256,512]{1,0:T(8,128)(2,1)} %all_gather.26) | copy-start | bytes 786436
  730.6 134.6 %copy-start.114 = (pred[512]{0:T(512)(128)(4,1)S(1)}, pred[512]{0:T(512)(128)(4,1)}, u32[]{:S(2)}) copy-start(pred[512]{0:T(512)(128)(4,1)} %concatenate.45) | copy-start | bytes 1540
  868.4 265.0 %reduce-scatter.6.cloned.1.call-start = ((), (), s32[]{:S(2)}) async-start(), calls=%async_computation.4 | async-start | bytes 540672 | tf_op jit(solution)/shard_map/reduce_scatter | solution.py:421
  869.6 611.2 %all-gather.2.cloned.1.call-start = ((), (), s32[]{:S(2)}) async-start(), calls=%async_computation.6 | async-start | bytes 5677056 | tf_op jit(solution)/shard_map/all_gather | solution.py:437
  869.7 304.6 %copy-start.84 = (f32[8,77]{1,0:T(8,128)}, f32[8,77]{1,0:T(8,128)S(1)}, u32[]{:S(2)}) copy-start(f32[8,77]{1,0:T(8,128)S(1)} %fusion.179) | copy-start | bytes 7396
  1155.2 4.2 copy-start.9
  1164.3 7.4 copy-start.115
  1164.5 7.2 copy-start.120
  1165.0 6.8 copy-start.94
  1166.3 5.5 copy-start.10
  1166.3 5.5 copy-start.43
  1185.9 5.1 slice-start.6
  1200.9 6.4 copy-start.92
  1239.1 5.5 copy-start.60
  1244.6 5.8 copy-start.132
  1244.6 8.0 slice-start.4
  1244.6 5.8 copy-start.12
  1244.7 6.1 copy-start.14
  1244.7 6.1 copy-start.67
  1244.7 6.1 copy-start.75
  1244.7 7.9 slice-start.5
  1244.7 11.8 slice-start.2
  1272.6 4.4 copy-start.20
  1272.6 4.4 copy-start.45
  1272.6 4.4 copy-start.46
  1295.2 4.7 copy-start.87
  1295.2 4.7 copy-start.105
  1295.2 4.8 copy-start.109
  1300.0 5.0 copy-start.6
  1300.0 5.0 copy-start.53
  1300.0 5.0 copy-start.54
  1300.0 5.0 copy-start.55
  1300.0 5.0 copy-start.124
  1312.1 8.3 copy-start.41
  1312.1 9.3 copy-start.23
  1345.5 4.7 copy-start.65
  1345.5 5.8 copy-start.2
  1355.3 4.3 copy-start.91
  1369.1 5.5 copy-start.13
  1388.4 11.0 copy-start.39
  1400.4 568.2 %all-reduce.10.cloned.1.call-start = ((), (), s32[]{:S(2)}) async-start(), calls=%async_computation.7 | async-start | bytes 12648448 | tf_op jit(solution)/shard_map/psum | solution.py:441
  1405.4 5.8 copy-start.33
  1430.8 50.0 %copy-start.79 = (pred[4928]{0:T(1024)(128)(4,1)S(1)}, pred[4928]{0:T(1024)(128)(4,1)}, u32[]{:S(2)}) copy-start(pred[4928]{0:T(1024)(128)(4,1)} %copy-done.78) | copy-start | bytes 14788
  1534.7 1188.3 %all-reduce.14.cloned.1.call-start = ((), (), s32[]{:S(2)}) async-start(), calls=%async_computation.9 | async-start | bytes 106610688
  1551.2 10.8 copy-start.27
  (85 other events, 196.8 us)
Sparse Core Ops, SparseCore 0:
  76.0 137.9 reduce-scatter.3
  1400.5 80.2 all-gather.1
Sparse Core Ops, SparseCore 1:
  100.1 453.8 all-reduce.11
  868.5 132.0 reduce-scatter.7
  1003.2 130.2 reduce-scatter.5
  1534.8 118.0 all-reduce.9
  1967.4 755.6 all-reduce.13
where the time goes:
time: 2850 us; the launch traced here: 2810 us
  waiting for transfers between devices  1340 us (47%)
  local copies, waits for them, and re-layouts  706 us (25%)
  blocking collectives  356 us (12%)
  other arithmetic  194 us (7%)
  matrix products  190 us (7%)
    unnamed x9, waiting for transfers between devices  1040 us
    concatenate x1, local copies, waits for them, and re-layouts, body(): jnp.concatenate([part_grad.reshape(-1) for part_grad in image_mats + text...  405 us
    reduce_scatter x1, waiting for transfers between devices, body(): lax.psum_scatter(img_cols, ('gx', 'gy'), scatter_dimension=0, tiled=True)  132 us
    reduce_scatter x1, waiting for transfers between devices, body(): lax.psum_scatter(txt_cols, ('gx', 'gy'), scatter_dimension=0, tiled=True)  129 us
    all_gather x1, blocking collectives, body(): lax.all_gather(cached_text, ('gx', 'gy'), axis=0, tiled=True)  76.2 us
    all_gather x1, blocking collectives, body(): lax.all_gather(cached_image, ('gx', 'gy'), axis=0, tiled=True)  75.7 us
    unnamed x295, local copies, waits for them, and re-layouts  69.7 us
    dot_general x22, matrix products, fwd_dot(): return jnp.dot(left_side, right_side, preferred_element_type=jnp.float32)  68.7 us
  transfers between devices with their start and end apart: 7, of which 5 were waited for; matrix products, arithmetic and copies ran while one was open for 18% of the time, Pallas kernels for 0%

commit v1 on v0

v1 whole, which is shorter than its diff:
```python
import functools

import jax
import jax.numpy as jnp
from jax import lax
from jax.experimental import pallas as pl
from jax.experimental.pallas import tpu as pltpu
from jax.sharding import PartitionSpec as P

D_IMG = 768
IMG_HEADS = 12
IMG_MLP = 3072
PATCH_DIM = 3072
D_TXT = 512
TXT_HEADS = 8
TXT_MLP = 2048
CTX = 77
EMBED = 512
STEP = 10
IMG_TOK = 50


clip_limit = 0.1
beta_one = 0.9
beta_two = 0.999
adam_eps = 1e-08
decay_rate = 0.1
rate_matrix = 0.01
rate_vector = 0.2
rate_table = 0.2
norm_eps = 1e-05


def segment_list():
    return [
        ("patch_embed", PATCH_DIM, D_IMG),
        ("image_attn", D_IMG, 4 * D_IMG),
        ("image_up", D_IMG, IMG_MLP),
        ("image_down", IMG_MLP, D_IMG),
        ("image_proj", D_IMG, EMBED),
        ("text_attn", D_TXT, 4 * D_TXT),
        ("text_up", D_TXT, TXT_MLP),
        ("text_down", TXT_MLP, D_TXT),
        ("text_proj", D_TXT, EMBED),
        ("image_vec", IMG_TOK + 9, D_IMG),
        ("text_vec", CTX + 6, D_TXT),
        ("temper", 1, 1),
    ]


LANES = 128
GROUP = 16
CHUNKS = 16
GATHER_CHUNKS = 14
CACHED_ROWS = 64
ID_ROWS = 16
MESH = pl.DeviceIdType.MESH


def dot_nn(left_side, right_side):
    return lax.dot_general(
        left_side, right_side, (((1,), (0,)), ((), ())), preferred_element_type=jnp.float32
    )


def dot_nt(left_side, right_side):
    return lax.dot_general(
        left_side, right_side, (((1,), (1,)), ((), ())), preferred_element_type=jnp.float32
    )


def dot_tn(left_side, right_side):
    return lax.dot_general(
        left_side, right_side, (((0,), (0,)), ((), ())), preferred_element_type=jnp.float32
    )


def back_dot(left_side, right_side):
    return dot_nt(left_side, right_side)


def fwd_dot(left_side, right_side):
    return dot_nn(left_side, right_side)


def weight_grad(left_side, right_side):
    return dot_tn(left_side, right_side)


def norm_parts(values):
    center = values - jnp.mean(values, -1, keepdims=True)
    scale = lax.rsqrt(jnp.mean(center * center, -1, keepdims=True) + norm_eps)
    return center * scale, scale


def layer_norm(values, gain_vec, shift_vec):
    return norm_parts(values)[0] * gain_vec + shift_vec


def layer_norm_back(values, gain_vec, grad):
    unit, scale = norm_parts(values)
    grad_unit = grad * gain_vec
    inner = jnp.mean(grad_unit, -1, keepdims=True)
    along = jnp.mean(grad_unit * unit, -1, keepdims=True)
    return scale * (grad_unit - inner - unit * along), grad * unit


def sum_rows(values):
    return jnp.sum(values, 0, keepdims=True)


def low16(values):
    return jnp.concatenate([values, jnp.zeros_like(values)], 0).astype(jnp.bfloat16)


SEQS = 8


class Tower:
    def __init__(self, image):
        self.image = image
        self.width = D_IMG if image else D_TXT
        self.heads = IMG_HEADS if image else TXT_HEADS
        self.length = IMG_TOK if image else CTX
        self.rows = -(-SEQS * self.length // GROUP) * GROUP
        self.lanes = 16 if image else 8
        self.queries = SEQS * self.lanes
        self.block = 80 if image else 48
        self.names = ("patch", "attn", "up", "down", "proj") if image else ("attn", "up", "down", "proj")

    def shapes(self):
        width = self.width
        found = dict(attn=(width, 4 * width), up=(width, 4 * width), down=(4 * width, width), proj=(width, EMBED))
        if self.image:
            found["patch"] = (PATCH_DIM, width)
        return found

    def head_mask(self):
        lane = lax.broadcasted_iota(jnp.int32, (self.lanes, self.width), 1)
        row = lax.broadcasted_iota(jnp.int32, (self.lanes, self.width), 0)
        return lane // (self.width // self.heads) == row

    def spread_heads(self, values, wide_ref):
        mask = self.head_mask()
        for s in range(SEQS):
            row = jnp.broadcast_to(values[s : s + 1].astype(jnp.float32), mask.shape)
            wide_ref[s * self.lanes : (s + 1) * self.lanes, :] = jnp.where(mask, row, 0.0)
        return wide_ref[...].astype(jnp.bfloat16)

    def join_heads(self, values, wide_ref):
        mask = self.head_mask()
        wide_ref[...] = values
        rows = [
            sum_rows(jnp.where(mask, wide_ref[s * self.lanes : (s + 1) * self.lanes, :], 0.0))
            for s in range(SEQS)
        ]
        return jnp.concatenate(rows, 0)

    def row_of(self, s, ends_ref):
        return s * self.length + (0 if self.image else ends_ref[s])

    def each_block(self, function, start):
        return lax.fori_loop(
            0,
            self.rows // self.block,
            lambda i, carry: function(pl.ds(pl.multiple_of(i * self.block, GROUP), self.block), carry),
            start,
        )


def tower_fetch(names, sources, landed, sems):
    copies = {
        name: pltpu.make_async_copy(source, ref, sems.at[i])
        for i, (name, source, ref) in enumerate(zip(names, sources, landed))
    }
    for copy in copies.values():
        copy.start()
    return copies, dict(zip(names, landed))


def tower_forward_kernel(tower, *refs):
    count = len(tower.names)
    ends_ref, gains_ref, base_ref, input_ref = refs[:4]
    sources = refs[4 : 4 + count]
    (tokens_ref, normed_ref, pair_ref, normed_own_ref, query_ref, probs_ref, attended_ref, middle_ref, normed_two_ref,
     upper_ref, act_ref, output_ref, head_ref, raw_ref, emb_ref) = refs[4 + count : 19 + count]
    hidden_ref, wide_ref = refs[19 + count : 21 + count]
    landed, sems = refs[21 + count : 21 + 2 * count], refs[21 + 2 * count]
    copies, weights = tower_fetch(tower.names, sources, landed, sems)
    width = tower.width
    gains = [gains_ref[i : i + 1, :] for i in range(8)]
    if tower.image:
        copies["patch"].wait()

        def patch(j, carry):
            cols = pl.ds(pl.multiple_of(j * 256, 256), 256)
            tokens_ref[:, cols] = dot_nn(input_ref[...], weights["patch"][:, cols]) + base_ref[:, cols]
            return carry

        lax.fori_loop(0, width // 256, patch, 0)

    def first(rows, carry):
        if tower.image:
            hidden = layer_norm(tokens_ref[rows, :], gains[0], gains[1])
        else:
            hidden = input_ref[rows, :].astype(jnp.float32) + base_ref[rows, :]
            tokens_ref[rows, :] = hidden
        hidden_ref[rows, :] = hidden
        normed_ref[rows, :] = layer_norm(hidden, gains[2], gains[3]).astype(jnp.bfloat16)
        return carry

    tower.each_block(first, 0)
    copies["attn"].wait()

    def pair(j, carry):
        at = pl.multiple_of(j * 256, 256)
        product = dot_nn(normed_ref[...], weights["attn"][:, pl.ds(width + at, 256)])
        pair_ref[:, pl.ds(at, 256)] = product.astype(jnp.bfloat16)
        return carry

    lax.fori_loop(0, 2 * width // 256, pair, 0)
    hidden_own = jnp.concatenate(
        [hidden_ref[pl.ds(tower.row_of(s, ends_ref), 1), :] for s in range(SEQS)], 0
    )
    normed_own = low16(layer_norm(hidden_own, gains[2], gains[3]))
    normed_own_ref[...] = normed_own
    query = dot_nn(normed_own, weights["attn"][:, :width]).astype(jnp.bfloat16)
    query_ref[...] = query
    queries = tower.spread_heads(query, wide_ref)
    scores = dot_nt(queries, pair_ref[:, :width]) * (width // tower.heads) ** (-0.5)
    row = lax.broadcasted_iota(jnp.int32, scores.shape, 0) // tower.lanes
    spot = lax.broadcasted_iota(jnp.int32, scores.shape, 1) - row * tower.length
    last = jnp.full(scores.shape, tower.length - 1, jnp.int32)
    if not tower.image:
        for s in range(SEQS):
            last = jnp.where(row == s, ends_ref[s], last)
    scores = jnp.where((spot >= 0) & (spot <= last), scores, -1e30)
    powers = jnp.exp(scores - jnp.max(scores, -1, keepdims=True))
    probs = powers / jnp.sum(powers, -1, keepdims=True)
    probs_ref[...] = probs
    attended = low16(tower.join_heads(dot_nn(probs.astype(jnp.bfloat16), pair_ref[:, width:]), wide_ref))
    attended_ref[...] = attended
    middle = hidden_own + dot_nn(attended, weights["attn"][:, 3 * width :])[:SEQS]
    middle_ref[...] = middle
    normed_two_ref[...] = low16(layer_norm(middle, gains[4], gains[5]))
    copies["up"].wait()

    def rise(j, carry):
        cols = pl.ds(pl.multiple_of(j * 512, 512), 512)
        upper = dot_nn(normed_two_ref[...], weights["up"][:, cols])[:SEQS]
        upper_ref[:, cols] = upper
        act_ref[:, cols] = low16(upper * jax.nn.sigmoid(1.702 * upper))
        return carry

    lax.fori_loop(0, 4 * width // 512, rise, 0)
    copies["down"].wait()

    def fall(j, carry):
        cols = pl.ds(pl.multiple_of(j * 256, 256), 256)
        output_ref[:, cols] = middle_ref[:, cols] + dot_nn(act_ref[...], weights["down"][:, cols])[:SEQS]
        return carry

    lax.fori_loop(0, width // 256, fall, 0)
    head_in = low16(layer_norm(output_ref[...], gains[6], gains[7]))
    head_ref[...] = head_in
    copies["proj"].wait()
    raw = dot_nn(head_in, weights["proj"][...])[:SEQS]
    raw_ref[...] = raw
    emb_ref[...] = raw * lax.rsqrt(jnp.sum(raw * raw, -1, keepdims=True) + 1e-06)


def tower_forward(tower, ends, gains, base, inputs, weights):
    width, rows = tower.width, tower.rows
    low, full = jnp.bfloat16, jnp.float32
    outs = [
        ((rows, width), full),
        ((rows, width), low),
        ((rows, 2 * width), low),
        ((GROUP, width), low),
        ((GROUP, width), low),
        ((tower.queries, rows), full),
        ((GROUP, width), low),
        ((SEQS, width), full),
        ((GROUP, width), low),
        ((SEQS, 4 * width), full),
        ((GROUP, 4 * width), low),
        ((SEQS, width), full),
        ((GROUP, width), low),
        ((SEQS, EMBED), full),
        ((SEQS, EMBED), full),
    ]
    vmem = pl.BlockSpec(memory_space=pltpu.VMEM)
    shapes = tower.shapes()
    return pl.pallas_call(
        functools.partial(tower_forward_kernel, tower),
        out_shape=[jax.ShapeDtypeStruct(shape, kind) for shape, kind in outs],
        in_specs=[pl.BlockSpec(memory_space=pltpu.SMEM)]
        + [vmem] * 3
        + [pl.BlockSpec(memory_space=pl.ANY)] * len(tower.names),
        out_specs=[vmem] * len(outs),
        scratch_shapes=[pltpu.VMEM((rows, width), full), pltpu.VMEM((tower.queries, width), full)]
        + [pltpu.VMEM(shapes[name], low) for name in tower.names]
        + [pltpu.SemaphoreType.DMA((len(tower.names),))],
        compiler_params=pltpu.CompilerParams(vmem_limit_bytes=58 << 20),
        name="image_forward" if tower.image else "text_forward",
    )(ends, gains, base, inputs, *[weights[name] for name in tower.names])


def tower_backward_kernel(tower, *refs):
    names = tower.names[-4:]
    count = len(names)
    ends_ref, gains_ref, grad_ref = refs[:3]
    (tokens_ref, normed_ref, pair_ref, normed_own_ref, query_ref, probs_ref, attended_ref, middle_ref, normed_two_ref,
     upper_ref, act_ref, output_ref, head_ref, raw_ref) = refs[3:17]
    sources = refs[17 : 17 + count]
    (grad_raw_ref, grad_mlp_ref, grad_upper_ref, grad_att_ref, grad_query_ref, grad_pair_ref, grad_rows_ref,
     places_ref, gain_grads_ref) = refs[17 + count : 26 + count]
    grad_ref_wide, wide_ref, grad_middle_ref = refs[26 + count : 29 + count]
    landed, sems = refs[29 + count : 29 + 2 * count], refs[29 + 2 * count]
    copies, weights = tower_fetch(names, sources, landed, sems)
    width, rows = tower.width, tower.rows
    scale = (width // tower.heads) ** (-0.5)
    gains = [gains_ref[i : i + 1, :] for i in range(8)]
    raw, grad_emb = raw_ref[...], grad_ref[...]
    norm = lax.rsqrt(jnp.sum(raw * raw, -1, keepdims=True) + 1e-06)
    along = jnp.sum(raw * grad_emb, -1, keepdims=True)
    grad_raw = low16(grad_emb * norm - raw * (norm * norm * norm * along))
    grad_raw_ref[...] = grad_raw
    copies["proj"].wait()
    grad_head = dot_nt(grad_raw, weights["proj"][...])[:SEQS]
    grad_out, gain_part = layer_norm_back(output_ref[...], gains[6], grad_head)
    gain_grads_ref[6:7, :] = sum_rows(gain_part)
    gain_grads_ref[7:8, :] = sum_rows(grad_head)
    grad_mlp_ref[...] = low16(grad_out)
    copies["down"].wait()

    def rise(j, carry):
        cols = pl.ds(pl.multiple_of(j * 512, 512), 512)
        grad_act = dot_nt(grad_mlp_ref[...], weights["down"][cols, :])[:SEQS]
        upper = upper_ref[:, cols]
        sig = jax.nn.sigmoid(1.702 * upper)
        grad_upper_ref[:, cols] = low16(grad_act * (sig + upper * (1.702 * (sig * (1.0 - sig)))))
        return carry

    lax.fori_loop(0, 4 * width // 512, rise, 0)
    copies["up"].wait()

    def fall(j, carry):
        cols = pl.ds(pl.multiple_of(j * 256, 256), 256)
        grad_middle_ref[:, cols] = dot_nt(grad_upper_ref[...], weights["up"][cols, :])[:SEQS]
        return carry

    lax.fori_loop(0, width // 256, fall, 0)
    grad_norm_two = grad_middle_ref[...]
    grad_mid, gain_part = layer_norm_back(middle_ref[...], gains[4], grad_norm_two)
    gain_grads_ref[4:5, :] = sum_rows(gain_part)
    gain_grads_ref[5:6, :] = sum_rows(grad_norm_two)
    grad_middle = grad_out + grad_mid
    grad_middle_ref[...] = grad_middle
    grad_att = low16(grad_middle)
    grad_att_ref[...] = grad_att
    copies["attn"].wait()
    grad_attended = dot_nt(grad_att, weights["attn"][:, 3 * width :]).astype(jnp.bfloat16)
    grads_heads = tower.spread_heads(grad_attended, wide_ref)
    queries = tower.spread_heads(query_ref[...], wide_ref)
    probs = probs_ref[...]
    grad_probs = dot_nt(grads_heads, pair_ref[:, width:])
    grad_scores = probs * (grad_probs - jnp.sum(grad_probs * probs, -1, keepdims=True))
    grad_scores = grad_scores.astype(jnp.bfloat16)
    grad_query = low16(tower.join_heads(dot_nn(grad_scores, pair_ref[:, :width]), wide_ref) * scale)
    grad_query_ref[...] = grad_query
    grad_pair_ref[:, :width] = (dot_tn(grad_scores, queries) * scale).astype(jnp.bfloat16)
    grad_pair_ref[:, width:] = dot_tn(probs.astype(jnp.bfloat16), grads_heads).astype(jnp.bfloat16)

    def inner(j, carry):
        at = pl.multiple_of(j * 256, 256)
        grad_ref_wide[:, pl.ds(at, 256)] = dot_nt(
            grad_pair_ref[...], weights["attn"][pl.ds(at, 256), width : 3 * width]
        )
        return carry

    lax.fori_loop(0, width // 256, inner, 0)
    grad_own = dot_nt(grad_query, weights["attn"][:, :width])
    for s in range(SEQS):
        grad_ref_wide[pl.ds(tower.row_of(s, ends_ref), 1), :] += grad_own[s : s + 1]

    def first(at, carry):
        grad = grad_ref_wide[at, :]
        hidden = tokens_ref[at, :]
        if tower.image:
            hidden = layer_norm(hidden, gains[0], gains[1])
        grad_in, gain_part = layer_norm_back(hidden, gains[2], grad)
        grad_ref_wide[at, :] = grad_in
        return carry[0] + sum_rows(gain_part), carry[1] + sum_rows(grad)

    nothing = jnp.zeros((1, width), jnp.float32)
    gain_one, shift_one = tower.each_block(first, (nothing, nothing))
    gain_grads_ref[2:3, :] = gain_one
    gain_grads_ref[3:4, :] = shift_one
    for s in range(SEQS):
        grad_ref_wide[pl.ds(tower.row_of(s, ends_ref), 1), :] += grad_middle_ref[s : s + 1, :]

    def second(at, carry):
        grad = grad_ref_wide[at, :]
        if not tower.image:
            grad_rows_ref[at, :] = grad.astype(jnp.bfloat16)
            return carry
        grad_in, gain_part = layer_norm_back(tokens_ref[at, :], gains[0], grad)
        grad_ref_wide[at, :] = grad_in
        grad_rows_ref[at, :] = grad_in.astype(jnp.bfloat16)
        return carry[0] + sum_rows(gain_part), carry[1] + sum_rows(grad)

    gain_pre, shift_pre = tower.each_block(second, (nothing, nothing))
    gain_grads_ref[0:1, :] = gain_pre
    gain_grads_ref[1:2, :] = shift_pre
    places = grad_ref_wide[0 : tower.length, :]
    for s in range(1, SEQS):
        places = places + grad_ref_wide[s * tower.length : (s + 1) * tower.length, :]
    places_ref[...] = places


def tower_backward(tower, ends, gains, grad_emb, kept, weights):
    width, rows = tower.width, tower.rows
    low, full = jnp.bfloat16, jnp.float32
    outs = [
        ((GROUP, EMBED), low),
        ((GROUP, width), low),
        ((GROUP, 4 * width), low),
        ((GROUP, width), low),
        ((GROUP, width), low),
        ((rows, 2 * width), low),
        ((rows, width), low),
        ((tower.length, width), full),
        ((8, width), full),
    ]
    vmem = pl.BlockSpec(memory_space=pltpu.VMEM)
    shapes, names = tower.shapes(), tower.names[-4:]
    return pl.pallas_call(
        functools.partial(tower_backward_kernel, tower),
        out_shape=[jax.ShapeDtypeStruct(shape, kind) for shape, kind in outs],
        in_specs=[pl.BlockSpec(memory_space=pltpu.SMEM)]
        + [vmem] * (2 + len(kept))
        + [pl.BlockSpec(memory_space=pl.ANY)] * len(names),
        out_specs=[vmem] * len(outs),
        scratch_shapes=[
            pltpu.VMEM((rows, width), full),
            pltpu.VMEM((tower.queries, width), full),
            pltpu.VMEM((SEQS, width), full),
        ]
        + [pltpu.VMEM(shapes[name], low) for name in names]
        + [pltpu.SemaphoreType.DMA((len(names),))],
        compiler_params=pltpu.CompilerParams(vmem_limit_bytes=58 << 20),
        name="image_backward" if tower.image else "text_backward",
    )(ends, gains, grad_emb, *kept, *[weights[name] for name in names])


def grad_pairs(kept, grads):
    (normed, normed_own, attended, normed_two, act_low, head_in) = (
        kept[1], kept[3], kept[6], kept[8], kept[10], kept[12]
    )
    grad_raw, grad_mlp, grad_upper, grad_att, grad_query, grad_pair = grads[:6]
    return (
        [(normed_own, grad_query), (normed, grad_pair), (attended, grad_att)],
        [(normed_two, grad_upper)],
        [(act_low, grad_mlp)],
        [(head_in, grad_raw)],
    )


def image_inputs(image_vec, pixels):
    pixels = jnp.pad(pixels, ((0, 0), (1, 0), (0, 0))).reshape(-1, PATCH_DIM)
    base = image_vec[1 : IMG_TOK + 1] + jnp.pad(image_vec[:1], ((0, IMG_TOK - 1), (0, 0)))
    return image_vec[IMG_TOK + 1 :], jnp.tile(base, (SEQS, 1)), pixels


def text_inputs(text_vec, token_rows):
    gains = jnp.pad(text_vec[CTX:], ((2, 0), (0, 0)))
    extra = TEXT.rows - SEQS * CTX
    base = jnp.pad(jnp.tile(text_vec[:CTX], (SEQS, 1)), ((0, extra), (0, 0)))
    return gains, base, jnp.pad(token_rows, ((0, extra), (0, 0)))


def adam_step(weight, first, second, grad, rate, decay):
    first = beta_one * first + (1.0 - beta_one) * grad
    second = beta_two * second + (1.0 - beta_two) * grad * grad
    first_hat = first / (1.0 - beta_one**STEP)
    second_hat = second / (1.0 - beta_two**STEP)
    weight = weight - rate * (first_hat / (jnp.sqrt(second_hat) + adam_eps) + decay * weight)
    return (weight, first, second)


IMAGE, TEXT = Tower(True), Tower(False)


def matrix_rows():
    return sum(seg_rows * seg_cols for seg_name, seg_rows, seg_cols in segment_list()[:9]) // LANES


def window_rows(shard, step=GROUP):
    need = -(-(GROUP * LANES - 1 + shard) // LANES)
    return -(-need // step) * step


def window_start(shard, index):
    return (shard * index // (GROUP * LANES)) * GROUP


def linear_index(gy_size):
    return lax.axis_index("gx") * gy_size + lax.axis_index("gy")


def place_kernel(shard, gy_size, flat_ref, out_ref, rolled):
    rows = flat_ref.shape[0]
    offset = lax.rem(shard * linear_index(gy_size), GROUP * LANES)
    down, right = offset // LANES, lax.rem(offset, LANES)
    pad = 2 * GROUP
    rolled[0:pad, :] = jnp.zeros((pad, LANES), jnp.float32)
    parts = 5 if rows % (5 * GROUP) == 0 else 1
    step = rows // parts

    def roll_rows(i, carry):
        at = pl.multiple_of(i * step, GROUP)
        rolled[pl.ds(pad + at, step), :] = pltpu.roll(flat_ref[pl.ds(at, step), :], right, 1)
        return carry

    lax.fori_loop(0, parts, roll_rows, 0)
    lane = lax.broadcasted_iota(jnp.int32, (step, LANES), 1)

    def put_rows(i, carry):
        at = pl.multiple_of(i * step, GROUP)
        upper = rolled[pl.ds(pad + at - down - 1, step), :]
        lower = rolled[pl.ds(pad + at - down, step), :]
        out_ref[pl.ds(at, step), :] = jnp.where(lane < right, upper, lower).astype(jnp.bfloat16)
        return carry

    lax.fori_loop(0, parts, put_rows, 0)


def place_window(flat, gy_size):
    shard = flat.shape[0]
    rows = window_rows(shard)
    padded = jnp.pad(flat, (0, rows * LANES - shard)).reshape(rows, LANES)
    return pl.pallas_call(
        functools.partial(place_kernel, shard, gy_size),
        out_shape=jax.ShapeDtypeStruct((rows, LANES), jnp.bfloat16),
        in_specs=[pl.BlockSpec(memory_space=pltpu.VMEM)],
        out_specs=pl.BlockSpec(memory_space=pltpu.VMEM),
        scratch_shapes=[pltpu.VMEM((rows + 2 * GROUP, LANES), jnp.float32)],
        compiler_params=pltpu.CompilerParams(vmem_limit_bytes=32 << 20),
        name="place_window",
    )(padded)


def lift_kernel(shard, gy_size, window_ref, out_ref, rolled):
    rows = window_ref.shape[0]
    offset = lax.rem(shard * linear_index(gy_size), GROUP * LANES)
    up, left = offset // LANES, lax.rem(offset, LANES)
    pad = 2 * GROUP
    step = rows // CHUNKS
    rolled[rows:, :] = jnp.zeros((pad, LANES), jnp.float32)

    def roll_rows(i, carry):
        at = pl.multiple_of(i * step, GROUP)
        rolled[pl.ds(at, step), :] = pltpu.roll(
            window_ref[pl.ds(at, step), :], lax.rem(LANES - left, LANES), 1
        )
        return carry

    lax.fori_loop(0, CHUNKS, roll_rows, 0)
    lane = lax.broadcasted_iota(jnp.int32, (step, LANES), 1)

    def put_rows(i, carry):
        at = pl.multiple_of(i * step, GROUP)
        first = rolled[pl.ds(at + up, step), :]
        second = rolled[pl.ds(at + up + 1, step), :]
        out_ref[pl.ds(at, step), :] = jnp.where(lane < LANES - left, first, second)
        return carry

    lax.fori_loop(0, CHUNKS, put_rows, 0)


def lift_window(window, shard, gy_size):
    rows = window.shape[0]
    lifted = pl.pallas_call(
        functools.partial(lift_kernel, shard, gy_size),
        out_shape=jax.ShapeDtypeStruct((rows, LANES), jnp.float32),
        in_specs=[pl.BlockSpec(memory_space=pltpu.VMEM)],
        out_specs=pl.BlockSpec(memory_space=pltpu.VMEM),
        scratch_shapes=[pltpu.VMEM((rows + 2 * GROUP, LANES), jnp.float32)],
        compiler_params=pltpu.CompilerParams(vmem_limit_bytes=32 << 20),
        name="lift_window",
    )(window)
    return lifted.reshape(-1)[:shard]


def spread_steps():
    steps = []
    base = 0
    for number, (seg_name, seg_rows, seg_cols) in enumerate(segment_list()[:9]):
        wide = seg_cols // LANES
        take = seg_rows
        while take * wide > 4608:
            take //= 2
        for start in range(0, seg_rows, take):
            steps.append((number, start, take, seg_cols, base + start * wide))
        base += seg_rows * wide
    return steps


def window_pieces(shard, count, stride, first, length):
    pieces, shared = [], []
    for index in range(count):
        low = window_start(shard, index)
        high = window_start(shard, index + 1) if index + 1 < count else low + window_rows(shard)
        start, stop = max(low, first), min(high, first + length)
        if start < stop:
            pieces.append((index * stride + start - low, start - first, stop - start))
        if index + 1 < count and first <= high < first + length:
            shared.append((index * stride + high - low, high - first))
    return pieces, shared


def spread_kernel(shard, count, vec_rows, gathered_ref, *refs):
    outs, vec_ref = refs[:9], refs[9]
    landed, edges, wide_rows, ready, in_sem, out_sem = refs[10:]
    rows = gathered_ref.shape[0] // count
    steps = spread_steps()
    steps.append((9, 0, vec_rows, LANES, matrix_rows()))

    def copies_in(number):
        seg, start, take, cols, base = steps[number]
        slot = number % 2
        pieces, shared = window_pieces(shard, count, rows, base, take * cols // LANES)
        found = [
            pltpu.make_async_copy(
                gathered_ref.at[pl.ds(src, size)], landed.at[slot, pl.ds(dst, size)], in_sem.at[slot]
            )
            for src, dst, size in pieces
        ]
        found += [
            pltpu.make_async_copy(
                gathered_ref.at[pl.ds(src, GROUP)], edges.at[slot, order], in_sem.at[slot]
            )
            for order, (src, dst) in enumerate(shared)
        ]
        return found, shared

    def copy_out(number):
        seg, start, take, cols, base = steps[number]
        slot = number % 2
        if seg == 9:
            return pltpu.make_async_copy(wide_rows.at[pl.ds(0, take)], vec_ref, out_sem.at[slot])
        return pltpu.make_async_copy(
            ready[cols].at[slot, pl.ds(0, take)], outs[seg].at[pl.ds(start, take)], out_sem.at[slot]
        )

    for copy in copies_in(0)[0]:
        copy.start()
    for number, (seg, start, take, cols, base) in enumerate(steps):
        slot = number % 2
        wide = cols // LANES
        total = take * wide
        if number + 1 < len(steps):
            for copy in copies_in(number + 1)[0]:
                copy.start()
        found, shared = copies_in(number)
        for copy in found:
            copy.wait()
        if number >= 2:
            copy_out(number - 2).wait()
        block = 256 if total % 256 == 0 else GROUP

        def widen(i, carry, slot=slot, block=block):
            at = pl.multiple_of(i * block, GROUP)
            wide_rows[pl.ds(at, block), :] = landed[slot, pl.ds(at, block), :].astype(jnp.float32)
            return carry

        lax.fori_loop(0, total // block, widen, 0)
        for order, (src, dst) in enumerate(shared):
            wide_rows[dst : dst + GROUP, :] += edges[slot, order].astype(jnp.float32)
        if seg < 9:

            def tile(i, carry, slot=slot, wide=wide, cols=cols):
                at = pl.multiple_of(i * GROUP, GROUP)
                for j in range(wide):
                    ready[cols][slot, pl.ds(at, GROUP), j * LANES : (j + 1) * LANES] = wide_rows[
                        pl.ds(at * wide + j, GROUP, stride=wide), :
                    ].astype(jnp.bfloat16)
                return carry

            lax.fori_loop(0, take // GROUP, tile, 0)
        copy_out(number).start()
    copy_out(len(steps) - 2).wait()
    copy_out(len(steps) - 1).wait()


def spread_entry(shard, count, vec_rows, gathered_ref, *refs):
    outs = refs[:10]
    landed, edges, wide_rows, ready_a, ready_b, ready_c, ready_d, in_sem, out_sem = refs[10:]
    ready = {D_IMG: ready_a, 4 * D_IMG: ready_b, D_TXT: ready_c, 4 * D_TXT: ready_d}
    spread_kernel(
        shard, count, vec_rows, gathered_ref, *outs, landed, edges, wide_rows, ready, in_sem, out_sem
    )


def spread_weights(gathered, shard, count):
    rows = gathered.shape[0] // count
    steps = spread_steps()
    tallest = {}
    for seg, start, take, cols, base in steps:
        tallest[cols] = max(tallest.get(cols, 0), take)
    most = max(take * cols // LANES for seg, start, take, cols, base in steps)
    vec_rows = -(-(sum(r * c for name, r, c in segment_list()[9:])) // (LANES * GROUP)) * GROUP
    edge_count = max(
        len(window_pieces(shard, count, rows, base, take * cols // LANES)[1])
        for seg, start, take, cols, base in steps
    )
    ready = [
        pltpu.VMEM((2, tallest[cols], cols), jnp.bfloat16)
        for cols in (D_IMG, 4 * D_IMG, D_TXT, 4 * D_TXT)
    ]
    return pl.pallas_call(
        functools.partial(spread_entry, shard, count, vec_rows),
        out_shape=[
            jax.ShapeDtypeStruct((seg_rows, seg_cols), jnp.bfloat16)
            for seg_name, seg_rows, seg_cols in segment_list()[:9]
        ]
        + [jax.ShapeDtypeStruct((vec_rows, LANES), jnp.float32)],
        in_specs=[pl.BlockSpec(memory_space=pl.ANY)],
        out_specs=[pl.BlockSpec(memory_space=pl.ANY)] * 10,
        scratch_shapes=[
            pltpu.VMEM((2, most, LANES), jnp.bfloat16),
            pltpu.VMEM((2, edge_count + 1, GROUP, LANES), jnp.bfloat16),
            pltpu.VMEM((most, LANES), jnp.float32),
        ]
        + ready
        + [pltpu.SemaphoreType.DMA((2,)), pltpu.SemaphoreType.DMA((2,))],
        compiler_params=pltpu.CompilerParams(vmem_limit_bytes=48 << 20),
        name="spread_weights",
    )(gathered)


def split_vectors(vec_rows):
    image_count, text_count = (IMG_TOK + 9) * D_IMG // LANES, (CTX + 6) * D_TXT // LANES
    image_vec = vec_rows[:image_count].reshape(IMG_TOK + 9, D_IMG)
    text_vec = vec_rows[image_count : image_count + text_count].reshape(CTX + 6, D_TXT)
    return image_vec, text_vec, vec_rows[image_count + text_count, 0]


def grads_kernel(parts, total_rows, *refs):
    operand_count = sum(2 * len(pairs) for seg_rows, seg_cols, take, pairs in parts)
    operands = refs[:operand_count]
    vec_ref, out_ref, flat_rows, vec_sem, out_sem = refs[operand_count:]
    tail = pltpu.make_async_copy(vec_ref, out_ref.at[pl.ds(matrix_rows(), vec_ref.shape[0])], vec_sem)
    tail.start()
    base = 0
    steps_before = 0
    for seg_rows, seg_cols, take, pairs in parts:
        wide = seg_cols // LANES
        size = take * wide
        count = seg_rows // take

        def step(i, carry, base=base, before=steps_before, size=size, take=take, wide=wide, pairs=pairs):
            slot = lax.rem(i + before, 2)

            def written(number):
                at = pl.multiple_of(base + number * size, 8)
                return pltpu.make_async_copy(
                    flat_rows.at[slot, pl.ds(0, size)], out_ref.at[pl.ds(at, size)], out_sem.at[slot]
                )

            @pl.when(i >= 2)
            def _():
                written(i - 2).wait()

            for left_number, right_number, first in pairs:
                left_ref, right_ref = operands[left_number], operands[right_number]
                at = pl.multiple_of(i * take, LANES)
                product = lax.dot_general(
                    left_ref[:, pl.ds(at, take)],
                    right_ref[...],
                    (((0,), (0,)), ((), ())),
                    preferred_element_type=jnp.float32,
                )
                for j in range(right_ref.shape[1] // LANES):
                    flat_rows[slot, pl.ds(first + j, take, stride=wide), :] = product[
                        :, j * LANES : (j + 1) * LANES
                    ]
            written(i).start()
            return carry

        lax.fori_loop(0, count, step, 0)
        for number in range(max(count - 2, 0), count):
            slot = (number + steps_before) % 2
            at = base + number * size
            pltpu.make_async_copy(
                flat_rows.at[slot, pl.ds(0, size)], out_ref.at[pl.ds(at, size)], out_sem.at[slot]
            ).wait()
        base += seg_rows * wide
        steps_before += count
    tail.wait()


def weight_grads(pair_lists, vec_rows):
    operands, parts = [], []
    for (seg_name, seg_rows, seg_cols), pairs in zip(segment_list()[:9], pair_lists):
        numbered, first = [], 0
        for left_side, right_side in pairs:
            numbered.append((len(operands), len(operands) + 1, first))
            for side in (left_side, right_side):
                side = side.reshape(-1, side.shape[-1])
                operands.append(jnp.pad(side, ((0, -side.shape[0] % GROUP), (0, 0))))
            first += right_side.shape[-1] // LANES
        parts.append((seg_rows, seg_cols, min(seg_rows, 256 if seg_cols <= 768 else 128), numbered))
    total_rows = matrix_rows() + vec_rows.shape[0]
    most = max(take * seg_cols // LANES for seg_rows, seg_cols, take, pairs in parts)
    return pl.pallas_call(
        functools.partial(grads_kernel, parts, total_rows),
        out_shape=jax.ShapeDtypeStruct((total_rows, LANES), jnp.float32),
        in_specs=[pl.BlockSpec(memory_space=pltpu.VMEM)] * (len(operands) + 1),
        out_specs=pl.BlockSpec(memory_space=pl.ANY),
        scratch_shapes=[
            pltpu.VMEM((2, most, LANES), jnp.float32),
            pltpu.SemaphoreType.DMA,
            pltpu.SemaphoreType.DMA((2,)),
        ],
        compiler_params=pltpu.CompilerParams(vmem_limit_bytes=56 << 20),
        name="weight_grads",
    )(*operands, vec_rows)


def exchange_kernel(gx_size, gy_size, many, *refs):
    blocks, outs = refs[:many], refs[many : 2 * many]
    send_sem, recv_sem, own_sem = refs[2 * many :]
    count = gx_size * gy_size
    me = linear_index(gy_size)
    barrier = pltpu.get_barrier_semaphore()

    def device(step):
        other = lax.rem(me + step, count)
        return (other // gy_size, lax.rem(other, gy_size))

    def greet(step, carry):
        pl.semaphore_signal(barrier, inc=1, device_id=device(step), device_id_type=MESH)
        return carry

    lax.fori_loop(1, count, greet, 0)
    own = [
        pltpu.make_async_copy(block, out.at[me], own_sem.at[i])
        for i, (block, out) in enumerate(zip(blocks, outs))
    ]
    for copy in own:
        copy.start()
    pl.semaphore_wait(barrier, count - 1)

    def send(step, carry):
        for i, (block, out) in enumerate(zip(blocks, outs)):
            pltpu.make_async_remote_copy(
                src_ref=block,
                dst_ref=out.at[me],
                send_sem=send_sem.at[i],
                recv_sem=recv_sem.at[i],
                device_id=device(step),
                device_id_type=MESH,
            ).start()
        return carry

    lax.fori_loop(1, count, send, 0)
    for i, out in enumerate(outs):
        own[i].wait()
        others = out.at[pl.ds(0, count - 1)]
        both = pltpu.make_async_remote_copy(
            src_ref=others,
            dst_ref=others,
            send_sem=send_sem.at[i],
            recv_sem=recv_sem.at[i],
            device_id=device(1),
            device_id_type=MESH,
        )
        both.wait_send()
        both.wait_recv()


def exchange_all(blocks, gx_size, gy_size, number, name):
    count, many = gx_size * gy_size, len(blocks)
    return pl.pallas_call(
        functools.partial(exchange_kernel, gx_size, gy_size, many),
        out_shape=[jax.ShapeDtypeStruct((count,) + block.shape, block.dtype) for block in blocks],
        in_specs=[pl.BlockSpec(memory_space=pltpu.VMEM)] * many,
        out_specs=[pl.BlockSpec(memory_space=pltpu.VMEM)] * many,
        scratch_shapes=[pltpu.SemaphoreType.DMA((many,))] * 3,
        compiler_params=pltpu.CompilerParams(
            collective_id=number, has_side_effects=True, vmem_limit_bytes=32 << 20
        ),
        name=name,
    )(*blocks)


class Places:
    def __init__(self, sizes):
        self.x_size, self.low_size, self.high_size = sizes
        self.mixed = self.x_size == self.low_size
        self.gy_size = self.high_size * self.low_size
        gx, gy = lax.axis_index("gx"), lax.axis_index("gy")
        self.core, x = lax.rem(gx, 2), gx // 2
        self.h, low = gy // self.low_size, lax.rem(gy, self.low_size)
        self.a, self.b = self.turned(self.core, x, low)
        self.a_size, self.b_size = self.x_size, self.low_size

    def turned(self, side, a, b):
        if not self.mixed:
            return a, b
        return a * (1 - side) + b * side, b * (1 - side) + a * side

    def device(self, side, a, b, h):
        dev_x, dev_low = self.turned(side, a, b)
        return (dev_x * 2 + side, h * self.low_size + dev_low)

    def linear(self, side, a, b, h):
        gx, gy = self.device(side, a, b, h)
        return gx * self.gy_size + gy

    def sibling(self):
        a, b = (self.b, self.a) if self.mixed else (self.a, self.b)
        return self.device(1 - self.core, a, b, self.h)

    def along_a(self):
        return [
            self.device(self.core, lax.rem(self.a + d, self.a_size), self.b, self.h)
            for d in range(1, self.a_size)
        ]

    def along_b(self):
        return [
            self.device(self.core, self.a, lax.rem(self.b + d, self.b_size), self.h)
            for d in range(1, self.b_size)
        ]

    def along_h(self):
        return [
            self.device(self.core, self.a, self.b, lax.rem(self.h + d, self.high_size))
            for d in range(1, self.high_size)
        ]


def greet_all(others):
    barrier = pltpu.get_barrier_semaphore()
    for other in others:
        pl.semaphore_signal(barrier, inc=1, device_id=other, device_id_type=MESH)
    pl.semaphore_wait(barrier, len(others))


def remote(src, dst, send_sem, recv_sem, other):
    return pltpu.make_async_remote_copy(
        src_ref=src, dst_ref=dst, send_sem=send_sem, recv_sem=recv_sem, device_id=other, device_id_type=MESH
    )


def axis_sizes(gx_size, gy_size):
    return gx_size // 2, gy_size // 4, 4


def route_capacity(tokens, gy_size):
    return max(5 * tokens // (2 * gy_size * GROUP), 1) * GROUP


def share_kernel(gx_size, gy_size, everyone, send_ref, out_ref, own_sem, row_send, row_recv, x_send, x_recv, core_send,
                 core_recv):
    gx, gy = lax.axis_index("gx"), lax.axis_index("gy")
    x_size = gx_size // 2
    core, x = lax.rem(gx, 2), gx // 2
    rows = [(gx, lax.rem(gy + d, gy_size)) for d in range(1, gy_size)]
    along_x = [(lax.rem(x + d, x_size) * 2 + core, gy) for d in range(1, x_size)] if everyone else []
    sibling = [(x * 2 + 1 - core, gy)] if everyone else []
    greet_all(rows + along_x + sibling)
    mine = out_ref.at[gx] if everyone else out_ref.at[0]
    own = pltpu.make_async_copy(send_ref.at[gy], mine.at[gy], own_sem)
    own.start()
    for d, other in enumerate(rows):
        remote(send_ref.at[other[1]], mine.at[gy], row_send.at[d], row_recv.at[d], other).start()
    own.wait()
    for d, other in enumerate(rows):
        copy = remote(send_ref.at[other[1]], mine.at[gy], row_send.at[d], row_recv.at[d], other)
        copy.wait_recv()
    for d, other in enumerate(along_x):
        remote(mine, mine, x_send.at[d], x_recv.at[d], other).start()
    for other in sibling:
        remote(mine, mine, core_send.at[0], core_recv.at[0], other).start()
    for d, other in enumerate(along_x):
        remote(mine, mine, x_send.at[d], x_recv.at[d], other).wait_recv()
        source = out_ref.at[lax.rem(x + x_size - d - 1, x_size) * 2 + core]
        remote(source, source, core_send.at[d + 1], core_recv.at[d + 1], sibling[0]).start()
    for d, other in enumerate(rows):
        remote(send_ref.at[other[1]], mine.at[gy], row_send.at[d], row_recv.at[d], other).wait_send()
    for d, other in enumerate(along_x):
        remote(mine, mine, x_send.at[d], x_recv.at[d], other).wait_send()
    for i in range(x_size if everyone else 0):
        copy = remote(mine, mine, core_send.at[i], core_recv.at[i], sibling[0])
        copy.wait_send()
        copy.wait_recv()


def share_rows(rows, gx_size, gy_size, everyone, number, name):
    groups, dma = (gx_size if everyone else 1), pltpu.SemaphoreType.DMA
    x_size = gx_size // 2
    return pl.pallas_call(
        functools.partial(share_kernel, gx_size, gy_size, everyone),
        out_shape=jax.ShapeDtypeStruct((groups,) + rows.shape, rows.dtype),
        in_specs=[pl.BlockSpec(memory_space=pltpu.VMEM)],
        out_specs=pl.BlockSpec(memory_space=pltpu.VMEM),
        scratch_shapes=[dma, dma((gy_size - 1,)), dma((gy_size - 1,)), dma((x_size,)), dma((x_size,)), dma((x_size,)),
                        dma((x_size,))],
        compiler_params=pltpu.CompilerParams(
            collective_id=number, has_side_effects=True, vmem_limit_bytes=48 << 20
        ),
        name=name,
    )(rows)


def table_sum_kernel(cap, counts_ref, index_ref, rows_ref, out_ref, square_ref, wide, row_sem):
    sources = rows_ref.shape[0]
    vocab = out_ref.shape[0]

    def fetch(source):
        slot = lax.rem(source, 2)
        return pltpu.make_async_copy(rows_ref.at[source], wide.at[slot], row_sem.at[slot])

    fetch(0).start()
    block = 32 if vocab % 32 == 0 else 8

    def clear(i, carry):
        out_ref[pl.ds(pl.multiple_of(i * block, 8), block), :] = jnp.zeros((block, D_TXT), jnp.float32)
        return carry

    lax.fori_loop(0, vocab // block, clear, 0)

    def one_source(source, carry):
        slot = lax.rem(source, 2)

        @pl.when(source + 1 < sources)
        def _():
            fetch(source + 1).start()

        fetch(source).wait()
        count = counts_ref[source]
        widened = wide.at[slot]

        def add(group, carry):
            rows = widened[pl.ds(pl.multiple_of(group * GROUP, GROUP), GROUP), :].astype(jnp.float32)
            for i in range(GROUP):
                @pl.when(group * GROUP + i < count)
                def _(i=i):
                    place = pl.ds(index_ref[source * cap + group * GROUP + i], 1)
                    out_ref[place, :] = out_ref[place, :] + rows[i : i + 1, :]

            return carry

        lax.fori_loop(0, (count + GROUP - 1) // GROUP, add, 0)
        return carry

    lax.fori_loop(0, sources, one_source, 0)

    def square(i, carry):
        part = out_ref[pl.ds(pl.multiple_of(i * block, 8), block), :]
        part = part * part
        total = carry
        for r in range(0, block, 8):
            total = total + part[r : r + 8]
        return total

    square_ref[...] = lax.fori_loop(0, vocab // block, square, jnp.zeros((8, D_TXT), jnp.float32))


def table_sum(counts, index, rows, vocab):
    sources, cap = rows.shape[0], rows.shape[1]
    return pl.pallas_call(
        functools.partial(table_sum_kernel, cap),
        out_shape=[
            jax.ShapeDtypeStruct((vocab, D_TXT), jnp.float32),
            jax.ShapeDtypeStruct((8, D_TXT), jnp.float32),
        ],
        in_specs=[pl.BlockSpec(memory_space=pltpu.SMEM)] * 2 + [pl.BlockSpec(memory_space=pl.ANY)],
        out_specs=[pl.BlockSpec(memory_space=pltpu.VMEM)] * 2,
        scratch_shapes=[pltpu.VMEM((2, cap, D_TXT), jnp.bfloat16), pltpu.SemaphoreType.DMA((2,))],
        compiler_params=pltpu.CompilerParams(vmem_limit_bytes=40 << 20),
        name="table_sum",
    )(counts, index, rows)


def ranks(flags):
    tokens = flags.shape[-1]
    before = (jnp.arange(tokens)[:, None] < jnp.arange(tokens)[None, :]).astype(jnp.bfloat16)
    return fwd_dot(flags.astype(jnp.bfloat16), before).astype(jnp.int32)


def pick_matrix(slots, count):
    return (jnp.arange(count)[:, None] == slots[None, :]).astype(jnp.bfloat16)


def gather_kernel(sizes, window_ref, out_ref, own_sem, h_send, h_recv, b_send, b_recv, a_send, a_recv, core_send,
                  core_recv):
    at = Places(sizes)
    rows = window_ref.shape[0]
    chunk = rows // GATHER_CHUNKS
    me = at.linear(at.core, at.a, at.b, at.h)
    sibling, peers_a, peers_b, peers_h = at.sibling(), at.along_a(), at.along_b(), at.along_h()
    greet_all([sibling] + peers_a + peers_b + peers_h)

    def part(block, t):
        return out_ref.at[pl.ds(pl.multiple_of(block * rows + t * chunk, GROUP), chunk)]

    def many(count):
        return out_ref.at[pl.ds(0, count * chunk)]

    def own_copy(t):
        src = window_ref.at[pl.ds(pl.multiple_of(t * chunk, GROUP), chunk)]
        return src, pltpu.make_async_copy(src, part(me, t), own_sem.at[t])

    def stage_h(t):
        src, own = own_copy(t)
        for d, other in enumerate(peers_h):
            remote(src, part(me, t), h_send.at[d], h_recv.at[t, d], other).start()
        own.start()

    def stage_b(t):
        own_copy(t)[1].wait()
        for d, other in enumerate(peers_h):
            remote(many(1), many(1), h_send.at[d], h_recv.at[t, d], other).wait_recv()
        for d, other in enumerate(peers_b):
            for h in range(at.high_size):
                block = part(at.linear(at.core, at.a, at.b, h), t)
                remote(block, block, b_send.at[d], b_recv.at[t, d], other).start()

    def stage_a(t):
        for d, other in enumerate(peers_b):
            remote(many(at.high_size), many(at.high_size), b_send.at[d], b_recv.at[t, d], other).wait_recv()
        for d, other in enumerate(peers_a):
            for b in range(at.b_size):
                for h in range(at.high_size):
                    block = part(at.linear(at.core, at.a, b, h), t)
                    remote(block, block, a_send.at[d], a_recv.at[t, d], other).start()

    plane = at.b_size * at.high_size

    def stage_core(t):
        for d, other in enumerate(peers_a):
            remote(many(plane), many(plane), a_send.at[d], a_recv.at[t, d], other).wait_recv()
        for a in range(at.a_size):
            for b in range(at.b_size):
                for h in range(at.high_size):
                    block = part(at.linear(at.core, a, b, h), t)
                    remote(block, block, core_send, core_recv, sibling).start()

    def turn(t, carry):
        for depth, stage in enumerate((stage_h, stage_b, stage_a, stage_core)):
            @pl.when((t >= depth) & (t < GATHER_CHUNKS + depth))
            def _():
                stage(t - depth)

        return carry

    lax.fori_loop(0, GATHER_CHUNKS + 3, turn, 0)

    def whole(count):
        return out_ref.at[pl.ds(0, count * rows)]

    for d, other in enumerate(peers_h):
        remote(whole(1), whole(1), h_send.at[d], h_recv.at[0, d], other).wait_send()
    for d, other in enumerate(peers_b):
        remote(whole(at.high_size), whole(at.high_size), b_send.at[d], b_recv.at[0, d], other).wait_send()
    for d, other in enumerate(peers_a):
        remote(whole(plane), whole(plane), a_send.at[d], a_recv.at[0, d], other).wait_send()
    half = whole(at.a_size * plane)
    last = remote(half, half, core_send, core_recv, sibling)
    last.wait_send()
    last.wait_recv()


def gather_windows(window, gx_size, gy_size, number):
    sizes = axis_sizes(gx_size, gy_size)
    a, b, h = sizes[0] - 1, sizes[1] - 1, sizes[2] - 1
    dma = pltpu.SemaphoreType.DMA
    return pl.pallas_call(
        functools.partial(gather_kernel, sizes),
        out_shape=jax.ShapeDtypeStruct((gx_size * gy_size * window.shape[0], LANES), window.dtype),
        in_specs=[pl.BlockSpec(memory_space=pltpu.VMEM)],
        out_specs=pl.BlockSpec(memory_space=pl.ANY),
        scratch_shapes=[dma((GATHER_CHUNKS,)), dma((h,)), dma((GATHER_CHUNKS, h)), dma((b,)), dma((GATHER_CHUNKS, b)), dma((a,)),
                        dma((GATHER_CHUNKS, a)), dma, dma],
        compiler_params=pltpu.CompilerParams(
            collective_id=number, has_side_effects=True, vmem_limit_bytes=32 << 20
        ),
        name="gather_windows",
    )(window)


def reduce_kernel(shard, sizes, grads_ref, out_ref, own, landed, keep_one, send_one, recv_one, keep_two, send_two,
                  recv_two, keep_three, send_three, recv_three, load_sem, pair_send, pair_recv, credit,
                  one_send, one_recv, two_send, two_recv, three_send, three_recv):
    at = Places(sizes)
    a_size, b_size, high_size = at.a_size, at.b_size, at.high_size
    core, my_a, my_b, high = at.core, at.a, at.b, at.h
    plane = b_size * high_size
    chunk = own.shape[2]
    chunks = out_ref.shape[0] // chunk

    def start_row(side, number):
        a, rest = number // plane, lax.rem(number, plane)
        return window_start(shard, at.linear(side, a, rest // high_size, lax.rem(rest, high_size)))

    sibling, peers, peers_two, peers_three = at.sibling(), at.along_a(), at.along_b(), at.along_h()
    greet_all([sibling] + peers + peers_two + peers_three)
    blocks = a_size * plane

    def pair_stage(t):
        slot = lax.rem(t, 2)

        @pl.when(t >= 2)
        def _():
            pl.semaphore_wait(credit, 1)

        def each(number, carry):
            theirs = pl.multiple_of(start_row(1 - core, number) + t * chunk, GROUP)
            mine = pl.multiple_of(start_row(core, number) + t * chunk, GROUP)
            remote(
                grads_ref.at[pl.ds(theirs, chunk)], landed.at[slot, number], pair_send.at[slot], pair_recv.at[slot], sibling
            ).start()
            pltpu.make_async_copy(
                grads_ref.at[pl.ds(mine, chunk)], own.at[slot, number], load_sem.at[slot]
            ).start()
            return carry

        lax.fori_loop(0, blocks, each, 0)

    def first_stage(u):
        slot = lax.rem(u, 2)
        both = remote(landed.at[slot], landed.at[slot], pair_send.at[slot], pair_recv.at[slot], sibling)
        pltpu.make_async_copy(own.at[slot], own.at[slot], load_sem.at[slot]).wait()
        both.wait_send()
        both.wait_recv()
        for d in range(1, a_size):
            @pl.when(u >= 2)
            def _():
                remote(send_one.at[slot, d - 1], recv_one.at[u - 2, d - 1], one_send.at[slot, d - 1],
                       one_recv.at[u - 2, d - 1], peers[d - 1]).wait_send()

            first = lax.rem(my_a + d, a_size) * plane

            def give(i, carry):
                send_one[slot, d - 1, i] = (own[slot, first + i] + landed[slot, first + i]).astype(jnp.bfloat16)
                return carry

            lax.fori_loop(0, plane, give, 0)
            remote(send_one.at[slot, d - 1], recv_one.at[u, d - 1], one_send.at[slot, d - 1],
                   one_recv.at[u, d - 1], peers[d - 1]).start()

        def hold(i, carry):
            keep_one[slot, i] = own[slot, my_a * plane + i] + landed[slot, my_a * plane + i]
            return carry

        lax.fori_loop(0, plane, hold, 0)

        @pl.when(u < chunks - 2)
        def _():
            pl.semaphore_signal(credit, inc=1, device_id=sibling, device_id_type=MESH)

    def second_stage(u):
        slot = lax.rem(u, 2)
        for d in range(1, a_size):
            remote(recv_one.at[u, d - 1], recv_one.at[u, d - 1], one_send.at[slot, d - 1], one_recv.at[u, d - 1],
                   peers[d - 1]).wait_recv()

        def total(number):
            value = keep_one[slot, number]
            for d in range(1, a_size):
                value = value + recv_one[u, d - 1, number].astype(jnp.float32)
            return value

        for d in range(1, b_size):
            @pl.when(u >= 2)
            def _():
                remote(send_two.at[slot, d - 1], recv_two.at[u - 2, d - 1], two_send.at[slot, d - 1],
                       two_recv.at[u - 2, d - 1], peers_two[d - 1]).wait_send()

            first = lax.rem(my_b + d, b_size) * high_size

            def give(i, carry):
                send_two[slot, d - 1, i] = total(first + i).astype(jnp.bfloat16)
                return carry

            lax.fori_loop(0, high_size, give, 0)
            remote(send_two.at[slot, d - 1], recv_two.at[u, d - 1], two_send.at[slot, d - 1],
                   two_recv.at[u, d - 1], peers_two[d - 1]).start()

        def hold(i, carry):
            keep_two[slot, i] = total(my_b * high_size + i)
            return carry

        lax.fori_loop(0, high_size, hold, 0)

    def third_stage(u):
        slot = lax.rem(u, 2)
        for d in range(1, b_size):
            remote(recv_two.at[u, d - 1], recv_two.at[u, d - 1], two_send.at[slot, d - 1], two_recv.at[u, d - 1],
                   peers_two[d - 1]).wait_recv()

        def total(number):
            value = keep_two[slot, number]
            for d in range(1, b_size):
                value = value + recv_two[u, d - 1, number].astype(jnp.float32)
            return value

        for d in range(1, high_size):
            @pl.when(u >= 2)
            def _():
                remote(send_three.at[slot, d - 1], recv_three.at[u - 2, d - 1], three_send.at[slot, d - 1],
                       three_recv.at[u - 2, d - 1], peers_three[d - 1]).wait_send()

            send_three[slot, d - 1] = total(lax.rem(high + d, high_size)).astype(jnp.bfloat16)
            remote(send_three.at[slot, d - 1], recv_three.at[u, d - 1], three_send.at[slot, d - 1],
                   three_recv.at[u, d - 1], peers_three[d - 1]).start()
        keep_three[slot] = total(high)

    def last_stage(u):
        slot = lax.rem(u, 2)
        value = keep_three[slot]
        for d in range(1, high_size):
            remote(recv_three.at[u, d - 1], recv_three.at[u, d - 1], three_send.at[slot, d - 1],
                   three_recv.at[u, d - 1], peers_three[d - 1]).wait_recv()
            value = value + recv_three[u, d - 1].astype(jnp.float32)
        out_ref[pl.ds(pl.multiple_of(u * chunk, GROUP), chunk), :] = value

    def turn(t, carry):
        stages = (pair_stage, first_stage, second_stage, third_stage, last_stage)
        for depth, stage in enumerate(stages):
            @pl.when((t >= depth) & (t < chunks + depth))
            def _():
                stage(t - depth)

        return carry

    lax.fori_loop(0, chunks + 4, turn, 0)
    for u in range(max(chunks - 2, 0), chunks):
        slot = u % 2
        for d in range(1, a_size):
            remote(send_one.at[slot, d - 1], recv_one.at[u, d - 1], one_send.at[slot, d - 1],
                   one_recv.at[u, d - 1], peers[d - 1]).wait_send()
        for d in range(1, b_size):
            remote(send_two.at[slot, d - 1], recv_two.at[u, d - 1], two_send.at[slot, d - 1],
                   two_recv.at[u, d - 1], peers_two[d - 1]).wait_send()
        for d in range(1, high_size):
            remote(send_three.at[slot, d - 1], recv_three.at[u, d - 1], three_send.at[slot, d - 1],
                   three_recv.at[u, d - 1], peers_three[d - 1]).wait_send()


def reduce_windows(grads, shard, gx_size, gy_size, number):
    rows = window_rows(shard, GROUP * CHUNKS)
    chunk = rows // CHUNKS
    x_size, low_size, high_size = axis_sizes(gx_size, gy_size)
    plane = low_size * high_size
    blocks = x_size * plane
    low_type, dma = jnp.bfloat16, pltpu.SemaphoreType.DMA
    a, b, h = x_size - 1, low_size - 1, high_size - 1
    return pl.pallas_call(
        functools.partial(reduce_kernel, shard, (x_size, low_size, high_size)),
        out_shape=jax.ShapeDtypeStruct((rows, LANES), jnp.float32),
        in_specs=[pl.BlockSpec(memory_space=pl.ANY)],
        out_specs=pl.BlockSpec(memory_space=pltpu.VMEM),
        scratch_shapes=[
            pltpu.VMEM((2, blocks, chunk, LANES), jnp.float32),
            pltpu.VMEM((2, blocks, chunk, LANES), jnp.float32),
            pltpu.VMEM((2, plane, chunk, LANES), jnp.float32),
            pltpu.VMEM((2, a, plane, chunk, LANES), low_type),
            pltpu.VMEM((CHUNKS, a, plane, chunk, LANES), low_type),
            pltpu.VMEM((2, high_size, chunk, LANES), jnp.float32),
            pltpu.VMEM((2, b, high_size, chunk, LANES), low_type),
            pltpu.VMEM((CHUNKS, b, high_size, chunk, LANES), low_type),
            pltpu.VMEM((2, chunk, LANES), jnp.float32),
            pltpu.VMEM((2, h, chunk, LANES), low_type),
            pltpu.VMEM((CHUNKS, h, chunk, LANES), low_type),
            dma((2,)),
            dma((2,)),
            dma((2,)),
            pltpu.SemaphoreType.REGULAR,
            dma((2, a)),
            dma((CHUNKS, a)),
            dma((2, b)),
            dma((CHUNKS, b)),
            dma((2, h)),
            dma((CHUNKS, h)),
        ],
        compiler_params=pltpu.CompilerParams(
            collective_id=number, has_side_effects=True, vmem_limit_bytes=60 << 20
        ),
        name="reduce_windows",
    )(grads)


def log_sums(rows, columns, column_ok, logit_scale, matches):
    total, taken = rows.shape[0], min(rows.shape[0], 256)

    def some(args):
        row_part, match_part = args
        logits = logit_scale * back_dot(row_part, columns)
        masked = jnp.where(column_ok[None, :], logits, -1e30)
        row_max = jnp.max(masked, 1, keepdims=True)
        log_total = row_max[:, 0] + jnp.log(jnp.sum(jnp.exp(masked - row_max), 1))
        gap = jnp.where(match_part > 0.0, logits[:, :total] - log_total[:, None], 0.0)
        return log_total, -jnp.sum(gap)

    if taken == total:
        return some((rows, matches))
    logs, parts = lax.map(
        some, (rows.reshape(-1, taken, rows.shape[1]), matches.reshape(-1, taken, total))
    )
    return logs.reshape(-1), jnp.sum(parts)


def side_grads(row_embed, columns, column_ok, same_own, positives_own, log_own, logit_scale, total_count):
    dot_vals = back_dot(row_embed, columns)
    masked = jnp.where(column_ok[None, :], logit_scale * dot_vals, -1e30)
    extra = columns.shape[0] - same_own.shape[1]
    weights_pos = jnp.concatenate(
        [same_own, jnp.zeros((same_own.shape[0], extra), jnp.float32)], 1
    )
    grad_logits = (
        positives_own[:, None] * jnp.exp(masked - log_own[:, None]) - weights_pos
    ) / total_count
    grad_dots = (logit_scale * grad_logits).astype(jnp.bfloat16)
    grad_temper = logit_scale * jnp.sum(grad_logits * dot_vals)
    return fwd_dot(grad_dots, columns), grad_temper


def cross_grads(rows, own, valid_own, same_own, positives_all, logs, logit_scale, total_count):
    logits = logit_scale * back_dot(rows, own)
    masked = jnp.where(valid_own[None, :], logits, -1e30)
    grad_logits = (
        positives_all[:, None] * jnp.exp(masked - logs[:, None]) - same_own.T
    ) / total_count
    grad_dots = (logit_scale * grad_logits).astype(jnp.bfloat16)
    return weight_grad(grad_dots, rows)


def body(
    flat_master,
    flat_first,
    flat_second,
    table,
    table_first,
    table_second,
    pixels,
    token_ids,
    end_pos,
    pair_counts,
    groups,
    cached_image,
    cached_text,
):
    gx_size, gy_size = lax.axis_size("gx"), lax.axis_size("gy")
    device_count = gx_size * gy_size
    my_index = linear_index(gy_size)
    pairs_dev = pixels.shape[0]
    shard = flat_master.shape[0]
    tokens = token_ids.size
    vocab_dev = table.shape[0]
    cap = route_capacity(tokens, gy_size)
    flat_ids = jnp.pad(token_ids.reshape(-1), (0, ID_ROWS * LANES // 2 - tokens)).reshape(-1, LANES)
    payload = [
        place_window(flat_master, gy_size),
        jnp.concatenate([cached_image, cached_text], 0).reshape(CACHED_ROWS, LANES),
        jnp.concatenate([flat_ids // 256, flat_ids % 256], 0).astype(jnp.bfloat16),
    ]
    used = sum(part.shape[0] for part in payload)
    step = GROUP * GATHER_CHUNKS
    payload = jnp.pad(jnp.concatenate(payload, 0), ((0, -used % step), (0, 0)))
    gathered = gather_windows(payload, gx_size, gy_size, 4)
    every_part = gathered.reshape(device_count, -1, LANES)
    cached = every_part[:, used - ID_ROWS - CACHED_ROWS : used - ID_ROWS].reshape(device_count, -1, EMBED)
    cache_img, cache_txt = lax.optimization_barrier((cached[:, :pairs_dev], cached[:, pairs_dev:]))
    cache_img, cache_txt = cache_img.reshape(-1, EMBED), cache_txt.reshape(-1, EMBED)
    coded = every_part[:, used - ID_ROWS : used].astype(jnp.int32)
    ids_all = coded[:, : ID_ROWS // 2] * 256 + coded[:, ID_ROWS // 2 :]
    ids_all = ids_all.reshape(device_count, -1)[:, :tokens]
    holders = ids_all // vocab_dev
    pair_rows = jnp.sum(holders[:, :, None] == jnp.arange(gy_size), 1)
    rounds = (jnp.max(pair_rows) + cap - 1) // cap
    me_y = lax.axis_index("gy")
    held = holders == me_y
    held_rank = jnp.where(held, ranks(held), -1)
    held_row = ids_all - me_y * vocab_dev
    held_count = jnp.sum(held, 1)
    own_holder = lax.dynamic_slice_in_dim(holders, my_index, 1, 0)[0]
    own_flags = jnp.arange(gy_size)[:, None] == own_holder[None, :]
    own_rank = jnp.sum(jnp.where(own_flags, ranks(own_flags), 0), 0)

    def held_rows(turn):
        slots = held_rank - turn * cap
        found = slots[:, None, :] == jnp.arange(cap)[None, :, None]
        return jnp.sum(jnp.where(found, held_row[:, None, :], 0), 2)

    def own_slots(turn):
        rank = own_rank - turn * cap
        return jnp.where((rank >= 0) & (rank < cap), own_holder * cap + rank, -1)

    first_rows = held_rows(0)
    group_start = lax.axis_index("gx") * gy_size

    def rows_to_send(index):
        index = lax.dynamic_slice_in_dim(index, group_start, gy_size, 0)
        return lax.optimization_barrier(jnp.take(table, index.reshape(-1), axis=0)).astype(jnp.bfloat16)

    landed = share_rows(
        rows_to_send(first_rows).reshape(gy_size, cap, D_TXT), gx_size, gy_size, False, 5, "token_rows"
    )
    slot_count = gy_size * cap
    picks = pick_matrix(own_slots(0), slot_count)
    token_rows = weight_grad(picks, landed.reshape(slot_count, D_TXT)).astype(jnp.bfloat16)

    def more_rows(turn, found):
        rows = rows_to_send(held_rows(turn)).reshape(gy_size, cap, D_TXT)
        rows = lax.all_to_all(rows, "gy", 0, 0, tiled=True).reshape(slot_count, D_TXT)
        return found + weight_grad(pick_matrix(own_slots(turn), slot_count), rows).astype(jnp.bfloat16)

    token_rows = lax.fori_loop(1, rounds, more_rows, token_rows)
    spread = spread_weights(gathered, shard, device_count)
    image_weights = dict(zip(IMAGE.names, spread[:5]))
    text_weights = dict(zip(TEXT.names, spread[5:9]))
    image_vec, text_vec, temper = split_vectors(spread[9])
    image_gains, image_base, image_rows = image_inputs(image_vec, pixels)
    text_gains, text_base, text_rows = text_inputs(text_vec, token_rows)
    image_kept = tower_forward(IMAGE, end_pos, image_gains, image_base, image_rows, image_weights)
    text_kept = tower_forward(TEXT, end_pos, text_gains, text_base, text_rows, text_weights)
    image_emb = image_kept[14].astype(jnp.bfloat16)
    text_emb = text_kept[14].astype(jnp.bfloat16)
    (embeds,) = exchange_all(
        [jnp.concatenate([image_emb, text_emb], 0)], gx_size, gy_size, 0, "embeddings"
    )
    all_img, all_txt = lax.optimization_barrier((embeds[:, :pairs_dev], embeds[:, pairs_dev:]))
    all_img, all_txt = all_img.reshape(-1, EMBED), all_txt.reshape(-1, EMBED)
    total_pairs = all_img.shape[0]
    valid_all = jnp.arange(total_pairs) % pairs_dev < jnp.repeat(pair_counts.reshape(-1), pairs_dev)
    matches = (
        (groups[:, None] == groups[None, :]) & valid_all[:, None] & valid_all[None, :]
    ).astype(jnp.float32)
    positives_all = jnp.sum(matches, 1)
    total_count = 2.0 * jnp.sum(positives_all)
    own_start = my_index * pairs_dev
    own_part = functools.partial(
        lax.dynamic_slice_in_dim, start_index=own_start, slice_size=pairs_dev, axis=0
    )
    same_own, positives_own, valid_own = own_part(matches), own_part(positives_all), own_part(valid_all)
    logit_scale = jnp.exp(temper)
    column_ok = jnp.concatenate([valid_all, jnp.ones((cache_img.shape[0],), jnp.bool_)])
    columns_txt = jnp.concatenate([all_txt, cache_txt])
    columns_img = jnp.concatenate([all_img, cache_img])
    log_img, loss_one = log_sums(all_img, columns_txt, column_ok, logit_scale, matches)
    log_txt, loss_two = log_sums(all_txt, columns_img, column_ok, logit_scale, matches)
    loss_sum = loss_one + loss_two
    grad_img, temper_one = side_grads(
        image_emb, columns_txt, column_ok, same_own, positives_own, own_part(log_img), logit_scale, total_count
    )
    grad_txt, temper_two = side_grads(
        text_emb, columns_img, column_ok, same_own, positives_own, own_part(log_txt), logit_scale, total_count
    )
    grad_img = grad_img + cross_grads(
        all_txt, image_emb, valid_own, same_own, positives_all, log_txt, logit_scale, total_count
    )
    grad_txt = grad_txt + cross_grads(
        all_img, text_emb, valid_own, same_own, positives_all, log_img, logit_scale, total_count
    )
    text_grads = tower_backward(TEXT, end_pos, text_gains, grad_txt, text_kept[:14], text_weights)
    grad_rows = text_grads[6][: SEQS * CTX]
    to_holders = fwd_dot(picks, grad_rows).astype(jnp.bfloat16).reshape(gy_size, cap, D_TXT)
    arrived = share_rows(to_holders, gx_size, gy_size, True, 6, "token_grads")
    image_grads = tower_backward(IMAGE, end_pos, image_gains, grad_img, image_kept[:14], image_weights)
    pair_lists = ([(image_rows, image_grads[6])],) + grad_pairs(image_kept, image_grads)
    pair_lists = pair_lists + grad_pairs(text_kept, text_grads)
    table_grad, table_square = table_sum(
        jnp.minimum(held_count, cap),
        first_rows.reshape(-1),
        arrived.reshape(device_count, cap, D_TXT),
        vocab_dev,
    )

    def more_grads(turn, total):
        rows = fwd_dot(pick_matrix(own_slots(turn), slot_count), grad_rows).astype(jnp.bfloat16)
        rows = lax.all_to_all(rows.reshape(gy_size, cap, D_TXT), "gy", 0, 0, tiled=True)
        rows = lax.all_gather(rows, "gx", axis=0).reshape(device_count * cap, D_TXT).astype(jnp.float32)
        taken = jnp.arange(cap)[None, :] < (held_count - turn * cap)[:, None]
        rows = jnp.where(taken.reshape(-1)[:, None], rows, 0.0)
        return total.at[held_rows(turn).reshape(-1)].add(rows)

    table_grad, table_squares = lax.cond(
        rounds > 1,
        lambda total, square: (
            lambda whole: (whole, jnp.sum(whole * whole))
        )(lax.fori_loop(1, rounds, more_grads, total)),
        lambda total, square: (total, jnp.sum(square)),
        table_grad,
        table_square,
    )
    total_rows = window_start(shard, device_count - 1) + window_rows(shard, GROUP * CHUNKS)
    vec_rows = jnp.concatenate(
        [
            image_grads[7][:1].reshape(-1, LANES),
            image_grads[7].reshape(-1, LANES),
            image_grads[8].reshape(-1, LANES),
            text_grads[7].reshape(-1, LANES),
            text_grads[8][2:].reshape(-1, LANES),
            jnp.pad((temper_one + temper_two).reshape(1, 1), ((0, 0), (0, LANES - 1))),
        ]
    )
    vec_rows = jnp.pad(vec_rows, ((0, total_rows - matrix_rows() - vec_rows.shape[0]), (0, 0)))
    local_grads = weight_grads(pair_lists, vec_rows)
    grad_window = reduce_windows(local_grads, shard, gx_size, gy_size, 1)
    grad_shard = lift_window(grad_window, shard, gy_size)
    table_squares = jnp.where(lax.axis_index("gx") == 0, table_squares, 0.0)
    squares = jnp.sum(grad_shard * grad_shard) + table_squares
    (every,) = exchange_all([jnp.full((8, LANES), squares)], gx_size, gy_size, 2, "squares")
    grad_norm = jnp.sqrt(jnp.sum(every[:, 0, 0]))
    factor = jnp.minimum(1.0, clip_limit / (grad_norm + 1e-06))
    matrix_stop = matrix_rows() * LANES
    position = my_index * shard + jnp.arange(shard)
    is_matrix = position < matrix_stop
    rates = jnp.where(is_matrix, rate_matrix, rate_vector)
    decays = jnp.where(is_matrix, decay_rate, 0.0)
    master_out, first_out, second_out = adam_step(
        flat_master, flat_first, flat_second, grad_shard * factor, rates, decays
    )
    table_out, table_first_out, table_second_out = adam_step(
        table, table_first, table_second, table_grad * factor, rate_table, 0.0
    )
    return (
        master_out,
        first_out,
        second_out,
        table_out,
        table_first_out,
        table_second_out,
        loss_sum,
        total_count,
        grad_norm,
    )


def solution(mesh):
    placed = (
        P(("gx", "gy")),
        P(("gx", "gy")),
        P(("gx", "gy")),
        P("gy", None),
        P("gy", None),
        P("gy", None),
        P(("gx", "gy"), None, None),
        P(("gx", "gy"), None),
        P(("gx", "gy")),
        P(),
        P(),
        P(("gx", "gy"), None),
        P(("gx", "gy"), None),
    )
    return jax.shard_map(
        body,
        mesh=mesh,
        in_specs=placed,
        out_specs=(
            P(("gx", "gy")),
            P(("gx", "gy")),
            P(("gx", "gy")),
            P("gy", None),
            P("gy", None),
            P("gy", None),
            P(),
            P(),
            P(),
        ),
        check_vma=False,
    )
```

time: 2850 us -> 727 us (0.26); the launches traced: 2810 us -> 723 us
  waiting for transfers between devices: 1340 us -> 0 us
  local copies, waits for them, and re-layouts: 706 us -> 37.4 us
  Pallas kernels: 0 us -> 597 us
  blocking collectives: 356 us -> 0 us
  matrix products: 190 us -> 7.5 us
  other arithmetic: 194 us -> 56 us
    unnamed x9 -> x0, waiting for transfers between devices: 1040 us -> none
    pallas_call x0 -> x15, Pallas kernels: none -> 597 us  [the longest x1 130 us: gather_windows(): pl.pallas_call(functools.partial(gather_kernel, sizes), out_shape=jax.Sha...]
    concatenate x6 -> x1, local copies, waits for them, and re-layouts: 406 us -> 1 us  [body(): jnp.concatenate([image_grads[7][:1].reshape(-1, LANES), image_grads[7].re...]
    all_gather x5 -> x0, blocking collectives: 317 us -> none  [the longest x1 76.2 us: body(): lax.all_gather(cached_text, ('gx', 'gy'), axis=0, tiled=True)]
    reduce_scatter x3 -> x0, waiting for transfers between devices: 261 us -> none  [the longest x1 132 us: body(): lax.psum_scatter(img_cols, ('gx', 'gy'), scatter_dimension=0, tiled=True)]
    dot_general x61 -> x12, matrix products: 181 us -> 7.5 us  [the longest x3 3.27 us: dot_tn(): lax.dot_general(left_side, right_side, (((0,), (0,)), ((), ())), preferre...]
    reshape x44 -> x12, local copies, waits for them, and re-layouts: 146 us -> 5.18 us  [the longest x1 2.03 us: image_inputs(): pixels = jnp.pad(pixels, ((0, 0), (1, 0), (0, 0))).reshape(-1, PATCH_DIM)]
    unnamed x295 -> x34, local copies, waits for them, and re-layouts: 69.7 us -> 11.7 us
  transfers between devices with their start and end apart: 7 -> 0, of which waited for: 5 -> 0; matrix products, arithmetic and copies ran while one was open for 18% -> 0% of each run, Pallas kernels for 0% -> 0%
where the time goes in v1:
time: 727 us; the launch traced here: 723 us
  Pallas kernels  597 us (82%)
  other arithmetic  56 us (8%)
  local copies, waits for them, and re-layouts  37.4 us (5%)
  between operations  24.9 us (3%)
  matrix products  7.5 us (1%)
    pallas_call x1, Pallas kernels, gather_windows(): pl.pallas_call(functools.partial(gather_kernel, sizes), out_shape=jax.Sha...  130 us
    pallas_call x1, Pallas kernels, reduce_windows(): pl.pallas_call(functools.partial(reduce_kernel, shard, (x_size, low_size,...  129 us
    pallas_call x2, Pallas kernels, share_rows(): pl.pallas_call(functools.partial(share_kernel, gx_size, gy_size, everyone...  96.9 us
    pallas_call x2, Pallas kernels, exchange_all(): pl.pallas_call(functools.partial(exchange_kernel, gx_size, gy_size, many)...  65.1 us
    pallas_call x1, Pallas kernels, weight_grads(): pl.pallas_call(functools.partial(grads_kernel, parts, total_rows), out_sh...  45.9 us
    sub x2, other arithmetic, adam_step(): weight - rate * (first_hat / (jnp.sqrt(second_hat) + adam_eps) + decay *...  37.9 us
    pallas_call x1, Pallas kernels, table_sum(): pl.pallas_call(functools.partial(table_sum_kernel, cap), out_shape=[jax.S...  36.4 us
    pallas_call x2, Pallas kernels, tower_backward(): pl.pallas_call(functools.partial(tower_backward_kernel, tower), out_shape...  34.4 us

profile of v1, /device:TPU:0, one launch (start us, length us, event | category | flops | bytes accessed | tf_op | source)
XLA Modules:
  0.0 723.0 jit_solution(13324393959438558935)
XLA Ops:
  7.2 3.0 copy.28
  10.2 0.7 pad.38.clone
  11.0 2.0 reshape.361.refs_3_.refs_0_
  13.1 1.6 pad_bitcast_fusion.flat_ref
  14.7 0.9 place_window.1
  15.7 130.5 %gather_windows.1.gathered_ref = bf16[107520,128]{1,0:T(8,128)(2,1)} custom-call(bf16[3360,128]{1,0:T(8,128)(2,1)S(1)} %pad_maximum_fusion.window_ref), custom_call_target="tpu_custom_call" | custom-call | tf_op jit(solution)/shard_map/gather_windows/pallas_call | solution.py:1183
  146.2 29.5 %spread_weights.1 = (bf16[3072,768]{1,0:T(8,128)(2,1)}, bf16[768,3072]{1,0:T(8,128)(2,1)}, bf16[768,3072]{1,0:T(8,128)(2,1)}, bf16[3072,768]{1,0:T(8,128)(2,1)},...) custom-call(bf16[107520,128]{1,0:T(8,128)(2,1)} %gather_windows.1.ga, ...), custom_call_target="tpu_custom_call" | custom-call | tf_op jit(solution)/shard_map/spread_weights/pallas_call | solution.py:722
  175.7 1.3 copy-done.1
  177.0 1.3 copy-done.2
  178.3 0.9 copy-done.4
  179.2 0.8 copy-done.5
  180.0 0.6 slice.87.refs_1_
  180.6 1.1 slice.120
  181.7 0.3 reshape.375
  182.0 0.7 fusion.99
  182.8 0.6 pad.42.refs_1_
  183.8 1.1 pad.43.refs_2_
  184.9 0.9 slice_convert_fusion
  186.3 1.8 select_reduce_fusion.2
  188.3 9.5 %gather_fusion.1 = bf16[1536,512]{1,0:T(8,128)(2,1)S(1)} fusion(f32[6176,512]{1,0:T(8,128)} %param.22, s32[2048]{0:T(1024)S(1)} %pad_clamp_fusion.1), kind=kCustom, calls=%fused_computation.1 | custom fusion | bytes 3151872 | tf_op jit(solution)/shard_map/jit(_take)/gather | solution.py:1510
  197.8 0.4 broadcast_select_fusion.1
  198.2 32.6 %token_rows.1 = bf16[1,8,192,512]{3,2,1,0:T(8,128)(2,1)S(1)} custom-call(bf16[8,192,512]{2,1,0:T(8,128)(2,1)S(1)} %bitcast.103), custom_call_target="tpu_custom_call" | custom-call | tf_op jit(solution)/shard_map/token_rows/pallas_call | solution.py:1006
  231.1 1.2 fusion.20
  232.3 0.6 convert_reduce_fusion
  232.9 0.6 reduce_max.27
  234.3 8.1 %convert.17 = bf16[6176,512]{1,0:T(8,128)(2,1)} convert(f32[6176,512]{1,0:T(8,128)} %param.22) | non-fusion elementwise | flops 3162112 | bytes 18972672
  242.4 0.4 while.22
  242.8 0.9 pad.44.refs_3_
  243.6 10.0 %text_forward.1 = (f32[624,512]{1,0:T(8,128)}, bf16[624,512]{1,0:T(8,128)(2,1)}, bf16[624,1024]{1,0:T(8,128)(2,1)}, bf16[16,512]{1,0:T(8,128)(2,1)}, bf16[16,512...) custom-call(s32[8]{0:T(128)} %refs_0_.7, ...), custom_call_target="tpu_custom_call" | custom-call | tf_op jit(solution)/shard_map/text_forward/pallas_call | solution.py:294
  253.6 0.7 convert_element_type.99
  254.5 1.2 tile.21.refs_2_
  255.7 16.8 %image_forward.1 = (f32[400,768]{1,0:T(8,128)}, bf16[400,768]{1,0:T(8,128)(2,1)}, bf16[400,1536]{1,0:T(8,128)(2,1)}, bf16[16,768]{1,0:T(8,128)(2,1)}, bf16[16,76...) custom-call(s32[8]{0:T(128)} %refs_0_.7, ...), custom_call_target="tpu_custom_call" | custom-call | tf_op jit(solution)/shard_map/image_forward/pallas_call | solution.py:294
  272.5 0.7 convert_element_type.92
  273.3 25.0 %embeddings.1 = bf16[32,16,512]{2,1,0:T(8,128)(2,1)S(1)} custom-call(bf16[16,512]{1,0:T(8,128)(2,1)S(1)} %pad_maximum_fusion.10.refs_0_), custom_call_target="tpu_custom_call" | custom-call | tf_op jit(solution)/shard_map/embeddings/pallas_call | solution.py:886
  298.3 0.5 slice.88
  300.0 0.2 fusion.49
  300.2 0.3 convolution_multiply_fusion.1
  300.6 0.5 select_reduce_fusion.3
  301.0 0.3 exponential_reduce_fusion
  301.4 0.9 fusion.43
  303.4 1.0 convolution_add_fusion.1.refs_2_
  304.4 19.7 %image_backward.1 = (bf16[16,512]{1,0:T(8,128)(2,1)}, bf16[16,768]{1,0:T(8,128)(2,1)}, bf16[16,3072]{1,0:T(8,128)(2,1)}, bf16[16,768]{1,0:T(8,128)(2,1)}, bf16[1...) custom-call(s32[8]{0:T(128)} %refs_0_.7, ...), custom_call_target="tpu_custom_call" | custom-call | tf_op jit(solution)/shard_map/image_backward/pallas_call | solution.py:438
  324.2 0.9 multiply_reduce_fusion.2
  325.4 1.0 convolution_add_fusion.refs_2_
  326.4 14.7 %text_backward.1 = (bf16[16,512]{1,0:T(8,128)(2,1)}, bf16[16,512]{1,0:T(8,128)(2,1)}, bf16[16,2048]{1,0:T(8,128)(2,1)}, bf16[16,512]{1,0:T(8,128)(2,1)}, bf16[16...) custom-call(s32[8]{0:T(128)} %refs_0_.7, ...), custom_call_target="tpu_custom_call" | custom-call | tf_op jit(solution)/shard_map/text_backward/pallas_call | solution.py:438
  341.2 0.9 reshape.382
  342.1 0.7 slice.106
  344.2 1.0 concatenate.35
  345.2 0.8 pad.46.refs_26_
  345.9 45.9 %weight_grads.1.grads_ref = f32[104176,128]{1,0:T(8,128)} custom-call(bf16[400,3072]{1,0:T(8,128)(2,1)} %reshape.361.refs_3_.refs_0_, bf16[400,768]{1,0:T(8,128)(2,1)} %get-tuple-element.294.refs_1_, bf16[16,768]{1,0:T(8,128)(2,1)} %get-tuple-element.283.refs_6_.refs_2_, bf16[16,768]{1,0:T(8,128)(2,1)} %get-tuple-element.295.refs_3_, ...), custom_call_target="tpu_custom_call" | custom-call | tf_op jit(solution)/shard_map/weight_grads/pallas_call | solution.py:817
  391.8 128.6 %reduce_windows.1.window_ref = f32[3328,128]{1,0:T(8,128)} custom-call(f32[104176,128]{1,0:T(8,128)} %weight_grads.1.grads_ref), custom_call_target="tpu_custom_call" | custom-call | tf_op jit(solution)/shard_map/reduce_windows/pallas_call | solution.py:1364
  520.4 1.4 copy-done.3
  521.9 1.7 lift_window.1
  523.6 1.0 multiply_reduce_fusion.1
  524.7 1.4 fusion.14
  526.1 64.3 %token_grads.1 = bf16[4,8,192,512]{3,2,1,0:T(8,128)(2,1)} custom-call(bf16[8,192,512]{2,1,0:T(8,128)(2,1)S(1)} %bitcast.105), custom_call_target="tpu_custom_call" | custom-call | tf_op jit(solution)/shard_map/token_grads/pallas_call | solution.py:1006
  590.5 2.8 copy-done
  593.2 36.4 %table_sum.1 = (f32[6176,512]{1,0:T(8,128)}, f32[8,512]{1,0:T(8,128)S(1)}) custom-call(s32[32]{0:T(128)S(1)} %broadcast_minimum_fusion.counts_ref, s32[6144]{0:T(1024)S(1)} %reshape.386.index_ref, bf16[32,192,512]{2,1,0:T(8,128)(2,1)S(1)} %bitcast.100), custom_call_target="tpu_custom_call" | custom-call | tf_op jit(solution)/shard_map/table_sum/pallas_call | solution.py:1076
  629.7 0.8 conditional.1
  629.7 0.6 reduce_sum.148
  631.8 40.1 %squares.1 = f32[32,8,128]{2,1,0:T(8,128)S(1)} custom-call(f32[8,128]{1,0:T(8,128)S(1)} %broadcast_in_dim.221.refs_0_), custom_call_target="tpu_custom_call" | custom-call | tf_op jit(solution)/shard_map/squares/pallas_call | solution.py:886
  671.9 0.6 slice_reduce_fusion
  673.3 5.8 multiply_subtract_fusion.1
  679.1 32.2 %multiply_subtract_fusion = (f32[6176,512]{1,0:T(8,128)}, f32[6176,512]{1,0:T(8,128)}, f32[6176,512]{1,0:T(8,128)}) fusion(f32[6176,512]{1,0:T(8,128)} %param.22, f32[6176,512]{1,0:T(8,128)} %get-tuple-element.329, f32[]{:T(128)S(6)} %min_shard_map.3, f32[6176,512]{1,0:T(8,128)} %param.23, f32[6176,512]{1,0:T(8,128)} %param.24), kind=kLoop, calls=%fused_computation.39 | loop fusion | flops 50593792 | bytes 88539136 | tf_op jit(solution)/shard_map/sub | solution.py:488
  (80 shorter events, 3.0 us)
Async XLA Ops:
  10.9 2.1 copy-start.13
  10.9 2.1 copy-start.11
  11.0 2.1 copy-start.12
  175.7 1.3 copy-start.1
  177.0 1.3 copy-start.2
  178.3 0.9 copy-start.4
  179.2 0.8 copy-start.5
  255.7 43.8 %copy-start.14 = (s32[4,8]{1,0:T(4,128)S(1)}, s32[4,8]{1,0:T(4,128)}, u32[]{:S(2)}) copy-start(s32[4,8]{1,0:T(4,128)} %param.28) | copy-start | bytes 388
  255.7 44.1 %copy-start.10 = (s32[256]{0:T(256)S(1)}, s32[256]{0:T(256)}, u32[]{:S(2)}) copy-start(s32[256]{0:T(256)} %param.29) | copy-start | bytes 3076
  255.7 44.2 %copy-start.7 = (bf16[32,8,512]{2,1,0:T(8,128)(2,1)S(1)}, bf16[32,8,512]{2,1,0:T(8,128)(2,1)}, u32[]{:S(2)}) copy-start(bf16[32,8,512]{2,1,0:T(8,128)(2,1)} %get-tuple-element.277) | copy-start | bytes 786436
  326.4 14.7 %copy-start.8 = (f32[50,768]{1,0:T(8,128)S(1)}, f32[50,768]{1,0:T(8,128)}, u32[]{:S(2)}) copy-start(f32[50,768]{1,0:T(8,128)} %get-tuple-element.321) | copy-start | bytes 460804
  326.4 14.8 %copy-start.9 = (f32[8,768]{1,0:T(8,128)S(1)}, f32[8,768]{1,0:T(8,128)}, u32[]{:S(2)}) copy-start(f32[8,768]{1,0:T(8,128)} %get-tuple-element.322) | copy-start | bytes 73732
  520.4 1.5 copy-start.3
  521.9 2.8 copy-start.6
  590.5 2.8 copy-start

commit v2 on v1

--- a/solution.py
+++ b/solution.py
@@ -960,8 +960,11 @@
     return gx_size // 2, gy_size // 4, 4
 
 
+NO_TOKEN = 65535
+
+
 def route_capacity(tokens, gy_size):
-    return max(5 * tokens // (2 * gy_size * GROUP), 1) * GROUP
+    return GROUP * (1 + 17 * tokens // (16 * gy_size * GROUP))
 
 
 def share_kernel(gx_size, gy_size, everyone, send_ref, out_ref, own_sem, row_send, row_recv, x_send, x_recv, core_send,
@@ -1019,7 +1022,7 @@
 
 def table_sum_kernel(cap, counts_ref, index_ref, rows_ref, out_ref, square_ref, wide, row_sem):
     sources = rows_ref.shape[0]
-    vocab = out_ref.shape[0]
+    vocab = out_ref.shape[0] - 8
 
     def fetch(source):
         slot = lax.rem(source, 2)
@@ -1033,6 +1036,7 @@
         return carry
 
     lax.fori_loop(0, vocab // block, clear, 0)
+    out_ref[vocab:, :] = jnp.zeros((8, D_TXT), jnp.float32)
 
     def one_source(source, carry):
         slot = lax.rem(source, 2)
@@ -1042,20 +1046,20 @@
             fetch(source + 1).start()
 
         fetch(source).wait()
-        count = counts_ref[source]
         widened = wide.at[slot]
 
         def add(group, carry):
             rows = widened[pl.ds(pl.multiple_of(group * GROUP, GROUP), GROUP), :].astype(jnp.float32)
-            for i in range(GROUP):
-                @pl.when(group * GROUP + i < count)
-                def _(i=i):
-                    place = pl.ds(index_ref[source * cap + group * GROUP + i], 1)
-                    out_ref[place, :] = out_ref[place, :] + rows[i : i + 1, :]
-
+            for half in range(0, GROUP, 8):
+                places = [
+                    pl.ds(index_ref[source * cap + group * GROUP + half + i], 1) for i in range(8)
+                ]
+                sums = [out_ref[place, :] + rows[half + i : half + i + 1, :] for i, place in enumerate(places)]
+                for place, value in zip(places, sums):
+                    out_ref[place, :] = value
             return carry
 
-        lax.fori_loop(0, (count + GROUP - 1) // GROUP, add, 0)
+        lax.fori_loop(0, (counts_ref[source] + GROUP - 1) // GROUP, add, 0)
         return carry
 
     lax.fori_loop(0, sources, one_source, 0)
@@ -1076,7 +1080,7 @@
     return pl.pallas_call(
         functools.partial(table_sum_kernel, cap),
         out_shape=[
-            jax.ShapeDtypeStruct((vocab, D_TXT), jnp.float32),
+            jax.ShapeDtypeStruct((vocab + 8, D_TXT), jnp.float32),
             jax.ShapeDtypeStruct((8, D_TXT), jnp.float32),
         ],
         in_specs=[pl.BlockSpec(memory_space=pltpu.SMEM)] * 2 + [pl.BlockSpec(memory_space=pl.ANY)],
@@ -1097,11 +1101,11 @@
     return (jnp.arange(count)[:, None] == slots[None, :]).astype(jnp.bfloat16)
 
 
-def gather_kernel(sizes, window_ref, out_ref, own_sem, h_send, h_recv, b_send, b_recv, a_send, a_recv, core_send,
+def gather_kernel(sizes, chunks, window_ref, out_ref, own_sem, h_send, h_recv, b_send, b_recv, a_send, a_recv, core_send,
                   core_recv):
     at = Places(sizes)
     rows = window_ref.shape[0]
-    chunk = rows // GATHER_CHUNKS
+    chunk = rows // chunks
     me = at.linear(at.core, at.a, at.b, at.h)
     sibling, peers_a, peers_b, peers_h = at.sibling(), at.along_a(), at.along_b(), at.along_h()
     greet_all([sibling] + peers_a + peers_b + peers_h)
@@ -1153,13 +1157,13 @@
 
     def turn(t, carry):
         for depth, stage in enumerate((stage_h, stage_b, stage_a, stage_core)):
-            @pl.when((t >= depth) & (t < GATHER_CHUNKS + depth))
+            @pl.when((t >= depth) & (t < chunks + depth))
             def _():
                 stage(t - depth)
 
         return carry
 
-    lax.fori_loop(0, GATHER_CHUNKS + 3, turn, 0)
+    lax.fori_loop(0, chunks + 3, turn, 0)
 
     def whole(count):
         return out_ref.at[pl.ds(0, count * rows)]
@@ -1176,21 +1180,21 @@
     last.wait_recv()
 
 
-def gather_windows(window, gx_size, gy_size, number):
+def gather_windows(window, gx_size, gy_size, chunks, number, name):
     sizes = axis_sizes(gx_size, gy_size)
     a, b, h = sizes[0] - 1, sizes[1] - 1, sizes[2] - 1
     dma = pltpu.SemaphoreType.DMA
     return pl.pallas_call(
-        functools.partial(gather_kernel, sizes),
+        functools.partial(gather_kernel, sizes, chunks),
         out_shape=jax.ShapeDtypeStruct((gx_size * gy_size * window.shape[0], LANES), window.dtype),
         in_specs=[pl.BlockSpec(memory_space=pltpu.VMEM)],
         out_specs=pl.BlockSpec(memory_space=pl.ANY),
-        scratch_shapes=[dma((GATHER_CHUNKS,)), dma((h,)), dma((GATHER_CHUNKS, h)), dma((b,)), dma((GATHER_CHUNKS, b)), dma((a,)),
-                        dma((GATHER_CHUNKS, a)), dma, dma],
+        scratch_shapes=[dma((chunks,)), dma((h,)), dma((chunks, h)), dma((b,)), dma((chunks, b)), dma((a,)),
+                        dma((chunks, a)), dma, dma],
         compiler_params=pltpu.CompilerParams(
             collective_id=number, has_side_effects=True, vmem_limit_bytes=32 << 20
         ),
-        name="gather_windows",
+        name=name,
     )(window)
 
 
@@ -1464,7 +1468,12 @@
     tokens = token_ids.size
     vocab_dev = table.shape[0]
     cap = route_capacity(tokens, gy_size)
-    flat_ids = jnp.pad(token_ids.reshape(-1), (0, ID_ROWS * LANES // 2 - tokens)).reshape(-1, LANES)
+    own_ids = token_ids.reshape(-1)
+    same = own_ids[:, None] == own_ids[None, :]
+    order = jnp.arange(tokens)
+    leading = ~jnp.any(same & (order[None, :] < order[:, None]), 1)
+    flat_ids = jnp.where(leading, own_ids, NO_TOKEN)
+    flat_ids = jnp.pad(flat_ids, (0, ID_ROWS * LANES // 2 - tokens)).reshape(-1, LANES)
     payload = [
         place_window(flat_master, gy_size),
         jnp.concatenate([cached_image, cached_text], 0).reshape(CACHED_ROWS, LANES),
@@ -1473,7 +1482,7 @@
     used = sum(part.shape[0] for part in payload)
     step = GROUP * GATHER_CHUNKS
     payload = jnp.pad(jnp.concatenate(payload, 0), ((0, -used % step), (0, 0)))
-    gathered = gather_windows(payload, gx_size, gy_size, 4)
+    gathered = gather_windows(payload, gx_size, gy_size, GATHER_CHUNKS, 4, "gather_weights")
     every_part = gathered.reshape(device_count, -1, LANES)
     cached = every_part[:, used - ID_ROWS - CACHED_ROWS : used - ID_ROWS].reshape(device_count, -1, EMBED)
     cache_img, cache_txt = lax.optimization_barrier((cached[:, :pairs_dev], cached[:, pairs_dev:]))
@@ -1489,14 +1498,16 @@
     held_rank = jnp.where(held, ranks(held), -1)
     held_row = ids_all - me_y * vocab_dev
     held_count = jnp.sum(held, 1)
-    own_holder = lax.dynamic_slice_in_dim(holders, my_index, 1, 0)[0]
-    own_flags = jnp.arange(gy_size)[:, None] == own_holder[None, :]
-    own_rank = jnp.sum(jnp.where(own_flags, ranks(own_flags), 0), 0)
+    own_flags = (jnp.arange(gy_size)[:, None] == own_ids[None, :] // vocab_dev) & leading[None, :]
+    own_place = jnp.arange(gy_size)[:, None] * tokens + ranks(own_flags)
+    own_place = jnp.sum(jnp.where(own_flags, own_place, 0), 0)
+    own_place = jnp.sum(jnp.where(same & leading[None, :], own_place[None, :], 0), 1)
+    own_holder, own_rank = own_place // tokens, own_place % tokens
 
     def held_rows(turn):
         slots = held_rank - turn * cap
         found = slots[:, None, :] == jnp.arange(cap)[None, :, None]
-        return jnp.sum(jnp.where(found, held_row[:, None, :], 0), 2)
+        return vocab_dev + jnp.sum(jnp.where(found, held_row[:, None, :] - vocab_dev, 0), 2)
 
     def own_slots(turn):
         rank = own_rank - turn * cap
@@ -1507,7 +1518,7 @@
 
     def rows_to_send(index):
         index = lax.dynamic_slice_in_dim(index, group_start, gy_size, 0)
-        return lax.optimization_barrier(jnp.take(table, index.reshape(-1), axis=0)).astype(jnp.bfloat16)
+        return lax.optimization_barrier(jnp.take(table, index.reshape(-1), axis=0, mode="clip")).astype(jnp.bfloat16)
 
     landed = share_rows(
         rows_to_send(first_rows).reshape(gy_size, cap, D_TXT), gx_size, gy_size, False, 5, "token_rows"
@@ -1532,9 +1543,9 @@
     text_kept = tower_forward(TEXT, end_pos, text_gains, text_base, text_rows, text_weights)
     image_emb = image_kept[14].astype(jnp.bfloat16)
     text_emb = text_kept[14].astype(jnp.bfloat16)
-    (embeds,) = exchange_all(
-        [jnp.concatenate([image_emb, text_emb], 0)], gx_size, gy_size, 0, "embeddings"
-    )
+    embeds = jnp.concatenate([image_emb, text_emb], 0).reshape(-1, LANES)
+    embeds = gather_windows(embeds, gx_size, gy_size, 1, 0, "embeddings")
+    embeds = embeds.reshape(device_count, 2 * pairs_dev, EMBED)
     all_img, all_txt = lax.optimization_barrier((embeds[:, :pairs_dev], embeds[:, pairs_dev:]))
     all_img, all_txt = all_img.reshape(-1, EMBED), all_txt.reshape(-1, EMBED)
     total_pairs = all_img.shape[0]
@@ -1586,14 +1597,12 @@
         rows = fwd_dot(pick_matrix(own_slots(turn), slot_count), grad_rows).astype(jnp.bfloat16)
         rows = lax.all_to_all(rows.reshape(gy_size, cap, D_TXT), "gy", 0, 0, tiled=True)
         rows = lax.all_gather(rows, "gx", axis=0).reshape(device_count * cap, D_TXT).astype(jnp.float32)
-        taken = jnp.arange(cap)[None, :] < (held_count - turn * cap)[:, None]
-        rows = jnp.where(taken.reshape(-1)[:, None], rows, 0.0)
         return total.at[held_rows(turn).reshape(-1)].add(rows)
 
     table_grad, table_squares = lax.cond(
         rounds > 1,
         lambda total, square: (
-            lambda whole: (whole, jnp.sum(whole * whole))
+            lambda whole: (whole, jnp.sum(whole[:vocab_dev] * whole[:vocab_dev]))
         )(lax.fori_loop(1, rounds, more_grads, total)),
         lambda total, square: (total, jnp.sum(square)),
         table_grad,
@@ -1628,7 +1637,7 @@
         flat_master, flat_first, flat_second, grad_shard * factor, rates, decays
     )
     table_out, table_first_out, table_second_out = adam_step(
-        table, table_first, table_second, table_grad * factor, rate_table, 0.0
+        table, table_first, table_second, table_grad[:vocab_dev] * factor, rate_table, 0.0
     )
     return (
         master_out,

time: 727 us -> 636 us (0.87)
  Pallas kernels: 597 us -> 505 us
    pallas_call x2 -> x1, Pallas kernels: 65.1 us -> 13.5 us  [exchange_all(): pl.pallas_call(functools.partial(exchange_kernel, gx_size, gy_size, many)...]
    pallas_call x2, Pallas kernels: 96.9 us -> 56.4 us  [share_rows(): pl.pallas_call(functools.partial(share_kernel, gx_size, gy_size, everyone...]
    pallas_call x1 -> x2, Pallas kernels: 130 us -> 150 us  [gather_windows(): pl.pallas_call(functools.partial(gather_kernel, sizes, chunks), out_shape...]
    pallas_call x1, Pallas kernels: 36.4 us -> 18.2 us  [table_sum(): pl.pallas_call(functools.partial(table_sum_kernel, cap), out_shape=[jax.S...]
where the time goes in v2:
time: 636 us; the launch traced here: 627 us
  Pallas kernels  505 us (79%)
  other arithmetic  56.4 us (9%)
  local copies, waits for them, and re-layouts  33.4 us (5%)
  between operations  24.8 us (4%)
  matrix products  6.38 us (1%)
    pallas_call x2, Pallas kernels, gather_windows(): pl.pallas_call(functools.partial(gather_kernel, sizes, chunks), out_shape...  150 us
    pallas_call x1, Pallas kernels, reduce_windows(): pl.pallas_call(functools.partial(reduce_kernel, shard, (x_size, low_size,...  128 us
    pallas_call x2, Pallas kernels, share_rows(): pl.pallas_call(functools.partial(share_kernel, gx_size, gy_size, everyone...  56.4 us
    pallas_call x1, Pallas kernels, weight_grads(): pl.pallas_call(functools.partial(grads_kernel, parts, total_rows), out_sh...  45.9 us
    sub x2, other arithmetic, adam_step(): weight - rate * (first_hat / (jnp.sqrt(second_hat) + adam_eps) + decay *...  37.4 us
    pallas_call x2, Pallas kernels, tower_backward(): pl.pallas_call(functools.partial(tower_backward_kernel, tower), out_shape...  34.4 us
    pallas_call x1, Pallas kernels, spread_weights(): pl.pallas_call(functools.partial(spread_entry, shard, count, vec_rows), o...  29.5 us
    pallas_call x2, Pallas kernels, tower_forward(): pl.pallas_call(functools.partial(tower_forward_kernel, tower), out_shape=...  26.7 us

profile of v2, /device:TPU:0, one launch (start us, length us, event | category | flops | bytes accessed | tf_op | source)
XLA Modules:
  0.0 626.7 jit_solution(13419067590059301335)
XLA Ops:
  7.2 3.0 copy.28
  10.2 0.7 pad.38.clone
  11.0 1.9 reshape.342.refs_3_.refs_0_
  13.3 1.6 pad_bitcast_fusion.flat_ref
  14.8 0.9 place_window.1
  15.9 130.5 %gather_weights.1.gathered_ref = bf16[107520,128]{1,0:T(8,128)(2,1)} custom-call(bf16[3360,128]{1,0:T(8,128)(2,1)S(1)} %pad_maximum_fusion.window_ref), custom_call_target="tpu_custom_call" | custom-call | tf_op jit(solution)/shard_map/gather_weights/pallas_call | solution.py:1187
  146.3 29.5 %spread_weights.1 = (bf16[3072,768]{1,0:T(8,128)(2,1)}, bf16[768,3072]{1,0:T(8,128)(2,1)}, bf16[768,3072]{1,0:T(8,128)(2,1)}, bf16[3072,768]{1,0:T(8,128)(2,1)},...) custom-call(bf16[107520,128]{1,0:T(8,128)(2,1)} %gather_weights.1.ga, ...), custom_call_target="tpu_custom_call" | custom-call | tf_op jit(solution)/shard_map/spread_weights/pallas_call | solution.py:722
  175.8 1.3 copy-done
  177.1 1.3 copy-done.1
  178.5 0.9 copy-done.3
  179.3 0.8 copy-done.4
  180.2 0.6 slice.94.refs_1_
  180.8 1.1 slice.130
  181.8 0.3 reshape.355
  182.2 0.7 fusion.102
  182.9 0.6 pad.42.refs_1_
  183.9 1.1 pad.43.refs_2_
  185.0 0.9 slice_convert_fusion
  186.0 0.7 convert_reduce_fusion.3
  186.9 0.9 select_reduce_fusion.2
  188.0 7.3 %gather_fusion.1 = bf16[768,512]{1,0:T(8,128)(2,1)S(1)} fusion(f32[6176,512]{1,0:T(8,128)} %param.22, s32[1024]{0:T(1024)S(1)} %pad_clamp_fusion.1), kind=kCustom, calls=%fused_computation.1 | custom fusion | bytes 1575936 | tf_op jit(solution)/shard_map/jit(_take)/gather | solution.py:1521
  195.3 19.8 %token_rows.1 = bf16[1,8,96,512]{3,2,1,0:T(8,128)(2,1)S(1)} custom-call(bf16[8,96,512]{2,1,0:T(8,128)(2,1)S(1)} %bitcast.103), custom_call_target="tpu_custom_call" | custom-call | tf_op jit(solution)/shard_map/token_rows/pallas_call | solution.py:1009
  215.4 0.5 select_reduce_fusion.3
  215.9 0.7 fusion.17
  216.6 0.6 convert_reduce_fusion
  217.2 0.6 reduce_max.27
  218.6 8.1 %convert.17 = bf16[6176,512]{1,0:T(8,128)(2,1)} convert(f32[6176,512]{1,0:T(8,128)} %param.22) | non-fusion elementwise | flops 3162112 | bytes 18972672
  226.7 0.3 while.24
  227.0 0.9 pad.44.refs_3_
  227.9 10.0 %text_forward.1 = (f32[624,512]{1,0:T(8,128)}, bf16[624,512]{1,0:T(8,128)(2,1)}, bf16[624,1024]{1,0:T(8,128)(2,1)}, bf16[16,512]{1,0:T(8,128)(2,1)}, bf16[16,512...) custom-call(s32[8]{0:T(128)} %refs_0_.7, ...), custom_call_target="tpu_custom_call" | custom-call | tf_op jit(solution)/shard_map/text_forward/pallas_call | solution.py:294
  237.9 0.7 convert_element_type.107
  238.8 1.2 tile.21.refs_2_
  240.0 16.8 %image_forward.1 = (f32[400,768]{1,0:T(8,128)}, bf16[400,768]{1,0:T(8,128)(2,1)}, bf16[400,1536]{1,0:T(8,128)(2,1)}, bf16[16,768]{1,0:T(8,128)(2,1)}, bf16[16,76...) custom-call(s32[8]{0:T(128)} %refs_0_.7, ...), custom_call_target="tpu_custom_call" | custom-call | tf_op jit(solution)/shard_map/image_forward/pallas_call | solution.py:294
  256.8 0.8 convert_element_type.100
  257.6 19.7 %embeddings.1 = bf16[2048,128]{1,0:T(8,128)(2,1)S(1)} custom-call(bf16[64,128]{1,0:T(8,128)(2,1)S(1)} %reshape.352.window_ref), custom_call_target="tpu_custom_call" | custom-call | tf_op jit(solution)/shard_map/embeddings/pallas_call | solution.py:1187
  277.7 0.5 slice.95
  279.6 0.4 convolution_multiply_fusion.1
  279.9 0.5 select_reduce_fusion.4
  280.4 0.3 exponential_reduce_fusion
  280.7 0.9 fusion.43
  282.8 1.0 convolution_add_fusion.1.refs_2_
  283.8 19.7 %image_backward.1 = (bf16[16,512]{1,0:T(8,128)(2,1)}, bf16[16,768]{1,0:T(8,128)(2,1)}, bf16[16,3072]{1,0:T(8,128)(2,1)}, bf16[16,768]{1,0:T(8,128)(2,1)}, bf16[1...) custom-call(s32[8]{0:T(128)} %refs_0_.7, ...), custom_call_target="tpu_custom_call" | custom-call | tf_op jit(solution)/shard_map/image_backward/pallas_call | solution.py:438
  303.6 0.9 multiply_reduce_fusion.2
  304.8 1.0 convolution_add_fusion.refs_2_
  305.8 14.7 %text_backward.1 = (bf16[16,512]{1,0:T(8,128)(2,1)}, bf16[16,512]{1,0:T(8,128)(2,1)}, bf16[16,2048]{1,0:T(8,128)(2,1)}, bf16[16,512]{1,0:T(8,128)(2,1)}, bf16[16...) custom-call(s32[8]{0:T(128)} %refs_0_.7, ...), custom_call_target="tpu_custom_call" | custom-call | tf_op jit(solution)/shard_map/text_backward/pallas_call | solution.py:438
  320.6 0.9 reshape.362
  321.5 0.7 slice.113
  323.5 1.0 concatenate.35
  324.5 0.8 pad.46.refs_26_
  325.2 45.9 %weight_grads.1.grads_ref = f32[104176,128]{1,0:T(8,128)} custom-call(bf16[400,3072]{1,0:T(8,128)(2,1)} %reshape.342.refs_3_.refs_0_, bf16[400,768]{1,0:T(8,128)(2,1)} %get-tuple-element.358.refs_1_, bf16[16,768]{1,0:T(8,128)(2,1)} %get-tuple-element.347.refs_6_.refs_2_, bf16[16,768]{1,0:T(8,128)(2,1)} %get-tuple-element.359.refs_3_, ...), custom_call_target="tpu_custom_call" | custom-call | tf_op jit(solution)/shard_map/weight_grads/pallas_call | solution.py:817
  371.1 128.0 %reduce_windows.1.window_ref = f32[3328,128]{1,0:T(8,128)} custom-call(f32[104176,128]{1,0:T(8,128)} %weight_grads.1.grads_ref), custom_call_target="tpu_custom_call" | custom-call | tf_op jit(solution)/shard_map/reduce_windows/pallas_call | solution.py:1368
  499.2 1.4 copy-done.2
  500.6 1.7 lift_window.1
  502.4 1.0 multiply_reduce_fusion.1
  503.5 0.8 fusion.16
  504.3 36.6 %token_grads.1 = bf16[4,8,96,512]{3,2,1,0:T(8,128)(2,1)S(1)} custom-call(bf16[8,96,512]{2,1,0:T(8,128)(2,1)S(1)} %bitcast.105), custom_call_target="tpu_custom_call" | custom-call | tf_op jit(solution)/shard_map/token_grads/pallas_call | solution.py:1009
  540.9 18.2 %table_sum.1 = (f32[6184,512]{1,0:T(8,128)}, f32[8,512]{1,0:T(8,128)}) custom-call(s32[32]{0:T(128)S(1)} %broadcast_minimum_fusion.counts_ref, s32[3072]{0:T(1024)S(1)} %add.304.index_ref, bf16[32,96,512]{2,1,0:T(8,128)(2,1)S(1)} %bitcast.102), custom_call_target="tpu_custom_call" | custom-call | tf_op jit(solution)/shard_map/table_sum/pallas_call | solution.py:1080
  559.1 0.9 slice.115
  560.0 1.4 conditional.1
  560.0 1.4 reduce_sum.159
  562.7 13.5 %squares.1 = f32[32,8,128]{2,1,0:T(8,128)S(1)} custom-call(f32[8,128]{1,0:T(8,128)S(1)} %broadcast_in_dim.224.refs_0_), custom_call_target="tpu_custom_call" | custom-call | tf_op jit(solution)/shard_map/squares/pallas_call | solution.py:886
  576.2 0.6 slice_reduce_fusion
  577.6 5.3 multiply_subtract_fusion.1
  582.9 32.1 %multiply_subtract_fusion = (f32[6176,512]{1,0:T(8,128)}, f32[6176,512]{1,0:T(8,128)}, f32[6176,512]{1,0:T(8,128)}) fusion(f32[6176,512]{1,0:T(8,128)} %param.22, f32[]{:T(128)S(6)} %min_shard_map.3, f32[6184,512]{1,0:T(8,128)} %get-tuple-element.393, f32[6176,512]{1,0:T(8,128)} %param.23, f32[6176,512]{1,0:T(8,128)} %param.24), kind=kLoop, calls=%fused_computation.32 | loop fusion | flops 50593792 | bytes 88539136 | tf_op jit(solution)/shard_map/sub | solution.py:488
  (91 shorter events, 3.6 us)
Async XLA Ops:
  10.9 1.9 copy-start.14
  10.9 2.3 copy-start.12
  11.0 2.3 copy-start.13
  175.8 1.3 copy-start
  177.1 1.3 copy-start.1
  178.5 0.9 copy-start.3
  179.3 0.8 copy-start.4
  215.9 10.8 %copy-start.15 = (s32[616]{0:T(1024)}, s32[616]{0:T(1024)S(1)}, u32[]{:S(2)}) copy-start(s32[616]{0:T(1024)S(1)} %get-tuple-element.462) | copy-start | bytes 7396
  227.0 10.9 %copy-start.7 = (s32[616]{0:T(1024)}, s32[616]{0:T(1024)S(1)}, u32[]{:S(2)}) copy-start(s32[616]{0:T(1024)S(1)} %get-tuple-element.665) | copy-start | bytes 7396
  256.8 22.1 %copy-start.17 = (s32[4,8]{1,0:T(4,128)S(1)}, s32[4,8]{1,0:T(4,128)}, u32[]{:S(2)}) copy-start(s32[4,8]{1,0:T(4,128)} %param.28) | copy-start | bytes 388
  256.8 22.4 %copy-start.11 = (s32[256]{0:T(256)S(1)}, s32[256]{0:T(256)}, u32[]{:S(2)}) copy-start(s32[256]{0:T(256)} %param.29) | copy-start | bytes 3076
  256.8 22.5 %copy-start.8 = (bf16[32,8,512]{2,1,0:T(8,128)(2,1)S(1)}, bf16[32,8,512]{2,1,0:T(8,128)(2,1)}, u32[]{:S(2)}) copy-start(bf16[32,8,512]{2,1,0:T(8,128)(2,1)} %get-tuple-element.341) | copy-start | bytes 786436
  305.8 14.7 %copy-start.9 = (f32[50,768]{1,0:T(8,128)S(1)}, f32[50,768]{1,0:T(8,128)}, u32[]{:S(2)}) copy-start(f32[50,768]{1,0:T(8,128)} %get-tuple-element.385) | copy-start | bytes 460804
  305.8 14.8 %copy-start.10 = (f32[8,768]{1,0:T(8,128)S(1)}, f32[8,768]{1,0:T(8,128)}, u32[]{:S(2)}) copy-start(f32[8,768]{1,0:T(8,128)} %get-tuple-element.386) | copy-start | bytes 73732
  499.2 1.5 copy-start.2
  500.6 2.8 copy-start.18
  500.6 2.9 copy-start.6
  500.6 2.9 copy-start.16
  560.0 17.6 %copy-start.5 = (f32[416441]{0:T(1024)S(1)}, f32[416441]{0:T(1024)}, u32[]{:S(2)}) copy-start(f32[416441]{0:T(1024)} %param.19) | copy-start | bytes 4997296

commit v3 on v2

--- a/solution.py
+++ b/solution.py
@@ -694,16 +694,22 @@
     copy_out(len(steps) - 1).wait()
 
 
-def spread_entry(shard, count, vec_rows, gathered_ref, *refs):
-    outs = refs[:10]
-    landed, edges, wide_rows, ready_a, ready_b, ready_c, ready_d, in_sem, out_sem = refs[10:]
+def spread_entry(shard, gx_size, gy_size, vec_rows, gathered_ref, rows_ref, *refs):
+    outs, landed_rows = refs[:10], refs[10]
+    landed, edges, wide_rows, ready_a, ready_b, ready_c, ready_d, in_sem, out_sem = refs[11:20]
     ready = {D_IMG: ready_a, 4 * D_IMG: ready_b, D_TXT: ready_c, 4 * D_TXT: ready_d}
+    share = Share(gx_size, gy_size, False, rows_ref, landed_rows, refs[20:])
+    share.greet()
+    share.begin()
     spread_kernel(
-        shard, count, vec_rows, gathered_ref, *outs, landed, edges, wide_rows, ready, in_sem, out_sem
-    )
-
-
-def spread_weights(gathered, shard, count):
+        shard, gx_size * gy_size, vec_rows, gathered_ref, *outs, landed, edges, wide_rows, ready, in_sem, out_sem
+    )
+    share.middle()
+    share.finish()
+
+
+def spread_weights(gathered, rows_to_send, shard, gx_size, gy_size, number):
+    count = gx_size * gy_size
     rows = gathered.shape[0] // count
     steps = spread_steps()
     tallest = {}
@@ -720,24 +726,30 @@
         for cols in (D_IMG, 4 * D_IMG, D_TXT, 4 * D_TXT)
     ]
     return pl.pallas_call(
-        functools.partial(spread_entry, shard, count, vec_rows),
+        functools.partial(spread_entry, shard, gx_size, gy_size, vec_rows),
         out_shape=[
             jax.ShapeDtypeStruct((seg_rows, seg_cols), jnp.bfloat16)
             for seg_name, seg_rows, seg_cols in segment_list()[:9]
         ]
-        + [jax.ShapeDtypeStruct((vec_rows, LANES), jnp.float32)],
-        in_specs=[pl.BlockSpec(memory_space=pl.ANY)],
-        out_specs=[pl.BlockSpec(memory_space=pl.ANY)] * 10,
+        + [
+            jax.ShapeDtypeStruct((vec_rows, LANES), jnp.float32),
+            jax.ShapeDtypeStruct((1,) + rows_to_send.shape, rows_to_send.dtype),
+        ],
+        in_specs=[pl.BlockSpec(memory_space=pl.ANY), pl.BlockSpec(memory_space=pltpu.VMEM)],
+        out_specs=[pl.BlockSpec(memory_space=pl.ANY)] * 10 + [pl.BlockSpec(memory_space=pltpu.VMEM)],
         scratch_shapes=[
             pltpu.VMEM((2, most, LANES), jnp.bfloat16),
             pltpu.VMEM((2, edge_count + 1, GROUP, LANES), jnp.bfloat16),
             pltpu.VMEM((most, LANES), jnp.float32),
         ]
         + ready
-        + [pltpu.SemaphoreType.DMA((2,)), pltpu.SemaphoreType.DMA((2,))],
-        compiler_params=pltpu.CompilerParams(vmem_limit_bytes=48 << 20),
+        + [pltpu.SemaphoreType.DMA((2,)), pltpu.SemaphoreType.DMA((2,))]
+        + share_sems(gx_size, gy_size),
+        compiler_params=pltpu.CompilerParams(
+            collective_id=number, has_side_effects=True, vmem_limit_bytes=48 << 20
+        ),
         name="spread_weights",
-    )(gathered)
+    )(gathered, rows_to_send)
 
 
 def split_vectors(vec_rows):
@@ -747,15 +759,22 @@
     return image_vec, text_vec, vec_rows[image_count + text_count, 0]
 
 
-def grads_kernel(parts, total_rows, *refs):
+def grads_kernel(parts, gx_size, gy_size, *refs):
     operand_count = sum(2 * len(pairs) for seg_rows, seg_cols, take, pairs in parts)
     operands = refs[:operand_count]
-    vec_ref, out_ref, flat_rows, vec_sem, out_sem = refs[operand_count:]
+    vec_ref, token_ref, out_ref, arrived_ref, flat_rows, vec_sem, out_sem = refs[operand_count : operand_count + 7]
+    share = Share(gx_size, gy_size, True, token_ref, arrived_ref, refs[operand_count + 7 :])
+    share.greet()
+    share.begin()
     tail = pltpu.make_async_copy(vec_ref, out_ref.at[pl.ds(matrix_rows(), vec_ref.shape[0])], vec_sem)
     tail.start()
     base = 0
     steps_before = 0
-    for seg_rows, seg_cols, take, pairs in parts:
+    for number, (seg_rows, seg_cols, take, pairs) in enumerate(parts):
+        if number == 2:
+            share.middle()
+        if number == 6:
+            share.rest()
         wide = seg_cols // LANES
         size = take * wide
         count = seg_rows // take
@@ -799,9 +818,10 @@
         base += seg_rows * wide
         steps_before += count
     tail.wait()
-
-
-def weight_grads(pair_lists, vec_rows):
+    share.finish()
+
+
+def weight_grads(pair_lists, vec_rows, token_grads, gx_size, gy_size, number):
     operands, parts = [], []
     for (seg_name, seg_rows, seg_cols), pairs in zip(segment_list()[:9], pair_lists):
         numbered, first = [], 0
@@ -815,18 +835,24 @@
     total_rows = matrix_rows() + vec_rows.shape[0]
     most = max(take * seg_cols // LANES for seg_rows, seg_cols, take, pairs in parts)
     return pl.pallas_call(
-        functools.partial(grads_kernel, parts, total_rows),
-        out_shape=jax.ShapeDtypeStruct((total_rows, LANES), jnp.float32),
-        in_specs=[pl.BlockSpec(memory_space=pltpu.VMEM)] * (len(operands) + 1),
-        out_specs=pl.BlockSpec(memory_space=pl.ANY),
+        functools.partial(grads_kernel, parts, gx_size, gy_size),
+        out_shape=[
+            jax.ShapeDtypeStruct((total_rows, LANES), jnp.float32),
+            jax.ShapeDtypeStruct((gx_size,) + token_grads.shape, token_grads.dtype),
+        ],
+        in_specs=[pl.BlockSpec(memory_space=pltpu.VMEM)] * (len(operands) + 2),
+        out_specs=[pl.BlockSpec(memory_space=pl.ANY)] * 2,
         scratch_shapes=[
             pltpu.VMEM((2, most, LANES), jnp.float32),
             pltpu.SemaphoreType.DMA,
             pltpu.SemaphoreType.DMA((2,)),
-        ],
-        compiler_params=pltpu.CompilerParams(vmem_limit_bytes=56 << 20),
+        ]
+        + share_sems(gx_size, gy_size),
+        compiler_params=pltpu.CompilerParams(
+            collective_id=number, has_side_effects=True, vmem_limit_bytes=56 << 20
+        ),
         name="weight_grads",
-    )(*operands, vec_rows)
+    )(*operands, vec_rows, token_grads)
 
 
 def exchange_kernel(gx_size, gy_size, many, *refs):
@@ -896,6 +922,72 @@
     )(*blocks)
 
 
+class Share:
+    def __init__(self, gx_size, gy_size, everyone, send_ref, out_ref, sems):
+        gx, self.gy = lax.axis_index("gx"), lax.axis_index("gy")
+        self.x_size, self.send_ref, self.out_ref = gx_size // 2, send_ref, out_ref
+        self.core, self.x = lax.rem(gx, 2), gx // 2
+        (self.own_sem, self.row_send, self.row_recv, self.x_send, self.x_recv, self.core_send, self.core_recv) = sems
+        self.rows = [(gx, lax.rem(self.gy + d, gy_size)) for d in range(1, gy_size)]
+        self.along_x, self.sibling = [], []
+        if everyone:
+            self.along_x = [
+                (lax.rem(self.x + d, self.x_size) * 2 + self.core, self.gy) for d in range(1, self.x_size)
+            ]
+            self.sibling = [(self.x * 2 + 1 - self.core, self.gy)]
+        self.mine = out_ref.at[gx if everyone else 0]
+
+    def greet(self):
+        greet_all(self.rows + self.along_x + self.sibling)
+
+    def own(self):
+        return pltpu.make_async_copy(self.send_ref.at[self.gy], self.mine.at[self.gy], self.own_sem)
+
+    def row(self, d):
+        other = self.rows[d]
+        return remote(self.send_ref.at[other[1]], self.mine.at[self.gy], self.row_send.at[d], self.row_recv.at[d], other)
+
+    def group(self, d):
+        return remote(self.mine, self.mine, self.x_send.at[d], self.x_recv.at[d], self.along_x[d])
+
+    def across(self, i, source):
+        return remote(source, source, self.core_send.at[i], self.core_recv.at[i], self.sibling[0])
+
+    def begin(self):
+        self.own().start()
+        for d in range(len(self.rows)):
+            self.row(d).start()
+
+    def middle(self):
+        self.own().wait()
+        for d in range(len(self.rows)):
+            self.row(d).wait_recv()
+        for d in range(len(self.along_x)):
+            self.group(d).start()
+        if self.sibling:
+            self.across(0, self.mine).start()
+
+    def rest(self):
+        for d in range(len(self.along_x)):
+            self.group(d).wait_recv()
+            sender = lax.rem(self.x + self.x_size - d - 1, self.x_size) * 2 + self.core
+            self.across(d + 1, self.out_ref.at[sender]).start()
+
+    def finish(self):
+        for d in range(len(self.rows)):
+            self.row(d).wait_send()
+        for d in range(len(self.along_x)):
+            self.group(d).wait_send()
+        for i in range(self.x_size if self.sibling else 0):
+            self.across(i, self.mine).wait_send()
+            self.across(i, self.mine).wait_recv()
+
+
+def share_sems(gx_size, gy_size):
+    dma, x_size = pltpu.SemaphoreType.DMA, gx_size // 2
+    return [dma, dma((gy_size - 1,)), dma((gy_size - 1,)), dma((x_size,)), dma((x_size,)), dma((x_size,)), dma((x_size,))]
+
+
 class Places:
     def __init__(self, sizes):
         self.x_size, self.low_size, self.high_size = sizes
@@ -965,59 +1057,6 @@
 
 def route_capacity(tokens, gy_size):
     return GROUP * (1 + 17 * tokens // (16 * gy_size * GROUP))
-
-
-def share_kernel(gx_size, gy_size, everyone, send_ref, out_ref, own_sem, row_send, row_recv, x_send, x_recv, core_send,
-                 core_recv):
-    gx, gy = lax.axis_index("gx"), lax.axis_index("gy")
-    x_size = gx_size // 2
-    core, x = lax.rem(gx, 2), gx // 2
-    rows = [(gx, lax.rem(gy + d, gy_size)) for d in range(1, gy_size)]
-    along_x = [(lax.rem(x + d, x_size) * 2 + core, gy) for d in range(1, x_size)] if everyone else []
-    sibling = [(x * 2 + 1 - core, gy)] if everyone else []
-    greet_all(rows + along_x + sibling)
-    mine = out_ref.at[gx] if everyone else out_ref.at[0]
-    own = pltpu.make_async_copy(send_ref.at[gy], mine.at[gy], own_sem)
-    own.start()
-    for d, other in enumerate(rows):
-        remote(send_ref.at[other[1]], mine.at[gy], row_send.at[d], row_recv.at[d], other).start()
-    own.wait()
-    for d, other in enumerate(rows):
-        copy = remote(send_ref.at[other[1]], mine.at[gy], row_send.at[d], row_recv.at[d], other)
-        copy.wait_recv()
-    for d, other in enumerate(along_x):
-        remote(mine, mine, x_send.at[d], x_recv.at[d], other).start()
-    for other in sibling:
-        remote(mine, mine, core_send.at[0], core_recv.at[0], other).start()
-    for d, other in enumerate(along_x):
-        remote(mine, mine, x_send.at[d], x_recv.at[d], other).wait_recv()
-        source = out_ref.at[lax.rem(x + x_size - d - 1, x_size) * 2 + core]
-        remote(source, source, core_send.at[d + 1], core_recv.at[d + 1], sibling[0]).start()
-    for d, other in enumerate(rows):
-        remote(send_ref.at[other[1]], mine.at[gy], row_send.at[d], row_recv.at[d], other).wait_send()
-    for d, other in enumerate(along_x):
-        remote(mine, mine, x_send.at[d], x_recv.at[d], other).wait_send()
-    for i in range(x_size if everyone else 0):
-        copy = remote(mine, mine, core_send.at[i], core_recv.at[i], sibling[0])
-        copy.wait_send()
-        copy.wait_recv()
-
-
-def share_rows(rows, gx_size, gy_size, everyone, number, name):
-    groups, dma = (gx_size if everyone else 1), pltpu.SemaphoreType.DMA
-    x_size = gx_size // 2
-    return pl.pallas_call(
-        functools.partial(share_kernel, gx_size, gy_size, everyone),
-        out_shape=jax.ShapeDtypeStruct((groups,) + rows.shape, rows.dtype),
-        in_specs=[pl.BlockSpec(memory_space=pltpu.VMEM)],
-        out_specs=pl.BlockSpec(memory_space=pltpu.VMEM),
-        scratch_shapes=[dma, dma((gy_size - 1,)), dma((gy_size - 1,)), dma((x_size,)), dma((x_size,)), dma((x_size,)),
-                        dma((x_size,))],
-        compiler_params=pltpu.CompilerParams(
-            collective_id=number, has_side_effects=True, vmem_limit_bytes=48 << 20
-        ),
-        name=name,
-    )(rows)
 
 
 def table_sum_kernel(cap, counts_ref, index_ref, rows_ref, out_ref, square_ref, wide, row_sem):
@@ -1520,9 +1559,8 @@
         index = lax.dynamic_slice_in_dim(index, group_start, gy_size, 0)
         return lax.optimization_barrier(jnp.take(table, index.reshape(-1), axis=0, mode="clip")).astype(jnp.bfloat16)
 
-    landed = share_rows(
-        rows_to_send(first_rows).reshape(gy_size, cap, D_TXT), gx_size, gy_size, False, 5, "token_rows"
-    )
+    sent = rows_to_send(first_rows).reshape(gy_size, cap, D_TXT)
+    *spread, landed = spread_weights(gathered, sent, shard, gx_size, gy_size, 5)
     slot_count = gy_size * cap
     picks = pick_matrix(own_slots(0), slot_count)
     token_rows = weight_grad(picks, landed.reshape(slot_count, D_TXT)).astype(jnp.bfloat16)
@@ -1532,8 +1570,9 @@
         rows = lax.all_to_all(rows, "gy", 0, 0, tiled=True).reshape(slot_count, D_TXT)
         return found + weight_grad(pick_matrix(own_slots(turn), slot_count), rows).astype(jnp.bfloat16)
 
-    token_rows = lax.fori_loop(1, rounds, more_rows, token_rows)
-    spread = spread_weights(gathered, shard, device_count)
+    token_rows = lax.cond(
+        rounds > 1, lambda rows: lax.fori_loop(1, rounds, more_rows, rows), lambda rows: rows, token_rows
+    )
     image_weights = dict(zip(IMAGE.names, spread[:5]))
     text_weights = dict(zip(TEXT.names, spread[5:9]))
     image_vec, text_vec, temper = split_vectors(spread[9])
@@ -1582,32 +1621,9 @@
     text_grads = tower_backward(TEXT, end_pos, text_gains, grad_txt, text_kept[:14], text_weights)
     grad_rows = text_grads[6][: SEQS * CTX]
     to_holders = fwd_dot(picks, grad_rows).astype(jnp.bfloat16).reshape(gy_size, cap, D_TXT)
-    arrived = share_rows(to_holders, gx_size, gy_size, True, 6, "token_grads")
     image_grads = tower_backward(IMAGE, end_pos, image_gains, grad_img, image_kept[:14], image_weights)
     pair_lists = ([(image_rows, image_grads[6])],) + grad_pairs(image_kept, image_grads)
     pair_lists = pair_lists + grad_pairs(text_kept, text_grads)
-    table_grad, table_square = table_sum(
-        jnp.minimum(held_count, cap),
-        first_rows.reshape(-1),
-        arrived.reshape(device_count, cap, D_TXT),
-        vocab_dev,
-    )
-
-    def more_grads(turn, total):
-        rows = fwd_dot(pick_matrix(own_slots(turn), slot_count), grad_rows).astype(jnp.bfloat16)
-        rows = lax.all_to_all(rows.reshape(gy_size, cap, D_TXT), "gy", 0, 0, tiled=True)
-        rows = lax.all_gather(rows, "gx", axis=0).reshape(device_count * cap, D_TXT).astype(jnp.float32)
-        return total.at[held_rows(turn).reshape(-1)].add(rows)
-
-    table_grad, table_squares = lax.cond(
-        rounds > 1,
-        lambda total, square: (
-            lambda whole: (whole, jnp.sum(whole[:vocab_dev] * whole[:vocab_dev]))
-        )(lax.fori_loop(1, rounds, more_grads, total)),
-        lambda total, square: (total, jnp.sum(square)),
-        table_grad,
-        table_square,
-    )
     total_rows = window_start(shard, device_count - 1) + window_rows(shard, GROUP * CHUNKS)
     vec_rows = jnp.concatenate(
         [
@@ -1620,7 +1636,29 @@
         ]
     )
     vec_rows = jnp.pad(vec_rows, ((0, total_rows - matrix_rows() - vec_rows.shape[0]), (0, 0)))
-    local_grads = weight_grads(pair_lists, vec_rows)
+    local_grads, arrived = weight_grads(pair_lists, vec_rows, to_holders, gx_size, gy_size, 6)
+    table_grad, table_square = table_sum(
+        jnp.minimum(held_count, cap),
+        first_rows.reshape(-1),
+        arrived.reshape(device_count, cap, D_TXT),
+        vocab_dev,
+    )
+
+    def more_grads(turn, total):
+        rows = fwd_dot(pick_matrix(own_slots(turn), slot_count), grad_rows).astype(jnp.bfloat16)
+        rows = lax.all_to_all(rows.reshape(gy_size, cap, D_TXT), "gy", 0, 0, tiled=True)
+        rows = lax.all_gather(rows, "gx", axis=0).reshape(device_count * cap, D_TXT).astype(jnp.float32)
+        return total.at[held_rows(turn).reshape(-1)].add(rows)
+
+    table_grad, table_squares = lax.cond(
+        rounds > 1,
+        lambda total, square: (
+            lambda whole: (whole, jnp.sum(whole[:vocab_dev] * whole[:vocab_dev]))
+        )(lax.fori_loop(1, rounds, more_grads, total)),
+        lambda total, square: (total, jnp.sum(square)),
+        table_grad,
+        table_square,
+    )
     grad_window = reduce_windows(local_grads, shard, gx_size, gy_size, 1)
     grad_shard = lift_window(grad_window, shard, gy_size)
     table_squares = jnp.where(lax.axis_index("gx") == 0, table_squares, 0.0)

time: 636 us -> 589 us (0.926)
  Pallas kernels: 505 us -> 454 us
  loops' own time: 0.33 us -> 9.26 us
  other arithmetic: 56.4 us -> 49.1 us
    pallas_call x4 -> x2, Pallas kernels: 132 us -> 85.9 us  [the longest x1 49.4 us: weight_grads(): pl.pallas_call(functools.partial(grads_kernel, parts, gx_size, gy_size),...]
    another operation x1, loops' own time: 0.32 us -> 9.25 us  [body(): lax.cond(rounds > 1, lambda rows: lax.fori_loop(1, rounds, more_rows, row...]
    unnamed x1 -> x0, other arithmetic: 8.12 us -> none
where the time goes in v3:
time: 589 us; the launch traced here: 579 us
  Pallas kernels  454 us (77%)
  other arithmetic  49.1 us (8%)
  local copies, waits for them, and re-layouts  35.3 us (6%)
  between operations  24.8 us (4%)
  loops' own time  9.26 us (2%)
  matrix products  7.21 us (1%)
    pallas_call x2, Pallas kernels, gather_windows(): pl.pallas_call(functools.partial(gather_kernel, sizes, chunks), out_shape...  144 us
    pallas_call x1, Pallas kernels, reduce_windows(): pl.pallas_call(functools.partial(reduce_kernel, shard, (x_size, low_size,...  131 us
    pallas_call x1, Pallas kernels, weight_grads(): pl.pallas_call(functools.partial(grads_kernel, parts, gx_size, gy_size),...  49.4 us
    sub x2, other arithmetic, adam_step(): weight - rate * (first_hat / (jnp.sqrt(second_hat) + adam_eps) + decay *...  37.4 us
    pallas_call x1, Pallas kernels, spread_weights(): pl.pallas_call(functools.partial(spread_entry, shard, gx_size, gy_size, v...  36.5 us
    pallas_call x2, Pallas kernels, tower_backward(): pl.pallas_call(functools.partial(tower_backward_kernel, tower), out_shape...  34.4 us
    pallas_call x2, Pallas kernels, tower_forward(): pl.pallas_call(functools.partial(tower_forward_kernel, tower), out_shape=...  26.7 us
    pallas_call x1, Pallas kernels, table_sum(): pl.pallas_call(functools.partial(table_sum_kernel, cap), out_shape=[jax.S...  17.4 us

profile of v3, /device:TPU:0, one launch (start us, length us, event | category | flops | bytes accessed | tf_op | source)
XLA Modules:
  0.0 579.3 jit_solution(17775205448673647872)
XLA Ops:
  7.2 0.8 reshape.349
  8.0 0.8 eq.175
  9.3 0.5 select_reduce_fusion.3
  10.1 0.7 pad_maximum_fusion.9
  10.8 0.9 fusion.51
  11.8 1.6 pad_bitcast_fusion.flat_ref
  13.3 0.9 place_window.1
  14.3 0.6 copy-done.6
  15.0 1.4 copy.28
  16.4 2.2 pad.38.clone
  18.6 3.1 reshape.342.refs_3_.refs_0_
  21.7 130.4 %gather_weights.1.gathered_ref = bf16[107520,128]{1,0:T(8,128)(2,1)} custom-call(bf16[3360,128]{1,0:T(8,128)(2,1)S(1)} %pad_maximum_fusion.window_ref), custom_call_target="tpu_custom_call" | custom-call | tf_op jit(solution)/shard_map/gather_weights/pallas_call | solution.py:1226
  152.1 0.9 slice_convert_fusion
  153.3 0.6 convert_reduce_fusion
  153.9 0.6 reduce_max.27
  155.5 0.9 select_reduce_fusion.2
  156.6 1.1 slice.130
  157.7 0.3 reshape.355
  158.0 0.7 fusion.102
  158.8 7.3 %gather_fusion.1 = bf16[768,512]{1,0:T(8,128)(2,1)S(1)} fusion(f32[6176,512]{1,0:T(8,128)} %param.24, s32[1024]{0:T(1024)S(1)} %pad_clamp_fusion.1), kind=kCustom, calls=%fused_computation.1 | custom fusion | bytes 1575936 | tf_op jit(solution)/shard_map/jit(_take)/gather | solution.py:1560
  166.1 36.5 %spread_weights.1 = (bf16[3072,768]{1,0:T(8,128)(2,1)}, bf16[768,3072]{1,0:T(8,128)(2,1)}, bf16[768,3072]{1,0:T(8,128)(2,1)}, bf16[3072,768]{1,0:T(8,128)(2,1)},...) custom-call(bf16[107520,128]{1,0:T(8,128)(2,1)} %gather_weights.1.ga, ...), custom_call_target="tpu_custom_call" | custom-call | tf_op jit(solution)/shard_map/spread_weights/pallas_call | solution.py:728
  202.6 1.3 copy-done
  203.9 0.9 copy-done.2
  204.8 0.8 copy-done.4
  205.6 0.5 slice.99
  206.8 0.7 fusion.17
  207.5 9.2 %conditional.2 = (bf16[616,512]{1,0:T(8,128)(2,1)S(1)}) conditional(s32[]{:T(128)} %convert_element_type.109, bf16[616,512]{1,0:T(8,128)(2,1)S(1)} %fusion.17, (s32[]{:T(128)}, s32[]{:T(128)}, s32[616]{0:T(1024)S(1)}, s32[616]{0:T(1024)S(1)}, s32[32,616]{1,0:T(8,128)S(1)}, /*index=5*/s32[32,616]{1,0:T(8,128)S(1)}, f32[6176,512]{1,0:T(8,128)}, ...), branch_computations={%region_7.8_spmd, %region_8.12_spmd} | conditional | flops 494427616 | bytes 25470896 | solution.py:1573
  216.8 0.9 pad.49.refs_3_
  217.7 0.6 pad.42.refs_1_
  218.3 0.6 slice.98.refs_1_
  219.4 1.1 pad.43.refs_2_
  220.6 1.2 tile.21.refs_2_
  221.8 16.8 %image_forward.1 = (f32[400,768]{1,0:T(8,128)}, bf16[400,768]{1,0:T(8,128)(2,1)}, bf16[400,1536]{1,0:T(8,128)(2,1)}, bf16[16,768]{1,0:T(8,128)(2,1)}, bf16[16,76...) custom-call(s32[8]{0:T(128)} %refs_0_.7, ...), custom_call_target="tpu_custom_call" | custom-call | tf_op jit(solution)/shard_map/image_forward/pallas_call | solution.py:294
  238.6 0.7 convert_element_type.107
  239.3 10.0 %text_forward.1 = (f32[624,512]{1,0:T(8,128)}, bf16[624,512]{1,0:T(8,128)(2,1)}, bf16[624,1024]{1,0:T(8,128)(2,1)}, bf16[16,512]{1,0:T(8,128)(2,1)}, bf16[16,512...) custom-call(s32[8]{0:T(128)} %refs_0_.7, ...), custom_call_target="tpu_custom_call" | custom-call | tf_op jit(solution)/shard_map/text_forward/pallas_call | solution.py:294
  249.3 0.8 convert_element_type.112
  250.1 14.0 %embeddings.1 = bf16[2048,128]{1,0:T(8,128)(2,1)S(1)} custom-call(bf16[64,128]{1,0:T(8,128)(2,1)S(1)} %reshape.352.window_ref), custom_call_target="tpu_custom_call" | custom-call | tf_op jit(solution)/shard_map/embeddings/pallas_call | solution.py:1226
  264.7 0.3 convolution_multiply_fusion.1
  265.1 0.5 select_reduce_fusion.4
  265.5 0.3 exponential_reduce_fusion
  265.9 0.9 fusion.43
  269.1 1.0 convolution_add_fusion.1.refs_2_
  270.2 19.7 %image_backward.1 = (bf16[16,512]{1,0:T(8,128)(2,1)}, bf16[16,768]{1,0:T(8,128)(2,1)}, bf16[16,3072]{1,0:T(8,128)(2,1)}, bf16[16,768]{1,0:T(8,128)(2,1)}, bf16[1...) custom-call(s32[8]{0:T(128)} %refs_0_.7, ...), custom_call_target="tpu_custom_call" | custom-call | tf_op jit(solution)/shard_map/image_backward/pallas_call | solution.py:438
  289.9 0.9 multiply_reduce_fusion.2
  292.3 1.0 convolution_add_fusion.refs_2_
  293.3 14.7 %text_backward.1 = (bf16[16,512]{1,0:T(8,128)(2,1)}, bf16[16,512]{1,0:T(8,128)(2,1)}, bf16[16,2048]{1,0:T(8,128)(2,1)}, bf16[16,512]{1,0:T(8,128)(2,1)}, bf16[16...) custom-call(s32[8]{0:T(128)} %refs_0_.7, ...), custom_call_target="tpu_custom_call" | custom-call | tf_op jit(solution)/shard_map/text_backward/pallas_call | solution.py:438
  308.1 0.8 slice.113
  308.9 0.9 reshape.362
  309.9 1.0 concatenate.35
  310.9 0.8 pad.46.refs_26_
  311.6 0.9 slice.114
  312.5 1.7 fusion.16
  314.2 49.4 %weight_grads.1 = (f32[104176,128]{1,0:T(8,128)}, bf16[4,8,96,512]{3,2,1,0:T(8,128)(2,1)}) custom-call(bf16[400,3072]{1,0:T(8,128)(2,1)} %reshape.342.refs_3_.refs_0_, bf16[400,768]{1,0:T(8,128)(2,1)} %get-tuple-element.395.refs_1_, bf16[16,768]{1,0:T(8,128)(2,1)} %get-tuple-element.384.refs_6_.refs_2_, bf16[16,768]{1,0:T(8,128)(2,1)} %get-tuple-element.396.refs_3_, ...), custom_call_target="tpu_custom_call" | custom-call | tf_op jit(solution)/shard_map/weight_grads/pallas_call | solution.py:837
  363.6 131.4 %reduce_windows.1.window_ref = f32[3328,128]{1,0:T(8,128)} custom-call(f32[104176,128]{1,0:T(8,128)} %get-tuple-element.427.grads_ref), custom_call_target="tpu_custom_call" | custom-call | tf_op jit(solution)/shard_map/reduce_windows/pallas_call | solution.py:1407
  495.0 1.4 copy-done.1
  496.4 1.7 lift_window.1
  498.1 1.0 multiply_reduce_fusion.1
  499.2 17.4 %table_sum.1 = (f32[6184,512]{1,0:T(8,128)}, f32[8,512]{1,0:T(8,128)}) custom-call(s32[32]{0:T(128)S(1)} %broadcast_minimum_fusion.counts_ref, s32[3072]{0:T(1024)S(1)} %add.306.index_ref, bf16[32,96,512]{2,1,0:T(8,128)(2,1)S(1)} %bitcast.103), custom_call_target="tpu_custom_call" | custom-call | tf_op jit(solution)/shard_map/table_sum/pallas_call | solution.py:1119
  516.5 1.5 conditional.3
  516.5 1.4 reduce_sum.159
  519.3 10.8 %squares.1 = f32[32,8,128]{2,1,0:T(8,128)S(1)} custom-call(f32[8,128]{1,0:T(8,128)S(1)} %broadcast_in_dim.224.refs_0_), custom_call_target="tpu_custom_call" | custom-call | tf_op jit(solution)/shard_map/squares/pallas_call | solution.py:912
  530.1 0.6 slice_reduce_fusion
  531.4 5.3 multiply_subtract_fusion.1
  536.7 32.1 %multiply_subtract_fusion = (f32[6176,512]{1,0:T(8,128)}, f32[6176,512]{1,0:T(8,128)}, f32[6176,512]{1,0:T(8,128)}) fusion(f32[6176,512]{1,0:T(8,128)} %param.24, f32[]{:T(128)S(6)} %min_shard_map.3, f32[6184,512]{1,0:T(8,128)} %get-tuple-element.432, f32[6176,512]{1,0:T(8,128)} %param.25, f32[6176,512]{1,0:T(8,128)} %param.26), kind=kLoop, calls=%fused_computation.32 | loop fusion | flops 50593792 | bytes 88539136 | tf_op jit(solution)/shard_map/sub | solution.py:488
  (76 shorter events, 3.4 us)
Async XLA Ops:
  9.8 197.7 %copy-start.8 = (s32[616]{0:T(1024)}, s32[616]{0:T(1024)S(1)}, u32[]{:S(2)}) copy-start(s32[616]{0:T(1024)S(1)} %get-tuple-element.504) | copy-start | bytes 7396
  13.3 1.7 copy-start.6
  202.6 1.3 copy-start
  203.9 0.9 copy-start.2
  204.8 0.8 copy-start.4
  249.3 15.2 %copy-start.9 = (bf16[32,8,512]{2,1,0:T(8,128)(2,1)S(1)}, bf16[32,8,512]{2,1,0:T(8,128)(2,1)}, u32[]{:S(2)}) copy-start(bf16[32,8,512]{2,1,0:T(8,128)(2,1)} %get-tuple-element.378) | copy-start | bytes 786436
  265.1 0.8 copy-start.12
  293.3 14.7 %copy-start.10 = (f32[50,768]{1,0:T(8,128)S(1)}, f32[50,768]{1,0:T(8,128)}, u32[]{:S(2)}) copy-start(f32[50,768]{1,0:T(8,128)} %get-tuple-element.422) | copy-start | bytes 460804
  293.3 15.6 %copy-start.11 = (f32[8,768]{1,0:T(8,128)S(1)}, f32[8,768]{1,0:T(8,128)}, u32[]{:S(2)}) copy-start(f32[8,768]{1,0:T(8,128)} %get-tuple-element.423) | copy-start | bytes 73732
  308.1 3.6 copy-start.7
  494.9 1.5 copy-start.1
  496.4 2.8 copy-start.3
  516.5 14.9 %copy-start.5 = (f32[416441]{0:T(1024)S(1)}, f32[416441]{0:T(1024)}, u32[]{:S(2)}) copy-start(f32[416441]{0:T(1024)} %param.21) | copy-start | bytes 4997296

commit v4 on v3

--- a/solution.py
+++ b/solution.py
@@ -494,6 +494,10 @@
 
 def matrix_rows():
     return sum(seg_rows * seg_cols for seg_name, seg_rows, seg_cols in segment_list()[:9]) // LANES
+
+
+def parameter_count():
+    return sum(seg_rows * seg_cols for seg_name, seg_rows, seg_cols in segment_list())
 
 
 def window_rows(shard, step=GROUP):
@@ -1439,24 +1443,31 @@
     )(grads)
 
 
-def log_sums(rows, columns, column_ok, logit_scale, matches):
+def log_sums(rows, columns, column_ok, logit_scale, matches, positives):
     total, taken = rows.shape[0], min(rows.shape[0], 256)
 
     def some(args):
-        row_part, match_part = args
-        logits = logit_scale * back_dot(row_part, columns)
+        row_part, match_part, positive_part = args
+        dots = back_dot(row_part, columns)
+        logits = logit_scale * dots
         masked = jnp.where(column_ok[None, :], logits, -1e30)
         row_max = jnp.max(masked, 1, keepdims=True)
         log_total = row_max[:, 0] + jnp.log(jnp.sum(jnp.exp(masked - row_max), 1))
         gap = jnp.where(match_part > 0.0, logits[:, :total] - log_total[:, None], 0.0)
-        return log_total, -jnp.sum(gap)
+        pulled = jnp.sum(positive_part[:, None] * jnp.exp(masked - log_total[:, None]) * dots)
+        return log_total, -jnp.sum(gap), pulled - jnp.sum(match_part * dots[:, :total])
 
     if taken == total:
-        return some((rows, matches))
-    logs, parts = lax.map(
-        some, (rows.reshape(-1, taken, rows.shape[1]), matches.reshape(-1, taken, total))
-    )
-    return logs.reshape(-1), jnp.sum(parts)
+        return some((rows, matches, positives))
+    logs, parts, pulls = lax.map(
+        some,
+        (
+            rows.reshape(-1, taken, rows.shape[1]),
+            matches.reshape(-1, taken, total),
+            positives.reshape(-1, taken),
+        ),
+    )
+    return logs.reshape(-1), jnp.sum(parts), jnp.sum(pulls)
 
 
 def side_grads(row_embed, columns, column_ok, same_own, positives_own, log_own, logit_scale, total_count):
@@ -1470,8 +1481,7 @@
         positives_own[:, None] * jnp.exp(masked - log_own[:, None]) - weights_pos
     ) / total_count
     grad_dots = (logit_scale * grad_logits).astype(jnp.bfloat16)
-    grad_temper = logit_scale * jnp.sum(grad_logits * dot_vals)
-    return fwd_dot(grad_dots, columns), grad_temper
+    return fwd_dot(grad_dots, columns)
 
 
 def cross_grads(rows, own, valid_own, same_own, positives_all, logs, logit_scale, total_count):
@@ -1557,22 +1567,27 @@
 
     def rows_to_send(index):
         index = lax.dynamic_slice_in_dim(index, group_start, gy_size, 0)
-        return lax.optimization_barrier(jnp.take(table, index.reshape(-1), axis=0, mode="clip")).astype(jnp.bfloat16)
-
-    sent = rows_to_send(first_rows).reshape(gy_size, cap, D_TXT)
+        rows = jnp.take(table, index.reshape(-1), axis=0, mode="clip")
+        return rows.reshape(gy_size, cap, D_TXT)
+
+    sent = rows_to_send(first_rows).astype(jnp.bfloat16)
+    slot_count = gy_size * cap
+
+    def more_rows(turn, found):
+        rows = lax.all_to_all(rows_to_send(held_rows(turn)), "gy", 0, 0, tiled=True)
+        rows = rows.reshape(slot_count, D_TXT).astype(jnp.bfloat16)
+        return found + weight_grad(pick_matrix(own_slots(turn), slot_count), rows).astype(jnp.bfloat16)
+
+    nothing = jnp.zeros((tokens, D_TXT), jnp.bfloat16)
+    extra_rows = lax.cond(
+        rounds > 1, lambda rows: lax.fori_loop(1, rounds, more_rows, rows), lambda rows: rows, nothing
+    )
+    sent, extra_rows = lax.optimization_barrier((sent, extra_rows))
     *spread, landed = spread_weights(gathered, sent, shard, gx_size, gy_size, 5)
-    slot_count = gy_size * cap
     picks = pick_matrix(own_slots(0), slot_count)
     token_rows = weight_grad(picks, landed.reshape(slot_count, D_TXT)).astype(jnp.bfloat16)
 
-    def more_rows(turn, found):
-        rows = rows_to_send(held_rows(turn)).reshape(gy_size, cap, D_TXT)
-        rows = lax.all_to_all(rows, "gy", 0, 0, tiled=True).reshape(slot_count, D_TXT)
-        return found + weight_grad(pick_matrix(own_slots(turn), slot_count), rows).astype(jnp.bfloat16)
-
-    token_rows = lax.cond(
-        rounds > 1, lambda rows: lax.fori_loop(1, rounds, more_rows, rows), lambda rows: rows, token_rows
-    )
+    token_rows = token_rows + extra_rows
     image_weights = dict(zip(IMAGE.names, spread[:5]))
     text_weights = dict(zip(TEXT.names, spread[5:9]))
     image_vec, text_vec, temper = split_vectors(spread[9])
@@ -1603,13 +1618,18 @@
     column_ok = jnp.concatenate([valid_all, jnp.ones((cache_img.shape[0],), jnp.bool_)])
     columns_txt = jnp.concatenate([all_txt, cache_txt])
     columns_img = jnp.concatenate([all_img, cache_img])
-    log_img, loss_one = log_sums(all_img, columns_txt, column_ok, logit_scale, matches)
-    log_txt, loss_two = log_sums(all_txt, columns_img, column_ok, logit_scale, matches)
+    log_img, loss_one, pull_one = log_sums(
+        all_img, columns_txt, column_ok, logit_scale, matches, positives_all
+    )
+    log_txt, loss_two, pull_two = log_sums(
+        all_txt, columns_img, column_ok, logit_scale, matches, positives_all
+    )
+    grad_temper = logit_scale * (pull_one + pull_two) / total_count
     loss_sum = loss_one + loss_two
-    grad_img, temper_one = side_grads(
+    grad_img = side_grads(
         image_emb, columns_txt, column_ok, same_own, positives_own, own_part(log_img), logit_scale, total_count
     )
-    grad_txt, temper_two = side_grads(
+    grad_txt = side_grads(
         text_emb, columns_img, column_ok, same_own, positives_own, own_part(log_txt), logit_scale, total_count
     )
     grad_img = grad_img + cross_grads(
@@ -1632,7 +1652,6 @@
             image_grads[8].reshape(-1, LANES),
             text_grads[7].reshape(-1, LANES),
             text_grads[8][2:].reshape(-1, LANES),
-            jnp.pad((temper_one + temper_two).reshape(1, 1), ((0, 0), (0, LANES - 1))),
         ]
     )
     vec_rows = jnp.pad(vec_rows, ((0, total_rows - matrix_rows() - vec_rows.shape[0]), (0, 0)))
@@ -1660,14 +1679,15 @@
         table_square,
     )
     grad_window = reduce_windows(local_grads, shard, gx_size, gy_size, 1)
+    position = my_index * shard + jnp.arange(shard)
     grad_shard = lift_window(grad_window, shard, gy_size)
+    grad_shard = jnp.where(position == parameter_count() - 1, grad_temper, grad_shard)
     table_squares = jnp.where(lax.axis_index("gx") == 0, table_squares, 0.0)
     squares = jnp.sum(grad_shard * grad_shard) + table_squares
     (every,) = exchange_all([jnp.full((8, LANES), squares)], gx_size, gy_size, 2, "squares")
     grad_norm = jnp.sqrt(jnp.sum(every[:, 0, 0]))
     factor = jnp.minimum(1.0, clip_limit / (grad_norm + 1e-06))
     matrix_stop = matrix_rows() * LANES
-    position = my_index * shard + jnp.arange(shard)
     is_matrix = position < matrix_stop
     rates = jnp.where(is_matrix, rate_matrix, rate_vector)
     decays = jnp.where(is_matrix, decay_rate, 0.0)

time: 589 us -> 587 us (level)
    another operation x1, loops' own time: 9.25 us -> 0.15 us  [body(): lax.cond(rounds > 1, lambda rows: lax.fori_loop(1, rounds, more_rows, row...]
where the time goes in v4:
time: 587 us; the launch traced here: 577 us
  Pallas kernels  454 us (77%)
  other arithmetic  50.4 us (9%)
  local copies, waits for them, and re-layouts  34 us (6%)
  between operations  26.4 us (4%)
  matrix products  7.52 us (1%)
    pallas_call x2, Pallas kernels, gather_windows(): pl.pallas_call(functools.partial(gather_kernel, sizes, chunks), out_shape...  144 us
    pallas_call x1, Pallas kernels, reduce_windows(): pl.pallas_call(functools.partial(reduce_kernel, shard, (x_size, low_size,...  132 us
    pallas_call x1, Pallas kernels, weight_grads(): pl.pallas_call(functools.partial(grads_kernel, parts, gx_size, gy_size),...  49.3 us
    sub x2, other arithmetic, adam_step(): weight - rate * (first_hat / (jnp.sqrt(second_hat) + adam_eps) + decay *...  37.5 us
    pallas_call x1, Pallas kernels, spread_weights(): pl.pallas_call(functools.partial(spread_entry, shard, gx_size, gy_size, v...  36.5 us
    pallas_call x2, Pallas kernels, tower_backward(): pl.pallas_call(functools.partial(tower_backward_kernel, tower), out_shape...  34.7 us
    pallas_call x2, Pallas kernels, tower_forward(): pl.pallas_call(functools.partial(tower_forward_kernel, tower), out_shape=...  26.7 us
    pallas_call x1, Pallas kernels, table_sum(): pl.pallas_call(functools.partial(table_sum_kernel, cap), out_shape=[jax.S...  17.8 us

profile of v4, /device:TPU:0, one launch (start us, length us, event | category | flops | bytes accessed | tf_op | source)
XLA Modules:
  0.0 577.0 jit_solution(3148413210133243318)
XLA Ops:
  7.2 0.8 reshape.342
  8.0 0.8 eq.183
  9.3 0.5 select_reduce_fusion.3
  10.1 0.7 pad_maximum_fusion.9
  10.8 0.9 fusion.131
  11.7 1.6 pad_bitcast_fusion.flat_ref
  13.3 0.9 place_window.1
  14.3 0.6 copy-done.6
  15.0 1.4 copy.28
  16.4 2.2 pad.37.clone
  18.6 3.1 reshape.344.refs_3_.refs_0_
  21.7 130.4 %gather_weights.1.gathered_ref = bf16[107520,128]{1,0:T(8,128)(2,1)} custom-call(bf16[3360,128]{1,0:T(8,128)(2,1)S(1)} %pad_maximum_fusion.window_ref), custom_call_target="tpu_custom_call" | custom-call | tf_op jit(solution)/shard_map/gather_weights/pallas_call | solution.py:1230
  152.1 0.9 slice_convert_fusion
  153.3 0.6 convert_reduce_fusion
  153.9 0.6 reduce_max.27
  155.5 0.9 select_reduce_fusion.2
  156.6 1.1 slice.138
  158.0 0.7 fusion.135
  158.8 1.0 conditional.2
  158.8 0.9 broadcast_in_dim.194
  159.8 7.3 %gather_fusion.1 = bf16[768,512]{1,0:T(8,128)(2,1)S(1)} fusion(f32[6176,512]{1,0:T(8,128)} %param.24, s32[1024]{0:T(1024)S(1)} %pad_clamp_fusion.1), kind=kCustom, calls=%fused_computation.1 | custom fusion | bytes 1575936 | tf_op jit(solution)/shard_map/jit(_take)/gather | solution.py:1570
  167.1 36.5 %spread_weights.1 = (bf16[3072,768]{1,0:T(8,128)(2,1)}, bf16[768,3072]{1,0:T(8,128)(2,1)}, bf16[768,3072]{1,0:T(8,128)(2,1)}, bf16[3072,768]{1,0:T(8,128)(2,1)},...) custom-call(bf16[107520,128]{1,0:T(8,128)(2,1)} %gather_weights.1.ga, ...), custom_call_target="tpu_custom_call" | custom-call | tf_op jit(solution)/shard_map/spread_weights/pallas_call | solution.py:732
  203.6 0.6 slice.103
  204.9 1.8 fusion.20
  206.7 0.9 pad.40.refs_3_
  207.7 0.6 pad.38.refs_1_
  208.3 0.6 slice.105.refs_1_
  209.3 1.1 pad.39.refs_2_
  210.6 1.2 tile.21.refs_2_
  211.8 16.8 %image_forward.1 = (f32[400,768]{1,0:T(8,128)}, bf16[400,768]{1,0:T(8,128)(2,1)}, bf16[400,1536]{1,0:T(8,128)(2,1)}, bf16[16,768]{1,0:T(8,128)(2,1)}, bf16[16,76...) custom-call(s32[8]{0:T(128)} %refs_0_.7, ...), custom_call_target="tpu_custom_call" | custom-call | tf_op jit(solution)/shard_map/image_forward/pallas_call | solution.py:294
  228.5 0.7 convert_element_type.112
  229.3 10.0 %text_forward.1 = (f32[624,512]{1,0:T(8,128)}, bf16[624,512]{1,0:T(8,128)(2,1)}, bf16[624,1024]{1,0:T(8,128)(2,1)}, bf16[16,512]{1,0:T(8,128)(2,1)}, bf16[16,512...) custom-call(s32[8]{0:T(128)} %refs_0_.7, ...), custom_call_target="tpu_custom_call" | custom-call | tf_op jit(solution)/shard_map/text_forward/pallas_call | solution.py:294
  239.2 0.7 convert_element_type.114
  240.0 14.0 %embeddings.1 = bf16[2048,128]{1,0:T(8,128)(2,1)S(1)} custom-call(bf16[64,128]{1,0:T(8,128)(2,1)S(1)} %reshape.346.window_ref), custom_call_target="tpu_custom_call" | custom-call | tf_op jit(solution)/shard_map/embeddings/pallas_call | solution.py:1230
  254.3 0.3 fusion.64
  254.7 0.5 select_reduce_fusion.4
  255.2 0.3 exponential_reduce_fusion
  255.5 0.9 fusion.66
  258.4 1.1 multiply_reduce_fusion.2
  262.2 0.4 fusion.43
  262.6 1.0 convolution_add_fusion.refs_2_
  263.7 14.9 %text_backward.1 = (bf16[16,512]{1,0:T(8,128)(2,1)}, bf16[16,512]{1,0:T(8,128)(2,1)}, bf16[16,2048]{1,0:T(8,128)(2,1)}, bf16[16,512]{1,0:T(8,128)(2,1)}, bf16[16...) custom-call(s32[8]{0:T(128)} %refs_0_.7, ...), custom_call_target="tpu_custom_call" | custom-call | tf_op jit(solution)/shard_map/text_backward/pallas_call | solution.py:438
  278.7 0.4 fusion.44
  279.0 1.0 convolution_add_fusion.1.refs_2_
  280.1 19.8 %image_backward.1 = (bf16[16,512]{1,0:T(8,128)(2,1)}, bf16[16,768]{1,0:T(8,128)(2,1)}, bf16[16,3072]{1,0:T(8,128)(2,1)}, bf16[16,768]{1,0:T(8,128)(2,1)}, bf16[1...) custom-call(s32[8]{0:T(128)} %refs_0_.7, ...), custom_call_target="tpu_custom_call" | custom-call | tf_op jit(solution)/shard_map/image_backward/pallas_call | solution.py:438
  299.9 0.8 slice_reduce_fusion.1
  300.7 0.9 reshape.354
  301.7 0.7 reshape.355
  302.4 1.0 concatenate.35
  303.4 0.8 pad.41.refs_26_
  304.2 0.9 slice.122
  305.0 1.7 fusion.18
  306.7 49.3 %weight_grads.1 = (f32[104176,128]{1,0:T(8,128)}, bf16[4,8,96,512]{3,2,1,0:T(8,128)(2,1)}) custom-call(bf16[400,3072]{1,0:T(8,128)(2,1)} %reshape.344.refs_3_.refs_0_, bf16[400,768]{1,0:T(8,128)(2,1)} %get-tuple-element.389.refs_1_, bf16[16,768]{1,0:T(8,128)(2,1)} %get-tuple-element.378.refs_6_.refs_2_, bf16[16,768]{1,0:T(8,128)(2,1)} %get-tuple-element.390.refs_3_, ...), custom_call_target="tpu_custom_call" | custom-call | tf_op jit(solution)/shard_map/weight_grads/pallas_call | solution.py:841
  356.0 131.5 %reduce_windows.1.window_ref = f32[3328,128]{1,0:T(8,128)} custom-call(f32[104176,128]{1,0:T(8,128)} %get-tuple-element.421.grads_ref), custom_call_target="tpu_custom_call" | custom-call | tf_op jit(solution)/shard_map/reduce_windows/pallas_call | solution.py:1411
  487.5 1.4 copy-done.1
  489.0 1.7 lift_window.1
  490.7 1.0 multiply_reduce_fusion.1
  491.8 17.8 %table_sum.1 = (f32[6184,512]{1,0:T(8,128)}, f32[8,512]{1,0:T(8,128)}) custom-call(s32[32]{0:T(128)S(1)} %broadcast_minimum_fusion.counts_ref, s32[3072]{0:T(1024)S(1)} %add.308.index_ref, bf16[32,96,512]{2,1,0:T(8,128)(2,1)S(1)} %bitcast.102), custom_call_target="tpu_custom_call" | custom-call | tf_op jit(solution)/shard_map/table_sum/pallas_call | solution.py:1123
  509.5 6.0 %conditional.3 = (f32[6184,512]{1,0:T(8,128)}, f32[]{:T(128)}) conditional(s32[]{:T(128)} %convert_element_type.109, (f32[8,512]{1,0:T(8,128)}, f32[6184,512]{1,0:T(8,128)}) %tuple.54, (s32[]{:T(128)}, s32[32,616]{1,0:T(8,128)S(1)}, s32[32,616]{1,0:T(8,128)S(1)}, s32[616]{0:T(1024)}, s32[616]{0:T(1024)S(1)}, ...), branch_computations={%region_23.25_spmd, %region_25.31_spmd} | conditional | flops 500508384 | bytes 43863948 | solution.py:1672
  509.6 1.4 reduce_sum.175
  516.9 10.5 %squares.1 = f32[32,8,128]{2,1,0:T(8,128)S(1)} custom-call(f32[8,128]{1,0:T(8,128)S(1)} %broadcast_in_dim.239.refs_0_), custom_call_target="tpu_custom_call" | custom-call | tf_op jit(solution)/shard_map/squares/pallas_call | solution.py:916
  527.4 0.6 slice_reduce_fusion
  528.8 5.4 multiply_subtract_fusion.1
  534.1 32.1 %multiply_subtract_fusion = (f32[6176,512]{1,0:T(8,128)}, f32[6176,512]{1,0:T(8,128)}, f32[6176,512]{1,0:T(8,128)}) fusion(f32[6176,512]{1,0:T(8,128)} %param.24, f32[]{:T(128)S(6)} %min_shard_map.3, f32[6184,512]{1,0:T(8,128)} %get-tuple-element.426, f32[6176,512]{1,0:T(8,128)} %param.25, f32[6176,512]{1,0:T(8,128)} %param.26), kind=kLoop, calls=%fused_computation.32 | loop fusion | flops 50593792 | bytes 88539136 | tf_op jit(solution)/shard_map/sub | solution.py:488
  (75 shorter events, 3.1 us)
Async XLA Ops:
  9.8 148.9 %copy-start.9 = (s32[616]{0:T(1024)}, s32[616]{0:T(1024)S(1)}, u32[]{:S(2)}) copy-start(s32[616]{0:T(1024)S(1)} %get-tuple-element.500) | copy-start | bytes 7396
  13.3 1.7 copy-start.6
  203.6 4.0 copy-start
  203.6 4.0 copy-start.2
  203.6 4.0 copy-start.4
  240.0 14.7 %copy-start.7 = (bf16[32,8,512]{2,1,0:T(8,128)(2,1)S(1)}, bf16[32,8,512]{2,1,0:T(8,128)(2,1)}, u32[]{:S(2)}) copy-start(bf16[32,8,512]{2,1,0:T(8,128)(2,1)} %get-tuple-element.374) | copy-start | bytes 786436
  254.7 0.8 copy-start.11
  280.1 21.5 %copy-start.12 = (f32[8,512]{1,0:T(8,128)S(1)}, f32[8,512]{1,0:T(8,128)}, u32[]{:S(2)}) copy-start(f32[8,512]{1,0:T(8,128)} %get-tuple-element.419) | copy-start | bytes 49156
  280.1 22.3 %copy-start.10 = (f32[77,512]{1,0:T(8,128)S(1)}, f32[77,512]{1,0:T(8,128)}, u32[]{:S(2)}) copy-start(f32[77,512]{1,0:T(8,128)} %get-tuple-element.418) | copy-start | bytes 473092
  299.9 4.3 copy-start.8
  487.5 1.5 copy-start.1
  489.0 2.8 copy-start.3
  509.5 19.2 %copy-start.5 = (f32[416441]{0:T(1024)S(1)}, f32[416441]{0:T(1024)}, u32[]{:S(2)}) copy-start(f32[416441]{0:T(1024)} %param.21) | copy-start | bytes 4997296

commit v5 on v4

--- a/solution.py
+++ b/solution.py
@@ -624,7 +624,7 @@
     return pieces, shared
 
 
-def spread_kernel(shard, count, vec_rows, gathered_ref, *refs):
+def spread_kernel(shard, count, vec_rows, share, gathered_ref, *refs):
     outs, vec_ref = refs[:9], refs[9]
     landed, edges, wide_rows, ready, in_sem, out_sem = refs[10:]
     rows = gathered_ref.shape[0] // count
@@ -661,6 +661,9 @@
     for copy in copies_in(0)[0]:
         copy.start()
     for number, (seg, start, take, cols, base) in enumerate(steps):
+        if number == 4:
+            share.greet()
+            share.begin()
         slot = number % 2
         wide = cols // LANES
         total = take * wide
@@ -703,10 +706,8 @@
     landed, edges, wide_rows, ready_a, ready_b, ready_c, ready_d, in_sem, out_sem = refs[11:20]
     ready = {D_IMG: ready_a, 4 * D_IMG: ready_b, D_TXT: ready_c, 4 * D_TXT: ready_d}
     share = Share(gx_size, gy_size, False, rows_ref, landed_rows, refs[20:])
-    share.greet()
-    share.begin()
     spread_kernel(
-        shard, gx_size * gy_size, vec_rows, gathered_ref, *outs, landed, edges, wide_rows, ready, in_sem, out_sem
+        shard, gx_size * gy_size, vec_rows, share, gathered_ref, *outs, landed, edges, wide_rows, ready, in_sem, out_sem
     )
     share.middle()
     share.finish()
@@ -859,73 +860,6 @@
     )(*operands, vec_rows, token_grads)
 
 
-def exchange_kernel(gx_size, gy_size, many, *refs):
-    blocks, outs = refs[:many], refs[many : 2 * many]
-    send_sem, recv_sem, own_sem = refs[2 * many :]
-    count = gx_size * gy_size
-    me = linear_index(gy_size)
-    barrier = pltpu.get_barrier_semaphore()
-
-    def device(step):
-        other = lax.rem(me + step, count)
-        return (other // gy_size, lax.rem(other, gy_size))
-
-    def greet(step, carry):
-        pl.semaphore_signal(barrier, inc=1, device_id=device(step), device_id_type=MESH)
-        return carry
-
-    lax.fori_loop(1, count, greet, 0)
-    own = [
-        pltpu.make_async_copy(block, out.at[me], own_sem.at[i])
-        for i, (block, out) in enumerate(zip(blocks, outs))
-    ]
-    for copy in own:
-        copy.start()
-    pl.semaphore_wait(barrier, count - 1)
-
-    def send(step, carry):
-        for i, (block, out) in enumerate(zip(blocks, outs)):
-            pltpu.make_async_remote_copy(
-                src_ref=block,
-                dst_ref=out.at[me],
-                send_sem=send_sem.at[i],
-                recv_sem=recv_sem.at[i],
-                device_id=device(step),
-                device_id_type=MESH,
-            ).start()
-        return carry
-
-    lax.fori_loop(1, count, send, 0)
-    for i, out in enumerate(outs):
-        own[i].wait()
-        others = out.at[pl.ds(0, count - 1)]
-        both = pltpu.make_async_remote_copy(
-            src_ref=others,
-            dst_ref=others,
-            send_sem=send_sem.at[i],
-            recv_sem=recv_sem.at[i],
-            device_id=device(1),
-            device_id_type=MESH,
-        )
-        both.wait_send()
-        both.wait_recv()
-
-
-def exchange_all(blocks, gx_size, gy_size, number, name):
-    count, many = gx_size * gy_size, len(blocks)
-    return pl.pallas_call(
-        functools.partial(exchange_kernel, gx_size, gy_size, many),
-        out_shape=[jax.ShapeDtypeStruct((count,) + block.shape, block.dtype) for block in blocks],
-        in_specs=[pl.BlockSpec(memory_space=pltpu.VMEM)] * many,
-        out_specs=[pl.BlockSpec(memory_space=pltpu.VMEM)] * many,
-        scratch_shapes=[pltpu.SemaphoreType.DMA((many,))] * 3,
-        compiler_params=pltpu.CompilerParams(
-            collective_id=number, has_side_effects=True, vmem_limit_bytes=32 << 20
-        ),
-        name=name,
-    )(*blocks)
-
-
 class Share:
     def __init__(self, gx_size, gy_size, everyone, send_ref, out_ref, sems):
         gx, self.gy = lax.axis_index("gx"), lax.axis_index("gy")
@@ -1241,8 +1175,8 @@
     )(window)
 
 
-def reduce_kernel(shard, sizes, grads_ref, out_ref, own, landed, keep_one, send_one, recv_one, keep_two, send_two,
-                  recv_two, keep_three, send_three, recv_three, load_sem, pair_send, pair_recv, credit,
+def reduce_kernel(shard, sizes, grads_ref, square_ref, out_ref, squares_ref, own, landed, keep_one, send_one, recv_one, keep_two, send_two,
+                  recv_two, keep_three, send_three, recv_three, partial, square_send, square_recv, load_sem, pair_send, pair_recv, credit,
                   one_send, one_recv, two_send, two_recv, three_send, three_recv):
     at = Places(sizes)
     a_size, b_size, high_size = at.a_size, at.b_size, at.high_size
@@ -1256,7 +1190,25 @@
         return window_start(shard, at.linear(side, a, rest // high_size, lax.rem(rest, high_size)))
 
     sibling, peers, peers_two, peers_three = at.sibling(), at.along_a(), at.along_b(), at.along_h()
-    greet_all([sibling] + peers + peers_two + peers_three)
+    count = squares_ref.shape[0]
+    me = linear_index(at.gy_size)
+
+    def device(step):
+        other = lax.rem(me + step, count)
+        return (other // at.gy_size, lax.rem(other, at.gy_size))
+
+    barrier = pltpu.get_barrier_semaphore()
+
+    def greet(step, carry):
+        pl.semaphore_signal(barrier, inc=1, device_id=device(step), device_id_type=MESH)
+        return carry
+
+    lax.fori_loop(1, count, greet, 0)
+    pl.semaphore_wait(barrier, count - 1)
+    table_part = square_ref[...]
+    partial[...] = sum(table_part[:, j * LANES : (j + 1) * LANES] for j in range(D_TXT // LANES))
+    spot = (lax.broadcasted_iota(jnp.int32, (chunk, LANES), 0) * LANES
+            + lax.broadcasted_iota(jnp.int32, (chunk, LANES), 1))
     blocks = a_size * plane
 
     def pair_stage(t):
@@ -1376,6 +1328,9 @@
                    three_recv.at[u, d - 1], peers_three[d - 1]).wait_recv()
             value = value + recv_three[u, d - 1].astype(jnp.float32)
         out_ref[pl.ds(pl.multiple_of(u * chunk, GROUP), chunk), :] = value
+        place = spot + (window_start(shard, me) + u * chunk) * LANES - me * shard
+        square = jnp.where((place >= 0) & (place < shard), value * value, 0.0)
+        partial[...] += sum(square[r : r + 8] for r in range(0, chunk, 8))
 
     def turn(t, carry):
         stages = (pair_stage, first_stage, second_stage, third_stage, last_stage)
@@ -1387,6 +1342,17 @@
         return carry
 
     lax.fori_loop(0, chunks + 4, turn, 0)
+    squares_ref[me] = partial[...]
+
+    def send(step, carry):
+        remote(partial, squares_ref.at[me], square_send, square_recv, device(step)).start()
+        return carry
+
+    lax.fori_loop(1, count, send, 0)
+    others = squares_ref.at[pl.ds(0, count - 1)]
+    both = remote(others, others, square_send, square_recv, device(1))
+    both.wait_send()
+    both.wait_recv()
     for u in range(max(chunks - 2, 0), chunks):
         slot = u % 2
         for d in range(1, a_size):
@@ -1400,7 +1366,7 @@
                    three_recv.at[u, d - 1], peers_three[d - 1]).wait_send()
 
 
-def reduce_windows(grads, shard, gx_size, gy_size, number):
+def reduce_windows(grads, square, shard, gx_size, gy_size, number):
     rows = window_rows(shard, GROUP * CHUNKS)
     chunk = rows // CHUNKS
     x_size, low_size, high_size = axis_sizes(gx_size, gy_size)
@@ -1410,9 +1376,12 @@
     a, b, h = x_size - 1, low_size - 1, high_size - 1
     return pl.pallas_call(
         functools.partial(reduce_kernel, shard, (x_size, low_size, high_size)),
-        out_shape=jax.ShapeDtypeStruct((rows, LANES), jnp.float32),
-        in_specs=[pl.BlockSpec(memory_space=pl.ANY)],
-        out_specs=pl.BlockSpec(memory_space=pltpu.VMEM),
+        out_shape=[
+            jax.ShapeDtypeStruct((rows, LANES), jnp.float32),
+            jax.ShapeDtypeStruct((gx_size * gy_size, 8, LANES), jnp.float32),
+        ],
+        in_specs=[pl.BlockSpec(memory_space=pl.ANY), pl.BlockSpec(memory_space=pltpu.VMEM)],
+        out_specs=[pl.BlockSpec(memory_space=pltpu.VMEM)] * 2,
         scratch_shapes=[
             pltpu.VMEM((2, blocks, chunk, LANES), jnp.float32),
             pltpu.VMEM((2, blocks, chunk, LANES), jnp.float32),
@@ -1425,6 +1394,9 @@
             pltpu.VMEM((2, chunk, LANES), jnp.float32),
             pltpu.VMEM((2, h, chunk, LANES), low_type),
             pltpu.VMEM((CHUNKS, h, chunk, LANES), low_type),
+            pltpu.VMEM((8, LANES), jnp.float32),
+            dma,
+            dma,
             dma((2,)),
             dma((2,)),
             dma((2,)),
@@ -1440,7 +1412,7 @@
             collective_id=number, has_side_effects=True, vmem_limit_bytes=60 << 20
         ),
         name="reduce_windows",
-    )(grads)
+    )(grads, square)
 
 
 def log_sums(rows, columns, column_ok, logit_scale, matches, positives):
@@ -1669,23 +1641,23 @@
         rows = lax.all_gather(rows, "gx", axis=0).reshape(device_count * cap, D_TXT).astype(jnp.float32)
         return total.at[held_rows(turn).reshape(-1)].add(rows)
 
-    table_grad, table_squares = lax.cond(
-        rounds > 1,
-        lambda total, square: (
-            lambda whole: (whole, jnp.sum(whole[:vocab_dev] * whole[:vocab_dev]))
-        )(lax.fori_loop(1, rounds, more_grads, total)),
-        lambda total, square: (total, jnp.sum(square)),
-        table_grad,
-        table_square,
-    )
-    grad_window = reduce_windows(local_grads, shard, gx_size, gy_size, 1)
+    def whole_squares(total):
+        return jnp.sum((total[:vocab_dev] * total[:vocab_dev]).reshape(-1, 8, D_TXT), 0)
+
+    def more_turns(total, square):
+        total = lax.fori_loop(1, rounds, more_grads, total)
+        return total, whole_squares(total)
+
+    table_grad, table_square = lax.cond(
+        rounds > 1, more_turns, lambda total, square: (total, square), table_grad, table_square
+    )
+    table_square = jnp.where(lax.axis_index("gx") == 0, table_square, 0.0)
+    grad_window, every = reduce_windows(local_grads, table_square, shard, gx_size, gy_size, 1)
     position = my_index * shard + jnp.arange(shard)
     grad_shard = lift_window(grad_window, shard, gy_size)
     grad_shard = jnp.where(position == parameter_count() - 1, grad_temper, grad_shard)
-    table_squares = jnp.where(lax.axis_index("gx") == 0, table_squares, 0.0)
-    squares = jnp.sum(grad_shard * grad_shard) + table_squares
-    (every,) = exchange_all([jnp.full((8, LANES), squares)], gx_size, gy_size, 2, "squares")
-    grad_norm = jnp.sqrt(jnp.sum(every[:, 0, 0]))
+    total_square = jnp.sum(every) + grad_temper * grad_temper
+    grad_norm = jnp.sqrt(total_square)
     factor = jnp.minimum(1.0, clip_limit / (grad_norm + 1e-06))
     matrix_stop = matrix_rows() * LANES
     is_matrix = position < matrix_stop

time: 587 us -> 578 us (0.985)
    pallas_call x1 -> x0, Pallas kernels: 10.5 us -> none  [exchange_all(): pl.pallas_call(functools.partial(exchange_kernel, gx_size, gy_size, many)...]
    pallas_call x1, Pallas kernels: 132 us -> 141 us  [reduce_windows(): pl.pallas_call(functools.partial(reduce_kernel, shard, (x_size, low_size,...]
where the time goes in v5:
time: 578 us; the launch traced here: 568 us
  Pallas kernels  452 us (78%)
  other arithmetic  47.5 us (8%)
  local copies, waits for them, and re-layouts  36.6 us (6%)
  between operations  24.9 us (4%)
  matrix products  7.52 us (1%)
    pallas_call x2, Pallas kernels, gather_windows(): pl.pallas_call(functools.partial(gather_kernel, sizes, chunks), out_shape...  144 us
    pallas_call x1, Pallas kernels, reduce_windows(): pl.pallas_call(functools.partial(reduce_kernel, shard, (x_size, low_size,...  141 us
    pallas_call x1, Pallas kernels, weight_grads(): pl.pallas_call(functools.partial(grads_kernel, parts, gx_size, gy_size),...  49.3 us
    pallas_call x1, Pallas kernels, spread_weights(): pl.pallas_call(functools.partial(spread_entry, shard, gx_size, gy_size, v...  36 us
    sub x2, other arithmetic, adam_step(): weight - rate * (first_hat / (jnp.sqrt(second_hat) + adam_eps) + decay *...  35.6 us
    pallas_call x2, Pallas kernels, tower_backward(): pl.pallas_call(functools.partial(tower_backward_kernel, tower), out_shape...  34.7 us
    pallas_call x2, Pallas kernels, tower_forward(): pl.pallas_call(functools.partial(tower_forward_kernel, tower), out_shape=...  26.7 us
    pallas_call x1, Pallas kernels, table_sum(): pl.pallas_call(functools.partial(table_sum_kernel, cap), out_shape=[jax.S...  17.1 us

profile of v5, /device:TPU:0, one launch (start us, length us, event | category | flops | bytes accessed | tf_op | source)
XLA Modules:
  0.0 568.4 jit_solution(8994953653478285680)
XLA Ops:
  7.2 0.8 reshape.345
  8.0 0.8 eq.183
  8.7 0.3 fusion.18
  9.3 0.5 select_reduce_fusion.3
  10.1 0.7 pad_maximum_fusion.9
  10.8 0.9 fusion.132
  11.7 1.6 pad_bitcast_fusion.flat_ref
  13.3 0.9 place_window.1
  14.3 0.6 copy-done.6
  15.0 1.4 copy.28
  16.3 2.2 pad.37.clone
  18.6 3.1 reshape.347.refs_3_.refs_0_
  21.7 130.4 %gather_weights.1.gathered_ref = bf16[107520,128]{1,0:T(8,128)(2,1)} custom-call(bf16[3360,128]{1,0:T(8,128)(2,1)S(1)} %pad_maximum_fusion.window_ref), custom_call_target="tpu_custom_call" | custom-call | tf_op jit(solution)/shard_map/gather_weights/pallas_call | solution.py:1164
  152.1 0.9 slice_convert_fusion
  153.3 0.6 convert_reduce_fusion
  153.9 0.6 reduce_max.27
  155.5 1.0 select_reduce_fusion.2
  156.6 1.1 slice.140
  157.7 0.3 reshape.353
  158.1 1.0 conditional.2
  158.1 0.9 broadcast_in_dim.195
  159.1 7.3 %gather_fusion.1 = bf16[768,512]{1,0:T(8,128)(2,1)S(1)} fusion(f32[6176,512]{1,0:T(8,128)} %param.24, s32[1024]{0:T(1024)S(1)} %pad_clamp_fusion.1), kind=kCustom, calls=%fused_computation.1 | custom fusion | bytes 1575936 | tf_op jit(solution)/shard_map/jit(_take)/gather | solution.py:1542
  166.4 36.0 %spread_weights.1 = (bf16[3072,768]{1,0:T(8,128)(2,1)}, bf16[768,3072]{1,0:T(8,128)(2,1)}, bf16[768,3072]{1,0:T(8,128)(2,1)}, bf16[3072,768]{1,0:T(8,128)(2,1)},...) custom-call(bf16[107520,128]{1,0:T(8,128)(2,1)} %gather_weights.1.ga, ...), custom_call_target="tpu_custom_call" | custom-call | tf_op jit(solution)/shard_map/spread_weights/pallas_call | solution.py:733
  202.4 0.6 slice.103
  203.7 1.8 fusion.21
  205.5 0.9 pad.40.refs_3_
  206.4 0.6 pad.38.refs_1_
  207.0 0.6 slice.105.refs_1_
  207.9 1.2 tile.24
  209.1 2.4 pad.39.refs_2_
  211.7 1.2 tile.21.refs_2_
  212.8 16.8 %image_forward.1 = (f32[400,768]{1,0:T(8,128)}, bf16[400,768]{1,0:T(8,128)(2,1)}, bf16[400,1536]{1,0:T(8,128)(2,1)}, bf16[16,768]{1,0:T(8,128)(2,1)}, bf16[16,76...) custom-call(s32[8]{0:T(128)} %refs_0_.7, ...), custom_call_target="tpu_custom_call" | custom-call | tf_op jit(solution)/shard_map/image_forward/pallas_call | solution.py:294
  229.6 0.7 convert_element_type.112
  230.3 10.0 %text_forward.1 = (f32[624,512]{1,0:T(8,128)}, bf16[624,512]{1,0:T(8,128)(2,1)}, bf16[624,1024]{1,0:T(8,128)(2,1)}, bf16[16,512]{1,0:T(8,128)(2,1)}, bf16[16,512...) custom-call(s32[8]{0:T(128)} %refs_0_.7, ...), custom_call_target="tpu_custom_call" | custom-call | tf_op jit(solution)/shard_map/text_forward/pallas_call | solution.py:294
  240.3 0.7 convert_element_type.114
  241.1 14.0 %embeddings.1 = bf16[2048,128]{1,0:T(8,128)(2,1)S(1)} custom-call(bf16[64,128]{1,0:T(8,128)(2,1)S(1)} %reshape.349.window_ref), custom_call_target="tpu_custom_call" | custom-call | tf_op jit(solution)/shard_map/embeddings/pallas_call | solution.py:1164
  255.0 0.3 reshape.350
  255.4 0.3 fusion.65
  255.8 0.5 select_reduce_fusion.4
  256.2 0.4 exponential_reduce_fusion
  256.6 0.9 fusion.67
  259.3 1.1 multiply_reduce_fusion
  263.0 0.4 fusion.44
  263.4 1.0 convolution_add_fusion.refs_2_
  264.4 14.9 %text_backward.1 = (bf16[16,512]{1,0:T(8,128)(2,1)}, bf16[16,512]{1,0:T(8,128)(2,1)}, bf16[16,2048]{1,0:T(8,128)(2,1)}, bf16[16,512]{1,0:T(8,128)(2,1)}, bf16[16...) custom-call(s32[8]{0:T(128)} %refs_0_.7, ...), custom_call_target="tpu_custom_call" | custom-call | tf_op jit(solution)/shard_map/text_backward/pallas_call | solution.py:438
  279.4 0.4 fusion.45
  279.8 1.0 convolution_add_fusion.1.refs_2_
  280.9 19.8 %image_backward.1 = (bf16[16,512]{1,0:T(8,128)(2,1)}, bf16[16,768]{1,0:T(8,128)(2,1)}, bf16[16,3072]{1,0:T(8,128)(2,1)}, bf16[16,768]{1,0:T(8,128)(2,1)}, bf16[1...) custom-call(s32[8]{0:T(128)} %refs_0_.7, ...), custom_call_target="tpu_custom_call" | custom-call | tf_op jit(solution)/shard_map/image_backward/pallas_call | solution.py:438
  300.6 0.8 slice_reduce_fusion
  301.5 0.9 reshape.357
  302.4 0.7 reshape.358
  303.2 1.0 concatenate.35
  304.2 0.8 pad.41.refs_26_
  305.0 1.7 fusion.19
  306.7 49.3 %weight_grads.1 = (f32[104176,128]{1,0:T(8,128)}, bf16[4,8,96,512]{3,2,1,0:T(8,128)(2,1)}) custom-call(bf16[400,3072]{1,0:T(8,128)(2,1)} %reshape.347.refs_3_.refs_0_, bf16[400,768]{1,0:T(8,128)(2,1)} %get-tuple-element.394.refs_1_, bf16[16,768]{1,0:T(8,128)(2,1)} %get-tuple-element.383.refs_6_.refs_2_, bf16[16,768]{1,0:T(8,128)(2,1)} %get-tuple-element.395.refs_3_, ...), custom_call_target="tpu_custom_call" | custom-call | tf_op jit(solution)/shard_map/weight_grads/pallas_call | solution.py:842
  356.0 1.9 copy-done.2
  357.9 17.1 %table_sum.1 = (f32[6184,512]{1,0:T(8,128)}, f32[8,512]{1,0:T(8,128)S(1)}) custom-call(s32[32]{0:T(128)S(1)} %broadcast_minimum_fusion.counts_ref, s32[3072]{0:T(1024)S(1)} %add.308.index_ref, bf16[32,96,512]{2,1,0:T(8,128)(2,1)S(1)} %bitcast.103), custom_call_target="tpu_custom_call" | custom-call | tf_op jit(solution)/shard_map/table_sum/pallas_call | solution.py:1057
  375.2 0.6 broadcast_select_fusion.square_ref
  375.9 140.8 %reduce_windows.1 = (f32[3328,128]{1,0:T(8,128)}, f32[32,8,128]{2,1,0:T(8,128)}) custom-call(f32[104176,128]{1,0:T(8,128)} %get-tuple-element.426.grads_ref, f32[8,512]{1,0:T(8,128)} %broadcast_select_fusion.square_ref), custom_call_target="tpu_custom_call" | custom-call | tf_op jit(solution)/shard_map/reduce_windows/pallas_call | solution.py:1377
  516.6 1.5 reduce_sum.190
  518.9 1.4 copy-done.4
  520.4 1.7 lift_window.1
  522.1 3.5 multiply_subtract_fusion.1
  525.6 32.1 %multiply_subtract_fusion = (f32[6176,512]{1,0:T(8,128)}, f32[6176,512]{1,0:T(8,128)}, f32[6176,512]{1,0:T(8,128)}) fusion(f32[6176,512]{1,0:T(8,128)} %param.24, f32[]{:T(128)S(6)} %min_shard_map.3, f32[6184,512]{1,0:T(8,128)} %get-tuple-element.438, f32[6176,512]{1,0:T(8,128)} %param.25, f32[6176,512]{1,0:T(8,128)} %param.26), kind=kLoop, calls=%fused_computation.33 | loop fusion | flops 50593792 | bytes 88539136 | tf_op jit(solution)/shard_map/sub | solution.py:488
  (72 shorter events, 2.3 us)
Async XLA Ops:
  13.3 1.7 copy-start.6
  202.4 4.0 copy-start
  202.4 4.0 copy-start.1
  202.4 4.0 copy-start.3
  255.7 0.8 copy-start.11
  280.9 21.5 %copy-start.12 = (f32[8,512]{1,0:T(8,128)S(1)}, f32[8,512]{1,0:T(8,128)}, u32[]{:S(2)}) copy-start(f32[8,512]{1,0:T(8,128)} %get-tuple-element.424) | copy-start | bytes 49156
  280.9 22.3 %copy-start.10 = (f32[77,512]{1,0:T(8,128)S(1)}, f32[77,512]{1,0:T(8,128)}, u32[]{:S(2)}) copy-start(f32[77,512]{1,0:T(8,128)} %get-tuple-element.423) | copy-start | bytes 473092
  300.6 4.3 copy-start.9
  356.0 1.9 copy-start.2
  375.9 146.2 %copy-start.5 = (f32[416441]{0:T(1024)S(1)}, f32[416441]{0:T(1024)}, u32[]{:S(2)}) copy-start(f32[416441]{0:T(1024)} %param.21) | copy-start | bytes 4997296
  375.9 146.2 %copy-start.7 = (f32[416441]{0:T(1024)S(1)}, f32[416441]{0:T(1024)}, u32[]{:S(2)}) copy-start(f32[416441]{0:T(1024)} %param.22) | copy-start | bytes 4997296
  518.9 1.5 copy-start.4
  520.4 1.8 copy-start.8

commit v6 on v5

--- a/solution.py
+++ b/solution.py
@@ -52,6 +52,7 @@
 GROUP = 16
 CHUNKS = 16
 GATHER_CHUNKS = 14
+TURNED = 6
 CACHED_ROWS = 64
 ID_ROWS = 16
 MESH = pl.DeviceIdType.MESH
@@ -1078,43 +1079,66 @@
     return (jnp.arange(count)[:, None] == slots[None, :]).astype(jnp.bfloat16)
 
 
+def turned_rows(chunk):
+    return TURNED * chunk // (16 * GROUP) * GROUP
+
+
 def gather_kernel(sizes, chunks, window_ref, out_ref, own_sem, h_send, h_recv, b_send, b_recv, a_send, a_recv, core_send,
                   core_recv):
     at = Places(sizes)
     rows = window_ref.shape[0]
     chunk = rows // chunks
+    changed = turned_rows(chunk)
+    ways = (False, True) if changed else (False,)
+    spans = {False: (0, chunk - changed), True: (chunk - changed, changed)}
     me = at.linear(at.core, at.a, at.b, at.h)
     sibling, peers_a, peers_b, peers_h = at.sibling(), at.along_a(), at.along_b(), at.along_h()
     greet_all([sibling] + peers_a + peers_b + peers_h)
-
-    def part(block, t):
-        return out_ref.at[pl.ds(pl.multiple_of(block * rows + t * chunk, GROUP), chunk)]
+    along_h, along_b = (peers_h, h_send, h_recv), (peers_b, b_send, b_recv)
+
+    def part(block, t, span=(0, chunk)):
+        return out_ref.at[pl.ds(pl.multiple_of(block * rows + t * chunk + span[0], GROUP), span[1])]
 
     def many(count):
-        return out_ref.at[pl.ds(0, count * chunk)]
+        return out_ref.at[pl.ds(0, count)]
 
     def own_copy(t):
         src = window_ref.at[pl.ds(pl.multiple_of(t * chunk, GROUP), chunk)]
-        return src, pltpu.make_async_copy(src, part(me, t), own_sem.at[t])
-
-    def stage_h(t):
-        src, own = own_copy(t)
-        for d, other in enumerate(peers_h):
-            remote(src, part(me, t), h_send.at[d], h_recv.at[t, d], other).start()
-        own.start()
-
-    def stage_b(t):
-        own_copy(t)[1].wait()
-        for d, other in enumerate(peers_h):
-            remote(many(1), many(1), h_send.at[d], h_recv.at[t, d], other).wait_recv()
-        for d, other in enumerate(peers_b):
-            for h in range(at.high_size):
-                block = part(at.linear(at.core, at.a, at.b, h), t)
-                remote(block, block, b_send.at[d], b_recv.at[t, d], other).start()
-
-    def stage_a(t):
-        for d, other in enumerate(peers_b):
-            remote(many(at.high_size), many(at.high_size), b_send.at[d], b_recv.at[t, d], other).wait_recv()
+        return pltpu.make_async_copy(src, part(me, t), own_sem.at[t])
+
+    def first(t):
+        for turned in ways:
+            peers, send, recv = along_b if turned else along_h
+            start, size = spans[turned]
+            src = window_ref.at[pl.ds(pl.multiple_of(t * chunk + start, GROUP), size)]
+            for d, other in enumerate(peers):
+                remote(src, part(me, t, spans[turned]), send.at[d], recv.at[int(turned), t, d], other).start()
+        own_copy(t).start()
+
+    def second(t):
+        own_copy(t).wait()
+        for turned in ways:
+            size = many(spans[turned][1])
+            peers, send, recv = along_b if turned else along_h
+            for d, other in enumerate(peers):
+                remote(size, size, send.at[d], recv.at[int(turned), t, d], other).wait_recv()
+            if turned:
+                blocks = [at.linear(at.core, at.a, b, at.h) for b in range(at.b_size)]
+            else:
+                blocks = [at.linear(at.core, at.a, at.b, h) for h in range(at.high_size)]
+            peers, send, recv = along_h if turned else along_b
+            for d, other in enumerate(peers):
+                for block in blocks:
+                    block = part(block, t, spans[turned])
+                    remote(block, block, send.at[d], recv.at[int(turned), t, d], other).start()
+
+    def third(t):
+        for turned in ways:
+            count = at.b_size if turned else at.high_size
+            size = many(count * spans[turned][1])
+            peers, send, recv = along_h if turned else along_b
+            for d, other in enumerate(peers):
+                remote(size, size, send.at[d], recv.at[int(turned), t, d], other).wait_recv()
         for d, other in enumerate(peers_a):
             for b in range(at.b_size):
                 for h in range(at.high_size):
@@ -1123,9 +1147,10 @@
 
     plane = at.b_size * at.high_size
 
-    def stage_core(t):
+    def fourth(t):
+        size = many(plane * chunk)
         for d, other in enumerate(peers_a):
-            remote(many(plane), many(plane), a_send.at[d], a_recv.at[t, d], other).wait_recv()
+            remote(size, size, a_send.at[d], a_recv.at[t, d], other).wait_recv()
         for a in range(at.a_size):
             for b in range(at.b_size):
                 for h in range(at.high_size):
@@ -1133,25 +1158,22 @@
                     remote(block, block, core_send, core_recv, sibling).start()
 
     def turn(t, carry):
-        for depth, stage in enumerate((stage_h, stage_b, stage_a, stage_core)):
-            @pl.when((t >= depth) & (t < chunks + depth))
-            def _():
-                stage(t - depth)
-
+        for depth, stage in enumerate((first, second, third, fourth)):
+            active = (t >= depth) & (t < chunks + depth)
+            pl.when(active)(functools.partial(stage, t - depth))
         return carry
 
     lax.fori_loop(0, chunks + 3, turn, 0)
-
-    def whole(count):
-        return out_ref.at[pl.ds(0, count * rows)]
-
-    for d, other in enumerate(peers_h):
-        remote(whole(1), whole(1), h_send.at[d], h_recv.at[0, d], other).wait_send()
-    for d, other in enumerate(peers_b):
-        remote(whole(at.high_size), whole(at.high_size), b_send.at[d], b_recv.at[0, d], other).wait_send()
-    for d, other in enumerate(peers_a):
-        remote(whole(plane), whole(plane), a_send.at[d], a_recv.at[0, d], other).wait_send()
-    half = whole(at.a_size * plane)
+    straight = chunk - changed
+    for peers, send, sent in (
+        (peers_h, h_send, straight + changed * at.b_size),
+        (peers_b, b_send, straight * at.high_size + changed),
+        (peers_a, a_send, chunk * plane),
+    ):
+        size = many(chunks * sent)
+        for d, other in enumerate(peers):
+            remote(size, size, send.at[d], core_recv, other).wait_send()
+    half = many(at.a_size * plane * rows)
     last = remote(half, half, core_send, core_recv, sibling)
     last.wait_send()
     last.wait_recv()
@@ -1166,7 +1188,7 @@
         out_shape=jax.ShapeDtypeStruct((gx_size * gy_size * window.shape[0], LANES), window.dtype),
         in_specs=[pl.BlockSpec(memory_space=pltpu.VMEM)],
         out_specs=pl.BlockSpec(memory_space=pl.ANY),
-        scratch_shapes=[dma((chunks,)), dma((h,)), dma((chunks, h)), dma((b,)), dma((chunks, b)), dma((a,)),
+        scratch_shapes=[dma((chunks,)), dma((h,)), dma((2, chunks, h)), dma((b,)), dma((2, chunks, b)), dma((a,)),
                         dma((chunks, a)), dma, dma],
         compiler_params=pltpu.CompilerParams(
             collective_id=number, has_side_effects=True, vmem_limit_bytes=32 << 20
@@ -1175,9 +1197,98 @@
     )(window)
 
 
-def reduce_kernel(shard, sizes, grads_ref, square_ref, out_ref, squares_ref, own, landed, keep_one, send_one, recv_one, keep_two, send_two,
-                  recv_two, keep_three, send_three, recv_three, partial, square_send, square_recv, load_sem, pair_send, pair_recv, credit,
-                  one_send, one_recv, two_send, two_recv, three_send, three_recv):
+class Way:
+    def __init__(self, at, turned, span, refs):
+        self.start, self.size = span
+        (self.keep_two, self.send_two, self.recv_two, self.keep_three, self.send_three, self.recv_three,
+         self.two_send, self.two_recv, self.three_send, self.three_recv) = refs
+        along_b, along_h = (at.along_b(), at.b, at.b_size), (at.along_h(), at.h, at.high_size)
+        high = at.high_size
+        if turned:
+            (self.peers, self.place, self.count), (self.last_peers, self.last_place, self.inner) = along_h, along_b
+            self.number = lambda other, i: i * high + other
+        else:
+            (self.peers, self.place, self.count), (self.last_peers, self.last_place, self.inner) = along_b, along_h
+            self.number = lambda other, i: other * high + i
+
+    def two(self, u, d):
+        slot = lax.rem(u, 2)
+        return remote(self.send_two.at[slot, d - 1], self.recv_two.at[u, d - 1], self.two_send.at[slot, d - 1],
+                      self.two_recv.at[u, d - 1], self.peers[d - 1])
+
+    def three(self, u, d):
+        slot = lax.rem(u, 2)
+        return remote(self.send_three.at[slot, d - 1], self.recv_three.at[u, d - 1], self.three_send.at[slot, d - 1],
+                      self.three_recv.at[u, d - 1], self.last_peers[d - 1])
+
+    def second(self, u, total):
+        slot, rows = lax.rem(u, 2), pl.ds(self.start, self.size)
+        for d in range(1, self.count):
+            pl.when(u >= 2)(lambda d=d: self.two(u - 2, d).wait_send())
+            other = lax.rem(self.place + d, self.count)
+
+            def give(i, carry):
+                self.send_two[slot, d - 1, i] = total(self.number(other, i), rows).astype(jnp.bfloat16)
+                return carry
+
+            lax.fori_loop(0, self.inner, give, 0)
+            self.two(u, d).start()
+
+        def hold(i, carry):
+            self.keep_two[slot, i] = total(self.number(self.place, i), rows)
+            return carry
+
+        lax.fori_loop(0, self.inner, hold, 0)
+
+    def third(self, u):
+        slot = lax.rem(u, 2)
+        for d in range(1, self.count):
+            self.two(u, d).wait_recv()
+
+        def total(i):
+            value = self.keep_two[slot, i]
+            for d in range(1, self.count):
+                value = value + self.recv_two[u, d - 1, i].astype(jnp.float32)
+            return value
+
+        for d in range(1, self.inner):
+            pl.when(u >= 2)(lambda d=d: self.three(u - 2, d).wait_send())
+            self.send_three[slot, d - 1] = total(lax.rem(self.last_place + d, self.inner)).astype(jnp.bfloat16)
+            self.three(u, d).start()
+        self.keep_three[slot] = total(self.last_place)
+
+    def last(self, u):
+        value = self.keep_three[lax.rem(u, 2)]
+        for d in range(1, self.inner):
+            self.three(u, d).wait_recv()
+            value = value + self.recv_three[u, d - 1].astype(jnp.float32)
+        return value
+
+    def drain(self, u):
+        for d in range(1, self.count):
+            self.two(u, d).wait_send()
+        for d in range(1, self.inner):
+            self.three(u, d).wait_send()
+
+
+def way_scratch(chunks, count, inner, size):
+    low, dma = jnp.bfloat16, pltpu.SemaphoreType.DMA
+    return [
+        pltpu.VMEM((2, inner, size, LANES), jnp.float32),
+        pltpu.VMEM((2, count - 1, inner, size, LANES), low),
+        pltpu.VMEM((chunks, count - 1, inner, size, LANES), low),
+        pltpu.VMEM((2, size, LANES), jnp.float32),
+        pltpu.VMEM((2, inner - 1, size, LANES), low),
+        pltpu.VMEM((chunks, inner - 1, size, LANES), low),
+        dma((2, count - 1)),
+        dma((chunks, count - 1)),
+        dma((2, inner - 1)),
+        dma((chunks, inner - 1)),
+    ]
+
+
+def reduce_kernel(shard, sizes, grads_ref, square_ref, out_ref, squares_ref, own, landed, keep_one, send_one, recv_one,
+                  partial, square_send, square_recv, load_sem, pair_send, pair_recv, credit, one_send, one_recv, *more):
     at = Places(sizes)
     a_size, b_size, high_size = at.a_size, at.b_size, at.high_size
     core, my_a, my_b, high = at.core, at.a, at.b, at.h
@@ -1189,7 +1300,12 @@
         a, rest = number // plane, lax.rem(number, plane)
         return window_start(shard, at.linear(side, a, rest // high_size, lax.rem(rest, high_size)))
 
-    sibling, peers, peers_two, peers_three = at.sibling(), at.along_a(), at.along_b(), at.along_h()
+    sibling, peers = at.sibling(), at.along_a()
+    changed = turned_rows(chunk)
+    straight = chunk - changed
+    ways = [Way(at, False, (0, straight), more[:10])]
+    if changed:
+        ways.append(Way(at, True, (straight, changed), more[10:]))
     count = squares_ref.shape[0]
     me = linear_index(at.gy_size)
 
@@ -1269,68 +1385,27 @@
             remote(recv_one.at[u, d - 1], recv_one.at[u, d - 1], one_send.at[slot, d - 1], one_recv.at[u, d - 1],
                    peers[d - 1]).wait_recv()
 
-        def total(number):
-            value = keep_one[slot, number]
+        def total(number, rows):
+            value = keep_one[slot, number, rows, :]
             for d in range(1, a_size):
-                value = value + recv_one[u, d - 1, number].astype(jnp.float32)
+                value = value + recv_one[u, d - 1, number, rows, :].astype(jnp.float32)
             return value
 
-        for d in range(1, b_size):
-            @pl.when(u >= 2)
-            def _():
-                remote(send_two.at[slot, d - 1], recv_two.at[u - 2, d - 1], two_send.at[slot, d - 1],
-                       two_recv.at[u - 2, d - 1], peers_two[d - 1]).wait_send()
-
-            first = lax.rem(my_b + d, b_size) * high_size
-
-            def give(i, carry):
-                send_two[slot, d - 1, i] = total(first + i).astype(jnp.bfloat16)
-                return carry
-
-            lax.fori_loop(0, high_size, give, 0)
-            remote(send_two.at[slot, d - 1], recv_two.at[u, d - 1], two_send.at[slot, d - 1],
-                   two_recv.at[u, d - 1], peers_two[d - 1]).start()
-
-        def hold(i, carry):
-            keep_two[slot, i] = total(my_b * high_size + i)
-            return carry
-
-        lax.fori_loop(0, high_size, hold, 0)
+        for way in ways:
+            way.second(u, total)
 
     def third_stage(u):
-        slot = lax.rem(u, 2)
-        for d in range(1, b_size):
-            remote(recv_two.at[u, d - 1], recv_two.at[u, d - 1], two_send.at[slot, d - 1], two_recv.at[u, d - 1],
-                   peers_two[d - 1]).wait_recv()
-
-        def total(number):
-            value = keep_two[slot, number]
-            for d in range(1, b_size):
-                value = value + recv_two[u, d - 1, number].astype(jnp.float32)
-            return value
-
-        for d in range(1, high_size):
-            @pl.when(u >= 2)
-            def _():
-                remote(send_three.at[slot, d - 1], recv_three.at[u - 2, d - 1], three_send.at[slot, d - 1],
-                       three_recv.at[u - 2, d - 1], peers_three[d - 1]).wait_send()
-
-            send_three[slot, d - 1] = total(lax.rem(high + d, high_size)).astype(jnp.bfloat16)
-            remote(send_three.at[slot, d - 1], recv_three.at[u, d - 1], three_send.at[slot, d - 1],
-                   three_recv.at[u, d - 1], peers_three[d - 1]).start()
-        keep_three[slot] = total(high)
+        for way in ways:
+            way.third(u)
 
     def last_stage(u):
-        slot = lax.rem(u, 2)
-        value = keep_three[slot]
-        for d in range(1, high_size):
-            remote(recv_three.at[u, d - 1], recv_three.at[u, d - 1], three_send.at[slot, d - 1],
-                   three_recv.at[u, d - 1], peers_three[d - 1]).wait_recv()
-            value = value + recv_three[u, d - 1].astype(jnp.float32)
-        out_ref[pl.ds(pl.multiple_of(u * chunk, GROUP), chunk), :] = value
-        place = spot + (window_start(shard, me) + u * chunk) * LANES - me * shard
-        square = jnp.where((place >= 0) & (place < shard), value * value, 0.0)
-        partial[...] += sum(square[r : r + 8] for r in range(0, chunk, 8))
+        for way in ways:
+            value = way.last(u)
+            row = u * chunk + way.start
+            out_ref[pl.ds(pl.multiple_of(row, GROUP), way.size), :] = value
+            place = spot[: way.size] + (window_start(shard, me) + row) * LANES - me * shard
+            square = jnp.where((place >= 0) & (place < shard), value * value, 0.0)
+            partial[...] += sum(square[r : r + 8] for r in range(0, way.size, 8))
 
     def turn(t, carry):
         stages = (pair_stage, first_stage, second_stage, third_stage, last_stage)
@@ -1358,12 +1433,8 @@
         for d in range(1, a_size):
             remote(send_one.at[slot, d - 1], recv_one.at[u, d - 1], one_send.at[slot, d - 1],
                    one_recv.at[u, d - 1], peers[d - 1]).wait_send()
-        for d in range(1, b_size):
-            remote(send_two.at[slot, d - 1], recv_two.at[u, d - 1], two_send.at[slot, d - 1],
-                   two_recv.at[u, d - 1], peers_two[d - 1]).wait_send()
-        for d in range(1, high_size):
-            remote(send_three.at[slot, d - 1], recv_three.at[u, d - 1], three_send.at[slot, d - 1],
-                   three_recv.at[u, d - 1], peers_three[d - 1]).wait_send()
+        for way in ways:
+            way.drain(u)
 
 
 def reduce_windows(grads, square, shard, gx_size, gy_size, number):
@@ -1373,7 +1444,7 @@
     plane = low_size * high_size
     blocks = x_size * plane
     low_type, dma = jnp.bfloat16, pltpu.SemaphoreType.DMA
-    a, b, h = x_size - 1, low_size - 1, high_size - 1
+    a = x_size - 1
     return pl.pallas_call(
         functools.partial(reduce_kernel, shard, (x_size, low_size, high_size)),
         out_shape=[
@@ -1388,12 +1459,6 @@
             pltpu.VMEM((2, plane, chunk, LANES), jnp.float32),
             pltpu.VMEM((2, a, plane, chunk, LANES), low_type),
             pltpu.VMEM((CHUNKS, a, plane, chunk, LANES), low_type),
-            pltpu.VMEM((2, high_size, chunk, LANES), jnp.float32),
-            pltpu.VMEM((2, b, high_size, chunk, LANES), low_type),
-            pltpu.VMEM((CHUNKS, b, high_size, chunk, LANES), low_type),
-            pltpu.VMEM((2, chunk, LANES), jnp.float32),
-            pltpu.VMEM((2, h, chunk, LANES), low_type),
-            pltpu.VMEM((CHUNKS, h, chunk, LANES), low_type),
             pltpu.VMEM((8, LANES), jnp.float32),
             dma,
             dma,
@@ -1403,11 +1468,9 @@
             pltpu.SemaphoreType.REGULAR,
             dma((2, a)),
             dma((CHUNKS, a)),
-            dma((2, b)),
-            dma((CHUNKS, b)),
-            dma((2, h)),
-            dma((CHUNKS, h)),
-        ],
+        ]
+        + way_scratch(CHUNKS, low_size, high_size, chunk - turned_rows(chunk))
+        + (way_scratch(CHUNKS, high_size, low_size, turned_rows(chunk)) if turned_rows(chunk) else []),
         compiler_params=pltpu.CompilerParams(
             collective_id=number, has_side_effects=True, vmem_limit_bytes=60 << 20
         ),

time: 578 us -> 563 us (0.974)
  Pallas kernels: 452 us -> 436 us
    pallas_call x1, Pallas kernels: 141 us -> 132 us  [reduce_windows(): pl.pallas_call(functools.partial(reduce_kernel, shard, (x_size, low_size,...]
    pallas_call x2, Pallas kernels: 144 us -> 136 us  [gather_windows(): pl.pallas_call(functools.partial(gather_kernel, sizes, chunks), out_shape...]
where the time goes in v6:
time: 563 us; the launch traced here: 553 us
  Pallas kernels  436 us (77%)
  other arithmetic  47.5 us (8%)
  local copies, waits for them, and re-layouts  36.6 us (7%)
  between operations  24.9 us (4%)
  matrix products  7.52 us (1%)
    pallas_call x2, Pallas kernels, gather_windows(): pl.pallas_call(functools.partial(gather_kernel, sizes, chunks), out_shape...  136 us
    pallas_call x1, Pallas kernels, reduce_windows(): pl.pallas_call(functools.partial(reduce_kernel, shard, (x_size, low_size,...  132 us
    pallas_call x1, Pallas kernels, weight_grads(): pl.pallas_call(functools.partial(grads_kernel, parts, gx_size, gy_size),...  49.1 us
    pallas_call x1, Pallas kernels, spread_weights(): pl.pallas_call(functools.partial(spread_entry, shard, gx_size, gy_size, v...  36.6 us
    sub x2, other arithmetic, adam_step(): weight - rate * (first_hat / (jnp.sqrt(second_hat) + adam_eps) + decay *...  35.6 us
    pallas_call x2, Pallas kernels, tower_backward(): pl.pallas_call(functools.partial(tower_backward_kernel, tower), out_shape...  34.7 us
    pallas_call x2, Pallas kernels, tower_forward(): pl.pallas_call(functools.partial(tower_forward_kernel, tower), out_shape=...  26.7 us
    pallas_call x1, Pallas kernels, table_sum(): pl.pallas_call(functools.partial(table_sum_kernel, cap), out_shape=[jax.S...  18.1 us

profile of v6, /device:TPU:0, one launch (start us, length us, event | category | flops | bytes accessed | tf_op | source)
XLA Modules:
  0.0 553.4 jit_solution(7326715739881033464)
XLA Ops:
  7.2 0.8 reshape.345
  8.0 0.8 eq.183
  8.7 0.3 fusion.18
  9.3 0.5 select_reduce_fusion.3
  10.1 0.7 pad_maximum_fusion.9
  10.8 0.9 fusion.132
  11.7 1.6 pad_bitcast_fusion.flat_ref
  13.3 0.9 place_window.1
  14.3 0.6 copy-done.6
  15.0 1.4 copy.28
  16.3 2.2 pad.37.clone
  18.6 3.1 reshape.347.refs_3_.refs_0_
  21.7 122.7 %gather_weights.1.gathered_ref = bf16[107520,128]{1,0:T(8,128)(2,1)} custom-call(bf16[3360,128]{1,0:T(8,128)(2,1)S(1)} %pad_maximum_fusion.window_ref), custom_call_target="tpu_custom_call" | custom-call | tf_op jit(solution)/shard_map/gather_weights/pallas_call | solution.py:1186
  144.4 0.9 slice_convert_fusion
  145.6 0.6 convert_reduce_fusion
  146.3 0.6 reduce_max.27
  147.8 1.0 select_reduce_fusion.2
  148.9 1.1 slice.140
  150.0 0.3 reshape.353
  150.4 1.0 conditional.2
  150.4 0.9 broadcast_in_dim.195
  151.4 7.3 %gather_fusion.1 = bf16[768,512]{1,0:T(8,128)(2,1)S(1)} fusion(f32[6176,512]{1,0:T(8,128)} %param.24, s32[1024]{0:T(1024)S(1)} %pad_clamp_fusion.1), kind=kCustom, calls=%fused_computation.1 | custom fusion | bytes 1575936 | tf_op jit(solution)/shard_map/jit(_take)/gather | solution.py:1605
  158.7 36.6 %spread_weights.1 = (bf16[3072,768]{1,0:T(8,128)(2,1)}, bf16[768,3072]{1,0:T(8,128)(2,1)}, bf16[768,3072]{1,0:T(8,128)(2,1)}, bf16[3072,768]{1,0:T(8,128)(2,1)},...) custom-call(bf16[107520,128]{1,0:T(8,128)(2,1)} %gather_weights.1.ga, ...), custom_call_target="tpu_custom_call" | custom-call | tf_op jit(solution)/shard_map/spread_weights/pallas_call | solution.py:734
  195.4 0.6 slice.103
  196.7 1.8 fusion.21
  198.5 0.9 pad.40.refs_3_
  199.4 0.6 pad.38.refs_1_
  200.0 0.6 slice.105.refs_1_
  200.9 1.2 tile.24
  202.1 2.4 pad.39.refs_2_
  204.6 1.2 tile.21.refs_2_
  205.8 16.8 %image_forward.1 = (f32[400,768]{1,0:T(8,128)}, bf16[400,768]{1,0:T(8,128)(2,1)}, bf16[400,1536]{1,0:T(8,128)(2,1)}, bf16[16,768]{1,0:T(8,128)(2,1)}, bf16[16,76...) custom-call(s32[8]{0:T(128)} %refs_0_.7, ...), custom_call_target="tpu_custom_call" | custom-call | tf_op jit(solution)/shard_map/image_forward/pallas_call | solution.py:295
  222.6 0.7 convert_element_type.112
  223.3 10.0 %text_forward.1 = (f32[624,512]{1,0:T(8,128)}, bf16[624,512]{1,0:T(8,128)(2,1)}, bf16[624,1024]{1,0:T(8,128)(2,1)}, bf16[16,512]{1,0:T(8,128)(2,1)}, bf16[16,512...) custom-call(s32[8]{0:T(128)} %refs_0_.7, ...), custom_call_target="tpu_custom_call" | custom-call | tf_op jit(solution)/shard_map/text_forward/pallas_call | solution.py:295
  233.3 0.7 convert_element_type.114
  234.0 13.7 %embeddings.1 = bf16[2048,128]{1,0:T(8,128)(2,1)S(1)} custom-call(bf16[64,128]{1,0:T(8,128)(2,1)S(1)} %reshape.349.window_ref), custom_call_target="tpu_custom_call" | custom-call | tf_op jit(solution)/shard_map/embeddings/pallas_call | solution.py:1186
  247.8 0.3 reshape.350
  248.1 0.3 fusion.65
  248.5 0.5 select_reduce_fusion.4
  248.9 0.4 exponential_reduce_fusion
  249.3 0.9 fusion.67
  252.1 1.1 multiply_reduce_fusion
  255.7 0.4 fusion.44
  256.1 1.0 convolution_add_fusion.refs_2_
  257.2 14.9 %text_backward.1 = (bf16[16,512]{1,0:T(8,128)(2,1)}, bf16[16,512]{1,0:T(8,128)(2,1)}, bf16[16,2048]{1,0:T(8,128)(2,1)}, bf16[16,512]{1,0:T(8,128)(2,1)}, bf16[16...) custom-call(s32[8]{0:T(128)} %refs_0_.7, ...), custom_call_target="tpu_custom_call" | custom-call | tf_op jit(solution)/shard_map/text_backward/pallas_call | solution.py:439
  272.1 0.4 fusion.45
  272.5 1.0 convolution_add_fusion.1.refs_2_
  273.6 19.8 %image_backward.1 = (bf16[16,512]{1,0:T(8,128)(2,1)}, bf16[16,768]{1,0:T(8,128)(2,1)}, bf16[16,3072]{1,0:T(8,128)(2,1)}, bf16[16,768]{1,0:T(8,128)(2,1)}, bf16[1...) custom-call(s32[8]{0:T(128)} %refs_0_.7, ...), custom_call_target="tpu_custom_call" | custom-call | tf_op jit(solution)/shard_map/image_backward/pallas_call | solution.py:439
  293.3 0.8 slice_reduce_fusion
  294.2 0.9 reshape.357
  295.1 0.7 reshape.358
  295.9 1.0 concatenate.35
  296.9 0.8 pad.41.refs_26_
  297.7 1.7 fusion.19
  299.4 49.1 %weight_grads.1 = (f32[104176,128]{1,0:T(8,128)}, bf16[4,8,96,512]{3,2,1,0:T(8,128)(2,1)}) custom-call(bf16[400,3072]{1,0:T(8,128)(2,1)} %reshape.347.refs_3_.refs_0_, bf16[400,768]{1,0:T(8,128)(2,1)} %get-tuple-element.394.refs_1_, bf16[16,768]{1,0:T(8,128)(2,1)} %get-tuple-element.383.refs_6_.refs_2_, bf16[16,768]{1,0:T(8,128)(2,1)} %get-tuple-element.395.refs_3_, ...), custom_call_target="tpu_custom_call" | custom-call | tf_op jit(solution)/shard_map/weight_grads/pallas_call | solution.py:843
  348.5 1.9 copy-done.2
  350.4 18.1 %table_sum.1 = (f32[6184,512]{1,0:T(8,128)}, f32[8,512]{1,0:T(8,128)S(1)}) custom-call(s32[32]{0:T(128)S(1)} %broadcast_minimum_fusion.counts_ref, s32[3072]{0:T(1024)S(1)} %add.308.index_ref, bf16[32,96,512]{2,1,0:T(8,128)(2,1)S(1)} %bitcast.103), custom_call_target="tpu_custom_call" | custom-call | tf_op jit(solution)/shard_map/table_sum/pallas_call | solution.py:1058
  368.8 0.6 broadcast_select_fusion.square_ref
  369.4 132.2 %reduce_windows.1 = (f32[3328,128]{1,0:T(8,128)}, f32[32,8,128]{2,1,0:T(8,128)}) custom-call(f32[104176,128]{1,0:T(8,128)} %get-tuple-element.426.grads_ref, f32[8,512]{1,0:T(8,128)} %broadcast_select_fusion.square_ref), custom_call_target="tpu_custom_call" | custom-call | tf_op jit(solution)/shard_map/reduce_windows/pallas_call | solution.py:1448
  501.6 1.5 reduce_sum.190
  503.9 1.4 copy-done.4
  505.3 1.7 lift_window.1
  507.1 3.5 multiply_subtract_fusion.1
  510.6 32.1 %multiply_subtract_fusion = (f32[6176,512]{1,0:T(8,128)}, f32[6176,512]{1,0:T(8,128)}, f32[6176,512]{1,0:T(8,128)}) fusion(f32[6176,512]{1,0:T(8,128)} %param.24, f32[]{:T(128)S(6)} %min_shard_map.3, f32[6184,512]{1,0:T(8,128)} %get-tuple-element.438, f32[6176,512]{1,0:T(8,128)} %param.25, f32[6176,512]{1,0:T(8,128)} %param.26), kind=kLoop, calls=%fused_computation.33 | loop fusion | flops 50593792 | bytes 88539136 | tf_op jit(solution)/shard_map/sub | solution.py:489
  (72 shorter events, 2.3 us)
Async XLA Ops:
  13.3 1.7 copy-start.6
  195.3 4.0 copy-start
  195.3 4.0 copy-start.1
  195.3 4.0 copy-start.3
  248.5 0.8 copy-start.11
  273.6 21.5 %copy-start.12 = (f32[8,512]{1,0:T(8,128)S(1)}, f32[8,512]{1,0:T(8,128)}, u32[]{:S(2)}) copy-start(f32[8,512]{1,0:T(8,128)} %get-tuple-element.424) | copy-start | bytes 49156
  273.6 22.3 %copy-start.10 = (f32[77,512]{1,0:T(8,128)S(1)}, f32[77,512]{1,0:T(8,128)}, u32[]{:S(2)}) copy-start(f32[77,512]{1,0:T(8,128)} %get-tuple-element.423) | copy-start | bytes 473092
  293.3 4.3 copy-start.9
  348.5 1.9 copy-start.2
  369.4 137.7 %copy-start.5 = (f32[416441]{0:T(1024)S(1)}, f32[416441]{0:T(1024)}, u32[]{:S(2)}) copy-start(f32[416441]{0:T(1024)} %param.21) | copy-start | bytes 4997296
  369.4 137.7 %copy-start.7 = (f32[416441]{0:T(1024)S(1)}, f32[416441]{0:T(1024)}, u32[]{:S(2)}) copy-start(f32[416441]{0:T(1024)} %param.22) | copy-start | bytes 4997296
  503.9 1.5 copy-start.4
  505.3 1.8 copy-start.8

commit v7 on v6

--- a/solution.py
+++ b/solution.py
@@ -158,7 +158,7 @@
         return jnp.concatenate(rows, 0)
 
     def row_of(self, s, ends_ref):
-        return s * self.length + (0 if self.image else ends_ref[s])
+        return s if self.image else s * self.length + ends_ref[s]
 
     def each_block(self, function, start):
         return lax.fori_loop(
@@ -230,12 +230,16 @@
     queries = tower.spread_heads(query, wide_ref)
     scores = dot_nt(queries, pair_ref[:, :width]) * (width // tower.heads) ** (-0.5)
     row = lax.broadcasted_iota(jnp.int32, scores.shape, 0) // tower.lanes
-    spot = lax.broadcasted_iota(jnp.int32, scores.shape, 1) - row * tower.length
-    last = jnp.full(scores.shape, tower.length - 1, jnp.int32)
-    if not tower.image:
+    spot = lax.broadcasted_iota(jnp.int32, scores.shape, 1)
+    if tower.image:
+        allowed = lax.rem(spot, SEQS) == row
+    else:
+        spot = spot - row * tower.length
+        last = jnp.zeros(scores.shape, jnp.int32)
         for s in range(SEQS):
             last = jnp.where(row == s, ends_ref[s], last)
-    scores = jnp.where((spot >= 0) & (spot <= last), scores, -1e30)
+        allowed = (spot >= 0) & (spot <= last)
+    scores = jnp.where(allowed, scores, -1e30)
     powers = jnp.exp(scores - jnp.max(scores, -1, keepdims=True))
     probs = powers / jnp.sum(powers, -1, keepdims=True)
     probs_ref[...] = probs
@@ -414,6 +418,10 @@
     gain_pre, shift_pre = tower.each_block(second, (nothing, nothing))
     gain_grads_ref[0:1, :] = gain_pre
     gain_grads_ref[1:2, :] = shift_pre
+    if tower.image:
+        for p in range(tower.length):
+            places_ref[p : p + 1, :] = sum_rows(grad_ref_wide[p * SEQS : (p + 1) * SEQS, :])
+        return
     places = grad_ref_wide[0 : tower.length, :]
     for s in range(1, SEQS):
         places = places + grad_ref_wide[s * tower.length : (s + 1) * tower.length, :]
@@ -469,9 +477,9 @@
 
 
 def image_inputs(image_vec, pixels):
-    pixels = jnp.pad(pixels, ((0, 0), (1, 0), (0, 0))).reshape(-1, PATCH_DIM)
+    pixels = jnp.pad(pixels.transpose(1, 0, 2), ((1, 0), (0, 0), (0, 0))).reshape(-1, PATCH_DIM)
     base = image_vec[1 : IMG_TOK + 1] + jnp.pad(image_vec[:1], ((0, IMG_TOK - 1), (0, 0)))
-    return image_vec[IMG_TOK + 1 :], jnp.tile(base, (SEQS, 1)), pixels
+    return image_vec[IMG_TOK + 1 :], jnp.repeat(base, SEQS, axis=0), pixels
 
 
 def text_inputs(text_vec, token_rows):

time: 563 us -> 557 us (0.989)
  no operation moved by 1% of the time
where the time goes in v7:
time: 557 us; the launch traced here: 548 us
  Pallas kernels  436 us (78%)
  other arithmetic  47.5 us (9%)
  local copies, waits for them, and re-layouts  31.4 us (6%)
  between operations  24.9 us (4%)
  matrix products  7.51 us (1%)
    pallas_call x2, Pallas kernels, gather_windows(): pl.pallas_call(functools.partial(gather_kernel, sizes, chunks), out_shape...  136 us
    pallas_call x1, Pallas kernels, reduce_windows(): pl.pallas_call(functools.partial(reduce_kernel, shard, (x_size, low_size,...  133 us
    pallas_call x1, Pallas kernels, weight_grads(): pl.pallas_call(functools.partial(grads_kernel, parts, gx_size, gy_size),...  49.1 us
    pallas_call x1, Pallas kernels, spread_weights(): pl.pallas_call(functools.partial(spread_entry, shard, gx_size, gy_size, v...  36.6 us
    sub x2, other arithmetic, adam_step(): weight - rate * (first_hat / (jnp.sqrt(second_hat) + adam_eps) + decay *...  35.6 us
    pallas_call x2, Pallas kernels, tower_backward(): pl.pallas_call(functools.partial(tower_backward_kernel, tower), out_shape...  34.7 us
    pallas_call x2, Pallas kernels, tower_forward(): pl.pallas_call(functools.partial(tower_forward_kernel, tower), out_shape=...  26.7 us
    pallas_call x1, Pallas kernels, table_sum(): pl.pallas_call(functools.partial(table_sum_kernel, cap), out_shape=[jax.S...  17.4 us

profile of v7, /device:TPU:0, one launch (start us, length us, event | category | flops | bytes accessed | tf_op | source)
XLA Modules:
  0.0 548.1 jit_solution(15412256405191225871)
XLA Ops:
  7.2 0.8 reshape.344
  8.0 0.8 eq.183
  8.7 0.3 fusion.18
  9.3 0.5 select_reduce_fusion.3
  10.1 0.7 pad_maximum_fusion.9
  10.8 0.9 fusion.132
  11.7 1.6 pad_bitcast_fusion.1.flat_ref
  13.3 0.9 place_window.1
  14.3 0.6 copy-done.6
  15.0 1.6 pad_bitcast_fusion.refs_3_.refs_0_
  16.6 122.7 %gather_weights.1.gathered_ref = bf16[107520,128]{1,0:T(8,128)(2,1)} custom-call(bf16[3360,128]{1,0:T(8,128)(2,1)S(1)} %pad_maximum_fusion.window_ref), custom_call_target="tpu_custom_call" | custom-call | tf_op jit(solution)/shard_map/gather_weights/pallas_call | solution.py:1194
  139.3 0.9 slice_convert_fusion
  140.5 0.6 convert_reduce_fusion
  141.1 0.6 reduce_max.27
  142.5 0.2 fusion.23
  142.7 1.0 select_reduce_fusion.2
  143.8 1.1 slice.140
  144.9 0.3 reshape.353
  145.3 1.0 conditional.2
  145.3 0.9 broadcast_in_dim.197
  146.3 7.3 %gather_fusion.1 = bf16[768,512]{1,0:T(8,128)(2,1)S(1)} fusion(f32[6176,512]{1,0:T(8,128)} %param.24, s32[1024]{0:T(1024)S(1)} %pad_clamp_fusion.1), kind=kCustom, calls=%fused_computation.1 | custom fusion | bytes 1575936 | tf_op jit(solution)/shard_map/jit(_take)/gather | solution.py:1613
  153.6 36.6 %spread_weights.1 = (bf16[3072,768]{1,0:T(8,128)(2,1)}, bf16[768,3072]{1,0:T(8,128)(2,1)}, bf16[768,3072]{1,0:T(8,128)(2,1)}, bf16[3072,768]{1,0:T(8,128)(2,1)},...) custom-call(bf16[107520,128]{1,0:T(8,128)(2,1)} %gather_weights.1.ga, ...), custom_call_target="tpu_custom_call" | custom-call | tf_op jit(solution)/shard_map/spread_weights/pallas_call | solution.py:742
  190.2 0.6 slice.103
  191.5 1.8 fusion.21
  193.4 0.9 pad.40.refs_3_
  194.3 0.6 pad.38.refs_1_
  194.9 0.6 slice.105.refs_1_
  195.6 1.1 broadcast_bitcast_fusion.refs_2_
  196.7 16.8 %image_forward.1 = (f32[400,768]{1,0:T(8,128)}, bf16[400,768]{1,0:T(8,128)(2,1)}, bf16[400,1536]{1,0:T(8,128)(2,1)}, bf16[16,768]{1,0:T(8,128)(2,1)}, bf16[16,76...) custom-call(s32[8]{0:T(128)} %refs_0_.7, ...), custom_call_target="tpu_custom_call" | custom-call | tf_op jit(solution)/shard_map/image_forward/pallas_call | solution.py:299
  213.5 0.7 convert_element_type.112
  214.4 1.2 tile.13
  215.6 2.4 pad.39.refs_2_
  218.0 10.0 %text_forward.1 = (f32[624,512]{1,0:T(8,128)}, bf16[624,512]{1,0:T(8,128)(2,1)}, bf16[624,1024]{1,0:T(8,128)(2,1)}, bf16[16,512]{1,0:T(8,128)(2,1)}, bf16[16,512...) custom-call(s32[8]{0:T(128)} %refs_0_.7, ...), custom_call_target="tpu_custom_call" | custom-call | tf_op jit(solution)/shard_map/text_forward/pallas_call | solution.py:299
  228.0 0.7 convert_element_type.114
  228.7 13.7 %embeddings.1 = bf16[2048,128]{1,0:T(8,128)(2,1)S(1)} custom-call(bf16[64,128]{1,0:T(8,128)(2,1)S(1)} %reshape.349.window_ref), custom_call_target="tpu_custom_call" | custom-call | tf_op jit(solution)/shard_map/embeddings/pallas_call | solution.py:1194
  242.5 0.3 reshape.350
  242.8 0.3 fusion.65
  243.2 0.5 select_reduce_fusion.4
  243.6 0.4 exponential_reduce_fusion
  244.0 0.9 fusion.67
  246.8 1.1 multiply_reduce_fusion
  250.5 0.4 fusion.44
  250.8 1.0 convolution_add_fusion.refs_2_
  251.9 14.9 %text_backward.1 = (bf16[16,512]{1,0:T(8,128)(2,1)}, bf16[16,512]{1,0:T(8,128)(2,1)}, bf16[16,2048]{1,0:T(8,128)(2,1)}, bf16[16,512]{1,0:T(8,128)(2,1)}, bf16[16...) custom-call(s32[8]{0:T(128)} %refs_0_.7, ...), custom_call_target="tpu_custom_call" | custom-call | tf_op jit(solution)/shard_map/text_backward/pallas_call | solution.py:447
  266.8 0.4 fusion.45
  267.2 1.0 convolution_add_fusion.1.refs_2_
  268.3 19.8 %image_backward.1 = (bf16[16,512]{1,0:T(8,128)(2,1)}, bf16[16,768]{1,0:T(8,128)(2,1)}, bf16[16,3072]{1,0:T(8,128)(2,1)}, bf16[16,768]{1,0:T(8,128)(2,1)}, bf16[1...) custom-call(s32[8]{0:T(128)} %refs_0_.7, ...), custom_call_target="tpu_custom_call" | custom-call | tf_op jit(solution)/shard_map/image_backward/pallas_call | solution.py:447
  288.1 0.8 slice_reduce_fusion
  288.9 0.9 reshape.357
  289.8 0.7 reshape.358
  290.6 1.0 concatenate.35
  291.6 0.8 pad.41.refs_26_
  292.4 1.7 fusion.19
  294.1 49.1 %weight_grads.1 = (f32[104176,128]{1,0:T(8,128)}, bf16[4,8,96,512]{3,2,1,0:T(8,128)(2,1)}) custom-call(bf16[400,3072]{1,0:T(8,128)(2,1)} %pad_bitcast_fusion.refs_3_.refs_0_, bf16[400,768]{1,0:T(8,128)(2,1)} %get-tuple-element.394.refs_1_, bf16[16,768]{1,0:T(8,128)(2,1)} %get-tuple-element.383.refs_6_.refs_2_, bf16[16,768]{1,0:T(8,128)(2,1)} %get-tuple-element.395.refs_3_, ...), custom_call_target="tpu_custom_call" | custom-call | tf_op jit(solution)/shard_map/weight_grads/pallas_call | solution.py:851
  343.2 1.9 copy-done.2
  345.1 17.4 %table_sum.1 = (f32[6184,512]{1,0:T(8,128)}, f32[8,512]{1,0:T(8,128)S(1)}) custom-call(s32[32]{0:T(128)S(1)} %broadcast_minimum_fusion.counts_ref, s32[3072]{0:T(1024)S(1)} %add.308.index_ref, bf16[32,96,512]{2,1,0:T(8,128)(2,1)S(1)} %bitcast.108), custom_call_target="tpu_custom_call" | custom-call | tf_op jit(solution)/shard_map/table_sum/pallas_call | solution.py:1066
  362.5 0.3 conditional.3
  362.8 0.6 broadcast_select_fusion.square_ref
  363.4 132.9 %reduce_windows.1 = (f32[3328,128]{1,0:T(8,128)}, f32[32,8,128]{2,1,0:T(8,128)}) custom-call(f32[104176,128]{1,0:T(8,128)} %get-tuple-element.426.grads_ref, f32[8,512]{1,0:T(8,128)} %broadcast_select_fusion.square_ref), custom_call_target="tpu_custom_call" | custom-call | tf_op jit(solution)/shard_map/reduce_windows/pallas_call | solution.py:1456
  496.3 1.5 reduce_sum.190
  498.6 1.4 copy-done.4
  500.0 1.7 lift_window.1
  501.8 3.5 multiply_subtract_fusion.1
  505.3 32.1 %multiply_subtract_fusion = (f32[6176,512]{1,0:T(8,128)}, f32[6176,512]{1,0:T(8,128)}, f32[6176,512]{1,0:T(8,128)}) fusion(f32[6176,512]{1,0:T(8,128)} %param.24, f32[]{:T(128)S(6)} %min_shard_map.3, f32[6184,512]{1,0:T(8,128)} %get-tuple-element.438, f32[6176,512]{1,0:T(8,128)} %param.25, f32[6176,512]{1,0:T(8,128)} %param.26), kind=kLoop, calls=%fused_computation.33 | loop fusion | flops 50593792 | bytes 88539136 | tf_op jit(solution)/shard_map/sub | solution.py:497
  (69 shorter events, 1.7 us)
Async XLA Ops:
  13.3 1.7 copy-start.6
  190.2 4.0 copy-start
  190.2 4.0 copy-start.1
  190.2 4.0 copy-start.3
  243.2 0.8 copy-start.11
  268.3 21.5 %copy-start.12 = (f32[8,512]{1,0:T(8,128)S(1)}, f32[8,512]{1,0:T(8,128)}, u32[]{:S(2)}) copy-start(f32[8,512]{1,0:T(8,128)} %get-tuple-element.424) | copy-start | bytes 49156
  268.3 22.3 %copy-start.10 = (f32[77,512]{1,0:T(8,128)S(1)}, f32[77,512]{1,0:T(8,128)}, u32[]{:S(2)}) copy-start(f32[77,512]{1,0:T(8,128)} %get-tuple-element.423) | copy-start | bytes 473092
  288.0 4.3 copy-start.9
  343.2 1.9 copy-start.2
  363.4 138.4 %copy-start.5 = (f32[416441]{0:T(1024)S(1)}, f32[416441]{0:T(1024)}, u32[]{:S(2)}) copy-start(f32[416441]{0:T(1024)} %param.21) | copy-start | bytes 4997296
  363.4 138.4 %copy-start.7 = (f32[416441]{0:T(1024)S(1)}, f32[416441]{0:T(1024)}, u32[]{:S(2)}) copy-start(f32[416441]{0:T(1024)} %param.22) | copy-start | bytes 4997296
  498.6 1.5 copy-start.4
  500.0 1.8 copy-start.8

commit v8 on v7

--- a/solution.py
+++ b/solution.py
@@ -51,7 +51,7 @@
 LANES = 128
 GROUP = 16
 CHUNKS = 16
-GATHER_CHUNKS = 14
+GATHER_CHUNKS = 21
 TURNED = 6
 CACHED_ROWS = 64
 ID_ROWS = 16

time: 557 us -> 553 us (level)
  no operation moved by 1% of the time
where the time goes in v8:
time: 553 us; the launch traced here: 545 us
  Pallas kernels  434 us (78%)
  other arithmetic  47.5 us (9%)
  local copies, waits for them, and re-layouts  31.4 us (6%)
  between operations  24.9 us (5%)
  matrix products  7.52 us (1%)
    pallas_call x2, Pallas kernels, gather_windows(): pl.pallas_call(functools.partial(gather_kernel, sizes, chunks), out_shape...  136 us
    pallas_call x1, Pallas kernels, reduce_windows(): pl.pallas_call(functools.partial(reduce_kernel, shard, (x_size, low_size,...  133 us
    pallas_call x1, Pallas kernels, weight_grads(): pl.pallas_call(functools.partial(grads_kernel, parts, gx_size, gy_size),...  49.3 us
    sub x2, other arithmetic, adam_step(): weight - rate * (first_hat / (jnp.sqrt(second_hat) + adam_eps) + decay *...  35.6 us
    pallas_call x2, Pallas kernels, tower_backward(): pl.pallas_call(functools.partial(tower_backward_kernel, tower), out_shape...  34.6 us
    pallas_call x1, Pallas kernels, spread_weights(): pl.pallas_call(functools.partial(spread_entry, shard, gx_size, gy_size, v...  33.2 us
    pallas_call x2, Pallas kernels, tower_forward(): pl.pallas_call(functools.partial(tower_forward_kernel, tower), out_shape=...  26.7 us
    pallas_call x1, Pallas kernels, table_sum(): pl.pallas_call(functools.partial(table_sum_kernel, cap), out_shape=[jax.S...  17.6 us

profile of v8, /device:TPU:0, one launch (start us, length us, event | category | flops | bytes accessed | tf_op | source)
XLA Modules:
  0.0 545.1 jit_solution(6812644143209452088)
XLA Ops:
  7.2 0.8 reshape.344
  8.0 0.8 eq.183
  8.7 0.3 fusion.18
  9.3 0.5 select_reduce_fusion.3
  10.1 0.7 pad_maximum_fusion.9
  10.8 0.9 fusion.132
  11.7 1.6 pad_bitcast_fusion.1.flat_ref
  13.3 0.9 place_window.1
  14.3 0.6 copy-done.6
  15.0 1.6 pad_bitcast_fusion.refs_3_.refs_0_
  16.6 122.1 %gather_weights.1.gathered_ref = bf16[107520,128]{1,0:T(8,128)(2,1)} custom-call(bf16[3360,128]{1,0:T(8,128)(2,1)S(1)} %pad_maximum_fusion.window_ref), custom_call_target="tpu_custom_call" | custom-call | tf_op jit(solution)/shard_map/gather_weights/pallas_call | solution.py:1194
  138.7 0.9 slice_convert_fusion
  139.9 0.6 convert_reduce_fusion
  140.5 0.6 reduce_max.27
  141.8 0.2 fusion.23
  142.1 1.0 select_reduce_fusion.2
  143.2 1.1 slice.140
  144.3 0.3 reshape.353
  144.7 1.0 conditional.2
  144.7 0.9 broadcast_in_dim.197
  145.7 7.3 %gather_fusion.1 = bf16[768,512]{1,0:T(8,128)(2,1)S(1)} fusion(f32[6176,512]{1,0:T(8,128)} %param.24, s32[1024]{0:T(1024)S(1)} %pad_clamp_fusion.1), kind=kCustom, calls=%fused_computation.1 | custom fusion | bytes 1575936 | tf_op jit(solution)/shard_map/jit(_take)/gather | solution.py:1613
  153.0 33.2 %spread_weights.1 = (bf16[3072,768]{1,0:T(8,128)(2,1)}, bf16[768,3072]{1,0:T(8,128)(2,1)}, bf16[768,3072]{1,0:T(8,128)(2,1)}, bf16[3072,768]{1,0:T(8,128)(2,1)},...) custom-call(bf16[107520,128]{1,0:T(8,128)(2,1)} %gather_weights.1.ga, ...), custom_call_target="tpu_custom_call" | custom-call | tf_op jit(solution)/shard_map/spread_weights/pallas_call | solution.py:742
  186.3 0.6 slice.103
  187.5 1.8 fusion.21
  189.4 0.9 pad.40.refs_3_
  190.3 0.6 pad.38.refs_1_
  190.9 0.6 slice.105.refs_1_
  191.6 1.1 broadcast_bitcast_fusion.refs_2_
  192.7 16.7 %image_forward.1 = (f32[400,768]{1,0:T(8,128)}, bf16[400,768]{1,0:T(8,128)(2,1)}, bf16[400,1536]{1,0:T(8,128)(2,1)}, bf16[16,768]{1,0:T(8,128)(2,1)}, bf16[16,76...) custom-call(s32[8]{0:T(128)} %refs_0_.7, ...), custom_call_target="tpu_custom_call" | custom-call | tf_op jit(solution)/shard_map/image_forward/pallas_call | solution.py:299
  209.5 0.7 convert_element_type.112
  210.4 1.2 tile.13
  211.6 2.4 pad.39.refs_2_
  214.0 10.0 %text_forward.1 = (f32[624,512]{1,0:T(8,128)}, bf16[624,512]{1,0:T(8,128)(2,1)}, bf16[624,1024]{1,0:T(8,128)(2,1)}, bf16[16,512]{1,0:T(8,128)(2,1)}, bf16[16,512...) custom-call(s32[8]{0:T(128)} %refs_0_.7, ...), custom_call_target="tpu_custom_call" | custom-call | tf_op jit(solution)/shard_map/text_forward/pallas_call | solution.py:299
  224.0 0.7 convert_element_type.114
  224.7 14.2 %embeddings.1 = bf16[2048,128]{1,0:T(8,128)(2,1)S(1)} custom-call(bf16[64,128]{1,0:T(8,128)(2,1)S(1)} %reshape.349.window_ref), custom_call_target="tpu_custom_call" | custom-call | tf_op jit(solution)/shard_map/embeddings/pallas_call | solution.py:1194
  238.9 0.3 reshape.350
  239.3 0.3 fusion.65
  239.7 0.5 select_reduce_fusion.4
  240.1 0.4 exponential_reduce_fusion
  240.5 0.9 fusion.67
  243.3 1.1 multiply_reduce_fusion
  246.9 0.4 fusion.44
  247.3 1.0 convolution_add_fusion.refs_2_
  248.4 14.9 %text_backward.1 = (bf16[16,512]{1,0:T(8,128)(2,1)}, bf16[16,512]{1,0:T(8,128)(2,1)}, bf16[16,2048]{1,0:T(8,128)(2,1)}, bf16[16,512]{1,0:T(8,128)(2,1)}, bf16[16...) custom-call(s32[8]{0:T(128)} %refs_0_.7, ...), custom_call_target="tpu_custom_call" | custom-call | tf_op jit(solution)/shard_map/text_backward/pallas_call | solution.py:447
  263.3 0.4 fusion.45
  263.7 1.0 convolution_add_fusion.1.refs_2_
  264.8 19.7 %image_backward.1 = (bf16[16,512]{1,0:T(8,128)(2,1)}, bf16[16,768]{1,0:T(8,128)(2,1)}, bf16[16,3072]{1,0:T(8,128)(2,1)}, bf16[16,768]{1,0:T(8,128)(2,1)}, bf16[1...) custom-call(s32[8]{0:T(128)} %refs_0_.7, ...), custom_call_target="tpu_custom_call" | custom-call | tf_op jit(solution)/shard_map/image_backward/pallas_call | solution.py:447
  284.5 0.8 slice_reduce_fusion
  285.3 0.9 reshape.357
  286.3 0.7 reshape.358
  287.1 1.0 concatenate.35
  288.1 0.8 pad.41.refs_26_
  288.9 1.7 fusion.19
  290.5 49.3 %weight_grads.1 = (f32[104176,128]{1,0:T(8,128)}, bf16[4,8,96,512]{3,2,1,0:T(8,128)(2,1)}) custom-call(bf16[400,3072]{1,0:T(8,128)(2,1)} %pad_bitcast_fusion.refs_3_.refs_0_, bf16[400,768]{1,0:T(8,128)(2,1)} %get-tuple-element.394.refs_1_, bf16[16,768]{1,0:T(8,128)(2,1)} %get-tuple-element.383.refs_6_.refs_2_, bf16[16,768]{1,0:T(8,128)(2,1)} %get-tuple-element.395.refs_3_, ...), custom_call_target="tpu_custom_call" | custom-call | tf_op jit(solution)/shard_map/weight_grads/pallas_call | solution.py:851
  339.8 1.9 copy-done.2
  341.7 17.6 %table_sum.1 = (f32[6184,512]{1,0:T(8,128)}, f32[8,512]{1,0:T(8,128)S(1)}) custom-call(s32[32]{0:T(128)S(1)} %broadcast_minimum_fusion.counts_ref, s32[3072]{0:T(1024)S(1)} %add.308.index_ref, bf16[32,96,512]{2,1,0:T(8,128)(2,1)S(1)} %bitcast.108), custom_call_target="tpu_custom_call" | custom-call | tf_op jit(solution)/shard_map/table_sum/pallas_call | solution.py:1066
  359.3 0.3 conditional.3
  359.6 0.6 broadcast_select_fusion.square_ref
  360.2 133.1 %reduce_windows.1 = (f32[3328,128]{1,0:T(8,128)}, f32[32,8,128]{2,1,0:T(8,128)}) custom-call(f32[104176,128]{1,0:T(8,128)} %get-tuple-element.426.grads_ref, f32[8,512]{1,0:T(8,128)} %broadcast_select_fusion.square_ref), custom_call_target="tpu_custom_call" | custom-call | tf_op jit(solution)/shard_map/reduce_windows/pallas_call | solution.py:1456
  493.3 1.5 reduce_sum.190
  495.6 1.4 copy-done.4
  497.1 1.7 lift_window.1
  498.8 3.5 multiply_subtract_fusion.1
  502.3 32.1 %multiply_subtract_fusion = (f32[6176,512]{1,0:T(8,128)}, f32[6176,512]{1,0:T(8,128)}, f32[6176,512]{1,0:T(8,128)}) fusion(f32[6176,512]{1,0:T(8,128)} %param.24, f32[]{:T(128)S(6)} %min_shard_map.3, f32[6184,512]{1,0:T(8,128)} %get-tuple-element.438, f32[6176,512]{1,0:T(8,128)} %param.25, f32[6176,512]{1,0:T(8,128)} %param.26), kind=kLoop, calls=%fused_computation.33 | loop fusion | flops 50593792 | bytes 88539136 | tf_op jit(solution)/shard_map/sub | solution.py:497
  (69 shorter events, 1.7 us)
Async XLA Ops:
  13.3 1.7 copy-start.6
  186.2 4.0 copy-start
  186.2 4.0 copy-start.1
  186.2 4.0 copy-start.3
  239.7 0.8 copy-start.11
  264.8 21.5 %copy-start.12 = (f32[8,512]{1,0:T(8,128)S(1)}, f32[8,512]{1,0:T(8,128)}, u32[]{:S(2)}) copy-start(f32[8,512]{1,0:T(8,128)} %get-tuple-element.424) | copy-start | bytes 49156
  264.8 22.3 %copy-start.10 = (f32[77,512]{1,0:T(8,128)S(1)}, f32[77,512]{1,0:T(8,128)}, u32[]{:S(2)}) copy-start(f32[77,512]{1,0:T(8,128)} %get-tuple-element.423) | copy-start | bytes 473092
  284.5 4.3 copy-start.9
  339.8 1.9 copy-start.2
  360.2 138.6 %copy-start.5 = (f32[416441]{0:T(1024)S(1)}, f32[416441]{0:T(1024)}, u32[]{:S(2)}) copy-start(f32[416441]{0:T(1024)} %param.21) | copy-start | bytes 4997296
  360.2 138.6 %copy-start.7 = (f32[416441]{0:T(1024)S(1)}, f32[416441]{0:T(1024)}, u32[]{:S(2)}) copy-start(f32[416441]{0:T(1024)} %param.22) | copy-start | bytes 4997296
  495.6 1.5 copy-start.4
  497.1 1.8 copy-start.8
